TPU v7x, 128 devices: a whole 4x4x4 slice. The times are simulated.
128 devices in a mesh: src: 4 (over z_lo, core), tile: 32 (over y, z_hi, x).
Axes of the slice: x: 4, y: 4, z: 4 (z_hi: 2, z_lo: 2; z = z_hi * 2 + z_lo), core: 2. Of those that a mesh axis runs over, the one named last changes fastest.
Arguments:
- mask_ids: int32 [4096, 4096], P(('src', 'tile')), may hold values from 0 to 3
- trans_table: float32 [2, 4], replicated, may hold values from -1 to 1
- pupil: float32 [2, 640, 640], replicated, may hold values from -1 to 1, as said below
- shifts: int32 [4, 2], P('src'), may hold values from -64 to 64
- weights: float32 [4], P('src'), may hold values from 0.03 to 0.12
- dose: float32 [2, 4096, 4096], P(None, 'tile', 'src'), may hold values from 2 to 8
- quencher: float32 [2], replicated, may hold values from 0.1 to 0.4
Outputs:
- acid: float32 [2, 4096, 4096], P(None, 'tile', 'src')
- inhibitor: float32 [2, 4096, 4096], P(None, 'tile', 'src')
Inputs may be any that keep to these rules, and one draw needn't show every extreme that they name: `pupil`: zero outside the disc of radius 512//2 - 64 around index 320 in both dimensions, complex magnitude at most 1 inside.
All inputs are finite; a program needn't handle non-finite values.
Results may differ from a plain program's by a relative error of at most 0.0028.
The roundings to bfloat16 on the way count: a program that leaves them out, or rounds other values in their place, can miss the bound.
Values may be sent and summed in bfloat16 or wider, within the bound.
No kernel may reach another device: no remote copies, remote signals or barrier semaphores. Data moves between devices by JAX's collectives and lax.ppermute only.
A program may use at most 128 MiB of HBM per device.

v0:
```python
import math

import jax
import jax.numpy as jnp
from jax import lax
from jax.sharding import PartitionSpec as P

NPIX = 4096
PASS = 512
SHIFT = 64
LEVELS = 4
BAKE = 4


DIFF_ACID = 0.12
DIFF_QUENCH = 0.04
QUENCH_RATE = 0.6
CATALYSIS = 0.4


def extended(x, sides, width):
    for axis, dim in sides:
        peers, length = (lax.axis_size(axis), x.shape[dim])
        up = [(i, (i + 1) % peers) for i in range(peers)]
        down = [(j, i) for i, j in up]
        last = lax.slice_in_dim(x, length - width, length, axis=dim)
        leading = lax.slice_in_dim(x, 0, width, axis=dim)
        before = lax.ppermute(last, axis, up)
        after = lax.ppermute(leading, axis, down)
        x = jnp.concatenate([before, x, after], axis=dim)
    return x


def phase_tables(first_index, second_index, npix):
    product = jnp.mod(first_index[:, None] * second_index[None, :], npix)
    theta = product.astype(jnp.float32) * (2.0 * math.pi / npix)
    return (jnp.cos(theta), jnp.sin(theta))


def band_freqs():
    return jnp.arange(PASS, dtype=jnp.int32) - PASS // 2


def transmission_planes(mask_ids, trans_table):
    real_part = jnp.zeros(mask_ids.shape, jnp.float32)
    imag_part = jnp.zeros(mask_ids.shape, jnp.float32)
    for level in range(LEVELS):
        hit = mask_ids == level
        real_part = jnp.where(hit, trans_table[0, level], real_part)
        imag_part = jnp.where(hit, trans_table[1, level], imag_part)
    return (real_part.astype(jnp.bfloat16), imag_part.astype(jnp.bfloat16))


def forward_table():
    pixels = jnp.arange(NPIX, dtype=jnp.int32)
    cosine, sine = phase_tables(pixels, band_freqs(), NPIX)
    return jnp.concatenate([cosine, -sine], axis=1).astype(jnp.bfloat16)


def inverse_table(col_count):
    pixels = jnp.arange(col_count, dtype=jnp.int32)
    cosine, sine = phase_tables(band_freqs(), pixels, NPIX)
    return jnp.concatenate([cosine, sine], axis=1).astype(jnp.bfloat16)


def column_spectrum(trans_real, trans_imag, forward):
    first = jnp.dot(trans_real, forward, preferred_element_type=jnp.float32)
    second = jnp.dot(trans_imag, forward, preferred_element_type=jnp.float32)
    real_part = first[:, :PASS] - second[:, PASS:]
    imag_part = first[:, PASS:] + second[:, :PASS]
    return jnp.concatenate([real_part, imag_part], axis=1).astype(jnp.bfloat16)


def row_terms(piece):
    pixels = jnp.arange(piece.shape[0], dtype=jnp.int32)
    cosine, sine = phase_tables(band_freqs(), pixels, NPIX)
    first = jnp.dot(cosine.astype(jnp.bfloat16), piece, preferred_element_type=jnp.float32)
    second = jnp.dot(sine.astype(jnp.bfloat16), piece, preferred_element_type=jnp.float32)
    real_part = first[:, :PASS] + second[:, PASS:]
    imag_part = first[:, PASS:] - second[:, :PASS]
    return (real_part, imag_part)


def source_intensity(spec_real, spec_imag, pupil, shift, row_start, row_count, inverse):
    start_row = SHIFT - shift[0]
    start_col = SHIFT - shift[1]
    window = lax.dynamic_slice(
        pupil, (jnp.zeros((), jnp.int32), start_row, start_col), (2, PASS, PASS)
    )
    filt_real = window[0] * spec_real - window[1] * spec_imag
    filt_imag = window[0] * spec_imag + window[1] * spec_real
    stacked = jnp.concatenate([filt_real, filt_imag], axis=1).astype(jnp.bfloat16)
    pixels = row_start + jnp.arange(row_count, dtype=jnp.int32)
    cosine, sine = phase_tables(pixels, band_freqs(), NPIX)
    first = jnp.dot(cosine.astype(jnp.bfloat16), stacked, preferred_element_type=jnp.float32)
    second = jnp.dot(sine.astype(jnp.bfloat16), stacked, preferred_element_type=jnp.float32)
    rows_real = (first[:, :PASS] - second[:, PASS:]).astype(jnp.bfloat16)
    rows_imag = (first[:, PASS:] + second[:, :PASS]).astype(jnp.bfloat16)
    upper = jnp.dot(rows_real, inverse, preferred_element_type=jnp.float32)
    lower = jnp.dot(rows_imag, inverse, preferred_element_type=jnp.float32)
    width = inverse.shape[1] // 2
    field_real = upper[:, :width] - lower[:, width:]
    field_imag = upper[:, width:] + lower[:, :width]
    return field_real * field_real + field_imag * field_imag


def bake_once(padded):
    center = padded[:, :, 1:-1, 1:-1]
    above = jnp.concatenate([center[:, 1:], center[:, -1:]], axis=1)
    below = jnp.concatenate([center[:, :1], center[:, :-1]], axis=1)
    lap = (
        padded[:, :, 2:, 1:-1]
        + padded[:, :, :-2, 1:-1]
        + padded[:, :, 1:-1, 2:]
        + padded[:, :, 1:-1, :-2]
        + above
        + below
        - 6.0 * center
    )
    acid_old = center[0]
    quench_old = center[1]
    reaction = QUENCH_RATE * acid_old * quench_old
    acid_new = acid_old + DIFF_ACID * lap[0] - reaction
    quench_new = quench_old + DIFF_QUENCH * lap[1] - reaction
    return (jnp.stack([acid_new, quench_new]), acid_old)


def body(mask_ids, trans_table, pupil, shifts, weights, dose, quencher):
    trans_real, trans_imag = transmission_planes(mask_ids, trans_table)
    columns = column_spectrum(trans_real, trans_imag, forward_table())
    part_real, part_imag = row_terms(lax.all_gather(columns, ("src", "tile"), axis=0, tiled=True))
    spec_real = part_real
    spec_imag = part_imag
    scale = 1.0 / (NPIX * NPIX)
    spec_real = spec_real * scale
    spec_imag = spec_imag * scale
    image_rows = NPIX // lax.axis_size("tile")
    row_start = lax.axis_index("tile") * image_rows
    inverse = inverse_table(NPIX)
    partial_value = weights[0] * source_intensity(
        spec_real, spec_imag, pupil, shifts[0], row_start, image_rows, inverse
    )
    intensity = lax.psum_scatter(partial_value, "src", scatter_dimension=1, tiled=True)
    acid = 1.0 - jnp.exp(-dose * intensity[None])
    quench = jnp.broadcast_to(quencher[:, None, None], acid.shape)
    fields = jnp.stack([acid, quench])
    inhibitor = jnp.ones_like(acid)
    for step in range(BAKE):
        padded = extended(fields, (("src", 3), ("tile", 2)), 1)
        fields, before = bake_once(padded)
        inhibitor = inhibitor * jnp.exp(-CATALYSIS * before)
    return (fields[0], inhibitor)


def solution(mesh):
    return jax.shard_map(
        body,
        mesh=mesh,
        in_specs=(
            P(("src", "tile"), None),
            P(),
            P(),
            P("src", None),
            P("src"),
            P(None, "tile", "src"),
            P(),
        ),
        out_specs=(P(None, "tile", "src"), P(None, "tile", "src")),
        check_vma=False,
    )
```

profile of v0, /device:TPU:1, one launch (start us, length us, event | category | flops | bytes accessed | tf_op | source)
XLA Modules:
  0.0 546.2 jit_solution(8254156573577203625)
XLA Ops:
  7.2 34.1 %cosine_convert_fusion = (bf16[4096,512]{1,0:T(8,128)(2,1)S(1)}, bf16[4096,512]{1,0:T(8,128)(2,1)S(1)}) fusion(s32[512]{0:T(512)S(1)} %iota_add_fusion), kind=kLoop, calls=%fused_computation.16 | loop fusion | flops 35651584 | bytes 8390656 | tf_op jit(solution)/shard_map/convert.6
  42.3 4.0 fusion.15
  46.3 4.1 fusion.14
  55.0 32.5 %cosine_convert_fusion.7 = bf16[512,4096]{1,0:T(8,128)(2,1)} fusion(s32[512]{0:T(512)S(1)} %iota_add_fusion), kind=kLoop, calls=%fused_computation.19.clone.clone.1 | loop fusion | flops 31457280 | bytes 4196352 | tf_op jit(solution)/shard_map/dot_general | solution.py:77
  87.6 32.7 %sine_convert_fusion.6 = bf16[512,4096]{1,0:T(8,128)(2,1)} fusion(s32[512]{0:T(512)S(1)} %iota_add_fusion), kind=kLoop, calls=%fused_computation.14.clone.clone.1 | loop fusion | flops 31457280 | bytes 4196352 | tf_op jit(solution)/shard_map/dot_general | solution.py:78
  120.2 36.7 %cosine_convert_fusion.1 = (bf16[512,4096]{1,0:T(8,128)(2,1)}, bf16[512,4096]{1,0:T(8,128)(2,1)}) fusion(s32[512]{0:T(512)S(1)} %iota_add_fusion), kind=kLoop, calls=%fused_computation.19 | loop fusion | flops 33554432 | bytes 8390656 | tf_op jit(solution)/shard_map/convert_element_type | solution.py:77
  156.9 210.0 %all-gather.2.cloned.1.call-done = bf16[4096,1024]{1,0:T(8,128)(2,1)} async-done(((bf16[32,1024]{1,0:T(8,128)(2,1)}), bf16[4096,1024]{1,0:T(8,128)(2,1)}) %all-gather.2.cloned.1.call-update) | async-done | bytes 8388624 | tf_op jit(solution)/shard_map/all_gather | solution.py:131
  366.9 8.4 %fusion.38 = f32[512,1024]{1,0:T(8,128)S(1)} fusion(bf16[4096,1024]{1,0:T(8,128)(2,1)} %all-gather.2.cloned.1.call-done, bf16[512,4096]{1,0:T(8,128)(2,1)} %cosine_convert_fusion.7), kind=kOutput, calls=%fused_computation.114 | convolution fusion | flops 4294967296 | bytes 14680064 | tf_op jit(solution)/shard_map/dot_general | solution.py:77
  375.4 4.5 fusion.39
  380.8 1.2 fusion.85
  382.1 1.2 fusion.84
  383.6 1.3 fusion.13
  384.9 1.3 fusion.12
  386.1 2.0 fusion.36
  388.8 27.7 %reduce-scatter.2.cloned.1.call-done = f32[128,1024]{1,0:T(8,128)} async-done(((f32[128,4096]{1,0:T(8,128)}), f32[128,1024]{1,0:T(8,128)}) %reduce-scatter.2.cloned.1.call-update) | async-done | bytes 524304 | tf_op jit(solution)/shard_map/reduce_scatter | solution.py:143
  416.5 1.2 fusion.140
  418.6 1.5 pad_maximum_fusion.2
  420.1 1.9 collective-permute-done
  422.0 4.5 collective-permute-done.1
  426.5 4.2 concatenate.108
  431.7 6.9 %collective-permute-start.2 = (f32[2,2,1,1026]{3,2,1,0:T(1,128)S(1)}, f32[2,2,1,1026]{3,2,1,0:T(1,128)S(1)}, u32[]{:S(2)}, u32[]{:S(2)}) collective-permute-start(f32[2,2,1,1026]{3,2,1,0:T(1,128)S(1)} %get-tuple-element.17), channel_id=1, source_target_pairs={{1,0},{2,1},{3,2},{4,3},{5,4},{6,5},{7,6},{8,7},{9,8},{10,9},{11,1... | collective-permute-start | bytes 49256 | tf_op jit(solution)/shard_map/ppermute | solution.py:29
  439.5 7.6 %collective-permute-done.3 = f32[2,2,1,1026]{3,2,1,0:T(1,128)S(1)} collective-permute-done((f32[2,2,1,1026]{3,2,1,0:T(1,128)S(1)}, f32[2,2,1,1026]{3,2,1,0:T(1,128)S(1)}, u32[]{:S(2)}, u32[]{:S(2)}) %collective-permute-start.3) | collective-permute-done | bytes 16448 | tf_op jit(solution)/shard_map/ppermute | solution.py:28
  447.2 4.8 fusion.31
  453.8 1.5 pad_maximum_fusion.8
  455.3 2.0 collective-permute-done.4
  457.3 4.4 collective-permute-done.5
  461.6 4.0 concatenate.115
  466.7 1.4 collective-permute-start.7
  469.3 5.8 %collective-permute-done.7 = f32[2,2,1,1026]{3,2,1,0:T(1,128)S(1)} collective-permute-done((f32[2,2,1,1026]{3,2,1,0:T(1,128)S(1)}, f32[2,2,1,1026]{3,2,1,0:T(1,128)S(1)}, u32[]{:S(2)}, u32[]{:S(2)}) %collective-permute-start.7) | collective-permute-done | bytes 16448 | tf_op jit(solution)/shard_map/ppermute | solution.py:28
  475.1 3.8 fusion.25
  479.0 1.7 fusion.72
  480.8 1.1 collective-permute-start.8
  482.5 1.5 pad_maximum_fusion.9
  484.0 1.5 collective-permute-done.8
  485.5 5.0 collective-permute-done.9
  490.5 4.2 concatenate.122
  495.7 1.7 collective-permute-start.11
  498.3 6.1 %collective-permute-done.11 = f32[2,2,1,1026]{3,2,1,0:T(1,128)S(1)} collective-permute-done((f32[2,2,1,1026]{3,2,1,0:T(1,128)S(1)}, f32[2,2,1,1026]{3,2,1,0:T(1,128)S(1)}, u32[]{:S(2)}, u32[]{:S(2)}) %collective-permute-start.11) | collective-permute-done | bytes 16448 | tf_op jit(solution)/shard_map/ppermute | solution.py:28
  504.4 4.9 fusion.19
  509.3 2.0 exponential_multiply_fusion
  513.2 1.5 pad_maximum_fusion.7
  514.7 1.0 collective-permute-done.12
  515.7 5.6 %collective-permute-done.13 = f32[2,2,128,1]{3,2,1,0:T(8,128)} collective-permute-done((f32[2,2,128,1]{3,2,1,0:T(8,128)S(1)}, f32[2,2,128,1]{3,2,1,0:T(8,128)}, u32[]{:S(2)}, u32[]{:S(2)}) %collective-permute-start.13) | collective-permute-done | bytes 2080 | tf_op jit(solution)/shard_map/ppermute | solution.py:29
  521.3 4.2 concatenate.129
  526.5 1.4 collective-permute-start.15
  528.0 1.4 fusion.60
  529.4 5.6 %collective-permute-done.15 = f32[2,2,1,1026]{3,2,1,0:T(1,128)S(1)} collective-permute-done((f32[2,2,1,1026]{3,2,1,0:T(1,128)S(1)}, f32[2,2,1,1026]{3,2,1,0:T(1,128)S(1)}, u32[]{:S(2)}, u32[]{:S(2)}) %collective-permute-start.15) | collective-permute-done | bytes 16448 | tf_op jit(solution)/shard_map/ppermute | solution.py:28
  534.9 3.9 fusion.50
  (87 shorter events, 16.6 us)
Async XLA Ops:
  7.2 359.8 %all-gather.2.cloned.1.call-start = ((), (), s32[]{:S(2)}) async-start(), calls=%async_computation.1 | async-start | bytes 8454144 | tf_op jit(solution)/shard_map/all_gather | solution.py:131
  7.2 34.1 %copy-start.19 = (f32[2,4]{1,0:T(2,128)S(1)}, f32[2,4]{1,0:T(2,128)}, u32[]{:S(2)}) copy-start(f32[2,4]{1,0:T(2,128)} %param.8) | copy-start | bytes 100
  7.2 34.8 %copy-start.18 = (s32[32,4096]{1,0:T(8,128)S(1)}, s32[32,4096]{1,0:T(8,128)}, u32[]{:S(2)}) copy-start(s32[32,4096]{1,0:T(8,128)} %param.7) | copy-start | bytes 1572868
  46.3 4.8 copy-start.21
  51.1 365.4 %reduce-scatter.2.cloned.1.call-start = ((), (), s32[]{:S(2)}) async-start(), calls=%async_computation.2 | async-start | bytes 2621440 | tf_op jit(solution)/shard_map/reduce_scatter | solution.py:143
  366.9 8.5 %copy-start.16 = (bf16[512,4096]{1,0:T(8,128)(2,1)S(1)}, bf16[512,4096]{1,0:T(8,128)(2,1)}, u32[]{:S(2)}) copy-start(bf16[512,4096]{1,0:T(8,128)(2,1)} %sine_convert_fusion.6) | copy-start | bytes 12582916
  366.9 8.5 %copy-start.22 = (bf16[4096,1024]{1,0:T(8,128)(2,1)S(1)}, bf16[4096,1024]{1,0:T(8,128)(2,1)}, u32[]{:S(2)}) copy-start(bf16[4096,1024]{1,0:T(8,128)(2,1)} %all-gather.2.cloned.1.call-done) | copy-start | bytes 25165828
  375.4 4.5 copy-start.17
  379.9 3.4 copy-start.15
  380.8 2.8 copy-start.14
  388.1 0.7 copy-start.20
  388.1 28.4 %copy-start.10 = (f32[2,128,1024]{2,1,0:T(8,128)S(1)}, f32[2,128,1024]{2,1,0:T(8,128)}, u32[]{:S(2)}) copy-start(f32[2,128,1024]{2,1,0:T(8,128)} %param.12) | copy-start | bytes 3145732
  418.0 4.0 collective-permute-start
  418.2 8.3 %collective-permute-start.1 = (f32[2,2,128,1]{3,2,1,0:T(8,128)S(1)}, f32[2,2,128,1]{3,2,1,0:T(8,128)}, u32[]{:S(2)}, u32[]{:S(2)}) collective-permute-start(f32[2,2,128,1]{3,2,1,0:T(8,128)S(1)} %get-tuple-element.33), channel_id=1, source_target_pairs={{32,0},{64,32},{96,64},{0,96},{33,1},{65,33},{97,65},{1,97},{34,2}... | collective-permute-start | bytes 6152 | tf_op jit(solution)/shard_map/ppermute | solution.py:29
  431.7 7.8 %collective-permute-start.2 = (f32[2,2,1,1026]{3,2,1,0:T(1,128)S(1)}, f32[2,2,1,1026]{3,2,1,0:T(1,128)S(1)}, u32[]{:S(2)}, u32[]{:S(2)}) collective-permute-start(f32[2,2,1,1026]{3,2,1,0:T(1,128)S(1)} %get-tuple-element.17), channel_id=1, source_target_pairs={{1,0},{2,1},{3,2},{4,3},{5,4},{6,5},{7,6},{8,7},{9,8},{10,9},{11,1... | collective-permute-start | bytes 49256 | tf_op jit(solution)/shard_map/ppermute | solution.py:29
  438.6 8.5 %copy-start.7 = (f32[2,2,128,1026]{3,2,1,0:T(8,128)S(1)}, f32[2,2,128,1026]{3,2,1,0:T(8,128)}, u32[]{:S(2)}) copy-start(f32[2,2,128,1026]{3,2,1,0:T(8,128)} %concatenate.108) | copy-start | bytes 6303748
  438.6 8.5 %collective-permute-start.3 = (f32[2,2,1,1026]{3,2,1,0:T(1,128)S(1)}, f32[2,2,1,1026]{3,2,1,0:T(1,128)S(1)}, u32[]{:S(2)}, u32[]{:S(2)}) collective-permute-start(f32[2,2,1,1026]{3,2,1,0:T(1,128)S(1)} %get-tuple-element.18), channel_id=1, source_target_pairs={{0,1},{1,2},{2,3},{3,4},{4,5},{5,6},{6,7},{7,8},{8,9},{9,10},{10,1... | collective-permute-start | bytes 49256 | tf_op jit(solution)/shard_map/ppermute | solution.py:28
  447.2 4.8 copy-start.12
  452.5 22.6 %copy-start = (f32[2,128,1024]{2,1,0:T(8,128)}, f32[2,128,1024]{2,1,0:T(8,128)S(1)}, u32[]{:S(2)}) copy-start(f32[2,128,1024]{2,1,0:T(8,128)S(1)} %get-tuple-element.9) | copy-start | bytes 3145732
  452.7 4.6 collective-permute-start.4
  453.4 8.2 %collective-permute-start.5 = (f32[2,2,128,1]{3,2,1,0:T(8,128)S(1)}, f32[2,2,128,1]{3,2,1,0:T(8,128)S(1)}, u32[]{:S(2)}, u32[]{:S(2)}) collective-permute-start(f32[2,2,128,1]{3,2,1,0:T(8,128)S(1)} %get-tuple-element.29), channel_id=1, source_target_pairs={{32,0},{64,32},{96,64},{0,96},{33,1},{65,33},{97,65},{1,97},{34,2}... | collective-permute-start | bytes 6152 | tf_op jit(solution)/shard_map/ppermute | solution.py:29
  466.6 2.7 collective-permute-start.6
  466.7 8.4 %copy-start.8 = (f32[2,2,128,1026]{3,2,1,0:T(8,128)S(1)}, f32[2,2,128,1026]{3,2,1,0:T(8,128)}, u32[]{:S(2)}) copy-start(f32[2,2,128,1026]{3,2,1,0:T(8,128)} %concatenate.115) | copy-start | bytes 6303748
  466.7 8.4 %collective-permute-start.7 = (f32[2,2,1,1026]{3,2,1,0:T(1,128)S(1)}, f32[2,2,1,1026]{3,2,1,0:T(1,128)S(1)}, u32[]{:S(2)}, u32[]{:S(2)}) collective-permute-start(f32[2,2,1,1026]{3,2,1,0:T(1,128)S(1)} %get-tuple-element.16), channel_id=1, source_target_pairs={{0,1},{1,2},{2,3},{3,4},{4,5},{5,6},{6,7},{7,8},{8,9},{9,10},{10,1... | collective-permute-start | bytes 49256 | tf_op jit(solution)/shard_map/ppermute | solution.py:28
  480.8 4.7 collective-permute-start.8
  481.9 8.6 %collective-permute-start.9 = (f32[2,2,128,1]{3,2,1,0:T(8,128)S(1)}, f32[2,2,128,1]{3,2,1,0:T(8,128)}, u32[]{:S(2)}, u32[]{:S(2)}) collective-permute-start(f32[2,2,128,1]{3,2,1,0:T(8,128)S(1)} %get-tuple-element.25), channel_id=1, source_target_pairs={{32,0},{64,32},{96,64},{0,96},{33,1},{65,33},{97,65},{1,97},{34,2}... | collective-permute-start | bytes 6152 | tf_op jit(solution)/shard_map/ppermute | solution.py:29
  495.6 2.7 collective-permute-start.10
  495.7 8.7 %copy-start.9 = (f32[2,2,128,1026]{3,2,1,0:T(8,128)S(1)}, f32[2,2,128,1026]{3,2,1,0:T(8,128)}, u32[]{:S(2)}) copy-start(f32[2,2,128,1026]{3,2,1,0:T(8,128)} %concatenate.122) | copy-start | bytes 6303748
  495.7 8.7 %collective-permute-start.11 = (f32[2,2,1,1026]{3,2,1,0:T(1,128)S(1)}, f32[2,2,1,1026]{3,2,1,0:T(1,128)S(1)}, u32[]{:S(2)}, u32[]{:S(2)}) collective-permute-start(f32[2,2,1,1026]{3,2,1,0:T(1,128)S(1)} %get-tuple-element.14), channel_id=1, source_target_pairs={{0,1},{1,2},{2,3},{3,4},{4,5},{5,6},{6,7},{7,8},{8,9},{9,10},{10,1... | collective-permute-start | bytes 49256 | tf_op jit(solution)/shard_map/ppermute | solution.py:28
  504.4 4.9 copy-start.11
  504.4 4.9 copy-start.13
  509.3 2.0 copy-start.5
  511.3 3.3 copy-start.1
  511.3 3.3 copy-start.3
  511.5 4.2 collective-permute-start.12
  512.4 8.9 %collective-permute-start.13 = (f32[2,2,128,1]{3,2,1,0:T(8,128)S(1)}, f32[2,2,128,1]{3,2,1,0:T(8,128)}, u32[]{:S(2)}, u32[]{:S(2)}) collective-permute-start(f32[2,2,128,1]{3,2,1,0:T(8,128)S(1)} %get-tuple-element.21), channel_id=1, source_target_pairs={{32,0},{64,32},{96,64},{0,96},{33,1},{65,33},{97,65},{1,97},{34,2}... | collective-permute-start | bytes 6152 | tf_op jit(solution)/shard_map/ppermute | solution.py:29
  515.7 12.3 %copy-start.2 = (f32[2,128,1024]{2,1,0:T(8,128)S(1)}, f32[2,128,1024]{2,1,0:T(8,128)}, u32[]{:S(2)}) copy-start(f32[2,128,1024]{2,1,0:T(8,128)} %copy-done.1) | copy-start | bytes 3145732
  526.4 2.9 collective-permute-start.14
  526.5 8.4 %copy-start.4 = (f32[1,2,128,1024]{3,2,1,0:T(8,128)S(1)}, f32[1,2,128,1024]{3,2,1,0:T(8,128)}, u32[]{:S(2)}) copy-start(f32[1,2,128,1024]{3,2,1,0:T(8,128)} %copy-done.3) | copy-start | bytes 3145732
  526.5 8.4 %copy-start.6 = (f32[2,2,128,1024]{3,2,1,0:T(8,128)S(1)}, f32[2,2,128,1024]{3,2,1,0:T(8,128)}, u32[]{:S(2)}) copy-start(f32[2,2,128,1024]{3,2,1,0:T(8,128)} %copy-done.5) | copy-start | bytes 6291460
  526.5 8.4 %collective-permute-start.15 = (f32[2,2,1,1026]{3,2,1,0:T(1,128)S(1)}, f32[2,2,1,1026]{3,2,1,0:T(1,128)S(1)}, u32[]{:S(2)}, u32[]{:S(2)}) collective-permute-start(f32[2,2,1,1026]{3,2,1,0:T(1,128)S(1)} %get-tuple-element.11), channel_id=1, source_target_pairs={{0,1},{1,2},{2,3},{3,4},{4,5},{5,6},{6,7},{7,8},{8,9},{9,10},{10,1... | collective-permute-start | bytes 49256 | tf_op jit(solution)/shard_map/ppermute | solution.py:28
Sparse Core Ops, SparseCore 0:
  51.2 315.6 all-gather.1
  388.2 28.1 reduce-scatter.1
where the time goes:
time: 556 us; the launch traced here: 546 us
  waiting for transfers between devices  291 us (52%)
  other arithmetic  171 us (31%)
  matrix products  26 us (5%)
  local copies, waits for them, and re-layouts  22.9 us (4%)
  between operations  18.2 us (3%)
  starting transfers between devices  17.1 us (3%)
    all_gather x1, waiting for transfers between devices, body(): lax.all_gather(columns, ('src', 'tile'), axis=0, tiled=True)  210 us
    convert_element_type x1, other arithmetic, row_terms(): cosine.astype(jnp.bfloat16)  36.7 us
    another operation x3, other arithmetic  35 us
    dot_general x1, other arithmetic, row_terms(): jnp.dot(sine.astype(jnp.bfloat16), piece, preferred_element_type=jnp.floa...  32.7 us
    dot_general x1, other arithmetic, row_terms(): jnp.dot(cosine.astype(jnp.bfloat16), piece, preferred_element_type=jnp.fl...  32.5 us
    ppermute x8, waiting for transfers between devices, extended(): before = lax.ppermute(last, axis, up)  31.5 us
    reduce_scatter x1, waiting for transfers between devices, body(): lax.psum_scatter(partial_value, 'src', scatter_dimension=1, tiled=True)  27.7 us
    ppermute x8, waiting for transfers between devices, extended(): after = lax.ppermute(leading, axis, down)  21.7 us
  transfers between devices with their start and end apart: 18, of which 17 were waited for; matrix products, arithmetic and copies ran while one was open for 20% of the time, Pallas kernels for 0%

commit v1 on v0

v1 whole, which is shorter than its diff:
```python
import math

import jax
import jax.numpy as jnp
import numpy as np
from jax import lax
from jax.experimental import pallas as pl
from jax.experimental.pallas import tpu as pltpu
from jax.sharding import Mesh, PartitionSpec as P

NPIX = 4096
PASS = 512
SHIFT = 64
LEVELS = 4
SOURCES = 4
BAKE = 4
Z = 2
DIFF_ACID = 0.12
DIFF_QUENCH = 0.04
QUENCH_RATE = 0.6
CATALYSIS = 0.4

DEVICES = 128
ROWS = NPIX // DEVICES
OWNERS = 32
FREQS = PASS // OWNERS
WIDE = 2 * FREQS
HALO = 4
TALL = 144
BRICK_ROWS = 128
BRICK_COLS = 1024
EXT_ROWS = BRICK_ROWS + 2 * HALO
EXT_COLS = BRICK_COLS + 128
COL_TILES = EXT_COLS // 128
ALL = ("zl", "c", "y", "zh", "x")
MIB = 1024 * 1024


def cos_sin(first, second):
    theta = (np.mod(first[:, None] * second[None, :], NPIX)).astype(np.float32)
    theta = (theta * np.float32(2.0 * math.pi / NPIX)).astype(np.float64)
    return np.cos(theta).astype(np.float32), np.sin(theta).astype(np.float32)


def bf16(table):
    return table.astype(jnp.bfloat16)


FREQ = np.arange(PASS, dtype=np.int64) - PASS // 2


def forward_columns():
    cosine, sine = cos_sin(np.arange(NPIX), FREQ)
    cosine = cosine.reshape(NPIX, OWNERS, 1, FREQS)
    sine = sine.reshape(NPIX, OWNERS, 1, FREQS)
    return bf16(np.concatenate([cosine, sine], axis=2).reshape(NPIX, 2 * PASS))


def forward_rows():
    order = np.arange(NPIX).reshape(DEVICES, 4, 8).transpose(1, 0, 2).reshape(NPIX)
    cosine, sine = cos_sin(FREQ, order)
    both = np.concatenate([cosine, sine], axis=0)
    return bf16(both.reshape(2 * PASS, 4, NPIX // 4).transpose(1, 0, 2))


def inverse_rows(tiles):
    blocks = []
    for tile in range(tiles):
        pixels = np.mod(tile * BRICK_ROWS - HALO + np.arange(TALL), NPIX)
        cosine, sine = cos_sin(pixels, FREQ)
        upper = np.concatenate([cosine, -sine], axis=1)
        lower = np.concatenate([sine, cosine], axis=1)
        blocks.append(np.concatenate([upper, lower], axis=0))
    return bf16(np.stack(blocks))


def inverse_cols(sources):
    lanes = np.arange(EXT_COLS)
    local = np.where(lanes < BRICK_COLS + 64, lanes, lanes - EXT_COLS)
    blocks = []
    for source in range(sources):
        pixels = np.mod(source * BRICK_COLS + local, NPIX)
        cosine, sine = cos_sin(FREQ, pixels)
        real = np.concatenate([cosine, -sine], axis=0).reshape(2 * PASS, COL_TILES, 1, 128)
        imag = np.concatenate([sine, cosine], axis=0).reshape(2 * PASS, COL_TILES, 1, 128)
        both = np.concatenate([real, imag], axis=2).reshape(2 * PASS, COL_TILES, 256)
        blocks.append(both.transpose(1, 0, 2))
    return bf16(np.stack(blocks))


def lane_ids(shape):
    return lax.broadcasted_iota(jnp.int32, shape, len(shape) - 1)


def columns_kernel(trans_ref, ids_ref, table_ref, out_ref, acc_ref):
    step = pl.program_id(0)
    ids = ids_ref[...]
    parts = []
    for plane in range(2):
        value = jnp.zeros(ids.shape, jnp.float32)
        for level in range(LEVELS):
            value = jnp.where(ids == level, trans_ref[plane, level], value)
        parts.append(value)
    trans = jnp.concatenate(parts, axis=0).astype(jnp.bfloat16)
    product = jnp.dot(trans, table_ref[...], preferred_element_type=jnp.float32)

    @pl.when(step == 0)
    def _():
        acc_ref[...] = product

    @pl.when(step > 0)
    def _():
        acc_ref[...] += product

    @pl.when(step == pl.num_programs(0) - 1)
    def _():
        upper = acc_ref[:ROWS, :]
        lower = acc_ref[ROWS:, :]
        width = upper.shape[1]
        is_real = lane_ids(upper.shape) % WIDE < FREQS
        columns = jnp.where(
            is_real,
            upper + pltpu.roll(lower, width - FREQS, 1),
            pltpu.roll(lower, FREQS, 1) - upper,
        )
        group = lane_ids((8, 128)) // WIDE
        chunks = []
        for owner in range(OWNERS):
            major, minor = owner // 4, owner % 4
            chunk = jnp.zeros((8, 128), jnp.float32)
            for q in range(4):
                piece = columns[8 * q : 8 * q + 8, 128 * major : 128 * major + 128]
                turn = (q - minor) % 4 * WIDE
                piece = pltpu.roll(piece, turn, 1) if turn else piece
                chunk = jnp.where(group == q, piece, chunk)
            chunks.append(chunk)
        for pair in range(DEVICES // 2):
            both = []
            for dest in (2 * pair, 2 * pair + 1):
                core, y, x = dest // 32 % 2, dest // 8 % 4, dest % 4
                both.append(chunks[core * 16 + y * 4 + x])
            out_ref[16 * pair : 16 * pair + 16, :] = jnp.concatenate(both, axis=0).astype(jnp.bfloat16)


def columns_call(trans_table, mask_ids, table):
    steps = 4
    depth = NPIX // steps
    return pl.pallas_call(
        columns_kernel,
        grid=(steps,),
        out_shape=jax.ShapeDtypeStruct((DEVICES * 8, 128), jnp.bfloat16),
        in_specs=[
            pl.BlockSpec(memory_space=pltpu.SMEM),
            pl.BlockSpec((ROWS, depth), lambda k: (0, k)),
            pl.BlockSpec((depth, 2 * PASS), lambda k: (k, 0)),
        ],
        out_specs=pl.BlockSpec((DEVICES * 8, 128), lambda k: (0, 0)),
        scratch_shapes=[pltpu.VMEM((2 * ROWS, 2 * PASS), jnp.float32)],
        compiler_params=pltpu.CompilerParams(vmem_limit_bytes=20 * MIB),
        name="columns",
    )(trans_table, mask_ids, table)


def spectrum_kernel(table_ref, cols_ref, out_ref, acc_ref):
    step = pl.program_id(0)
    product = jnp.dot(table_ref[0], cols_ref[...], preferred_element_type=jnp.float32)
    group = lane_ids(product.shape) // WIDE

    @pl.when(step == 0)
    def _():
        acc_ref[...] = product

    @pl.when(step > 0)
    def _():
        acc_ref[...] = jnp.where(group == step, product, acc_ref[...])

    @pl.when(step == pl.num_programs(0) - 1)
    def _():
        total = acc_ref[...]
        total = total + pltpu.roll(total, 64, 1)
        total = total + pltpu.roll(total, 32, 1)
        cosine, sine = total[:PASS], total[PASS:]
        is_real = lane_ids(cosine.shape) % WIDE < FREQS
        turned = jnp.where(is_real, pltpu.roll(sine, 128 - FREQS, 1), -pltpu.roll(sine, FREQS, 1))
        spectrum = (cosine + turned) * (1.0 / (NPIX * NPIX))
        block = jnp.transpose(spectrum)[:WIDE, :]
        for dest in range(16):
            out_ref[dest * WIDE : (dest + 1) * WIDE, :] = block


def spectrum_call(table, cols):
    return pl.pallas_call(
        spectrum_kernel,
        grid=(4,),
        out_shape=jax.ShapeDtypeStruct((16 * WIDE, PASS), jnp.float32),
        in_specs=[
            pl.BlockSpec((1, 2 * PASS, NPIX // 4), lambda q: (q, 0, 0)),
            pl.BlockSpec((NPIX // 4, 128), lambda q: (0, 0)),
        ],
        out_specs=pl.BlockSpec((16 * WIDE, PASS), lambda q: (0, 0)),
        scratch_shapes=[pltpu.VMEM((2 * PASS, 128), jnp.float32)],
        compiler_params=pltpu.CompilerParams(vmem_limit_bytes=20 * MIB),
        name="spectrum",
    )(table, cols)


def resist_kernel(
    core_ref, weights_ref, quencher_ref, own_ref, other_ref, window_ref, rows_ref, cols_ref, dose_ref,
    acid_ref, inhibitor_ref, filt_ref, field_ref, a_ref, b_ref, p_ref, q_ref, sum_ref,
):
    core = core_ref[0]

    def source_step(s, carry):
        def filter_from(spec_ref, half):
            def block(o, inner):
                row = pl.multiple_of(half * (PASS // 2) + o * FREQS, FREQS)
                base = pl.multiple_of(o * WIDE, WIDE)
                real = spec_ref[pl.ds(base, FREQS), :]
                imag = spec_ref[pl.ds(base + FREQS, FREQS), :]
                w_real = window_ref[2 * s, pl.ds(row, FREQS), :]
                w_imag = window_ref[2 * s + 1, pl.ds(row, FREQS), :]
                filt_ref[pl.ds(row, FREQS), :PASS] = (w_real * real - w_imag * imag).astype(jnp.bfloat16)
                filt_ref[pl.ds(row, FREQS), PASS:] = (w_real * imag + w_imag * real).astype(jnp.bfloat16)
                return inner

            lax.fori_loop(0, 16, block, 0, unroll=4)

        filter_from(own_ref, core)
        filter_from(other_ref, 1 - core)
        rowfield = lax.dot_general(
            rows_ref[...], filt_ref[...], (((1,), (1,)), ((), ())), preferred_element_type=jnp.float32
        ).astype(jnp.bfloat16)
        top = pl.multiple_of(s * TALL, 16)
        field_ref[pl.ds(top, TALL), :PASS] = rowfield[:TALL]
        field_ref[pl.ds(top, TALL), PASS:] = rowfield[TALL:]
        return carry

    lax.fori_loop(0, SOURCES, source_step, 0)

    def tile_step(b, carry):
        field = jnp.dot(field_ref[...], cols_ref[b], preferred_element_type=jnp.float32)
        intensity = jnp.zeros((EXT_ROWS, 128), jnp.float32)
        for s in range(SOURCES):
            part = field[s * TALL : s * TALL + EXT_ROWS]
            real, imag = part[:, :128], part[:, 128:]
            intensity = intensity + weights_ref[s] * (real * real + imag * imag)
        lanes = pl.ds(pl.multiple_of(b * 128, 128), 128)
        for z in range(Z):
            a_ref[z, :, lanes] = 1.0 - jnp.exp(-dose_ref[z, :, lanes] * intensity)
        return carry

    lax.fori_loop(0, COL_TILES, tile_step, 0)

    tiles = EXT_ROWS // 8
    row_id = lax.broadcasted_iota(jnp.int32, (8, EXT_COLS), 0)
    quench = [quencher_ref[0], quencher_ref[1]]

    def neighbours(ref, z, t):
        here = ref[z, pl.ds(pl.multiple_of(t * 8, 8), 8), :]
        before = ref[z, pl.ds(pl.multiple_of(jnp.maximum(t - 1, 0) * 8, 8), 8), :]
        after = ref[z, pl.ds(pl.multiple_of(jnp.minimum(t + 1, tiles - 1) * 8, 8), 8), :]
        above = pltpu.roll(jnp.where(row_id == 7, before, here), 1, 0)
        below = pltpu.roll(jnp.where(row_id == 0, after, here), 7, 0)
        left = pltpu.roll(here, 1, 1)
        right = pltpu.roll(here, EXT_COLS - 1, 1)
        return here, (above + below) + (left + right)

    buffers = [(a_ref, b_ref), (b_ref, a_ref), (a_ref, b_ref), (b_ref, a_ref)]
    quenches = [(None, p_ref), (p_ref, q_ref), (q_ref, p_ref), (p_ref, None)]
    for step in range(BAKE):
        old, new = buffers[step]
        q_old, q_new = quenches[step]

        def row_step(t, carry):
            rows = pl.ds(pl.multiple_of(t * 8, 8), 8)
            acid = [neighbours(old, z, t) for z in range(Z)]
            acid_z = acid[0][0] + acid[1][0]
            if q_old is None:
                quench_here = quench
                quench_sum = [4.0 * quench[z] for z in range(Z)]
            elif q_new is None:
                quench_here = [q_old[z, rows, :] for z in range(Z)]
            else:
                pairs = [neighbours(q_old, z, t) for z in range(Z)]
                quench_here = [pair[0] for pair in pairs]
                quench_sum = [pair[1] for pair in pairs]
            quench_z = quench_here[0] + quench_here[1]
            for z in range(Z):
                here, around = acid[z]
                reaction = QUENCH_RATE * here * quench_here[z]
                lap = (around + acid_z) - 6.0 * here
                new[z, rows, :] = here + DIFF_ACID * lap - reaction
                if q_new is not None:
                    q_lap = (quench_sum[z] + quench_z) - 6.0 * quench_here[z]
                    q_new[z, rows, :] = quench_here[z] + DIFF_QUENCH * q_lap - reaction
                if step == 0:
                    sum_ref[z, rows, :] = here[:, :BRICK_COLS]
                else:
                    sum_ref[z, rows, :] = sum_ref[z, rows, :] + here[:, :BRICK_COLS]
            return carry

        lax.fori_loop(0, tiles, row_step, 0)

    for z in range(Z):
        acid_ref[z] = a_ref[z, HALO : HALO + BRICK_ROWS, :BRICK_COLS]
        inhibitor_ref[z] = jnp.exp(-CATALYSIS * sum_ref[z, HALO : HALO + BRICK_ROWS, :])


def resist_call(core, weights, quencher, own, other, window, rows, cols, dose):
    smem = pl.BlockSpec(memory_space=pltpu.SMEM)
    vmem = pl.BlockSpec(memory_space=pltpu.VMEM)
    out = jax.ShapeDtypeStruct((Z, BRICK_ROWS, BRICK_COLS), jnp.float32)
    brick = pltpu.VMEM((Z, EXT_ROWS, EXT_COLS), jnp.float32)
    return pl.pallas_call(
        resist_kernel,
        out_shape=(out, out),
        in_specs=[smem, smem, smem] + [vmem] * 6,
        out_specs=(vmem, vmem),
        scratch_shapes=[
            pltpu.VMEM((PASS, 2 * PASS), jnp.bfloat16),
            pltpu.VMEM((SOURCES * TALL, 2 * PASS), jnp.bfloat16),
            brick, brick, brick, brick,
            pltpu.VMEM((Z, EXT_ROWS, BRICK_COLS), jnp.float32),
        ],
        compiler_params=pltpu.CompilerParams(vmem_limit_bytes=40 * MIB),
        name="resist",
    )(core, weights, quencher, own, other, window, rows, cols, dose)


def ring(axes, step):
    size = lax.axis_size(axes)
    return [(i, (i + step) % size) for i in range(size)]


def extend_dose(dose):
    src, tile = ("zl", "c"), ("y", "zh", "x")
    left = lax.ppermute(dose[:, :, BRICK_COLS - HALO :], src, ring(src, 1))
    right = lax.ppermute(dose[:, :, :HALO], src, ring(src, -1))
    middle = jnp.zeros((Z, BRICK_ROWS, EXT_COLS - BRICK_COLS - 2 * HALO), dose.dtype)
    wide = jnp.concatenate([dose, right, middle, left], axis=2)
    above = lax.ppermute(wide[:, BRICK_ROWS - HALO :], tile, ring(tile, 1))
    below = lax.ppermute(wide[:, :HALO], tile, ring(tile, -1))
    return jnp.concatenate([above, wide, below], axis=1)


def gather_sources(shifts, weights):
    src = ("zl", "c")
    mine = jnp.concatenate([shifts[0].astype(jnp.float32), weights])
    me = lax.axis_index(src)
    rows = [mine]
    for step in (1, 2, 3):
        rows.append(lax.ppermute(mine, src, [(i, i ^ step) for i in range(4)]))
    stacked = jnp.stack(rows)
    order = jnp.bitwise_xor(jnp.arange(SOURCES), me)
    picked = sum(jnp.where((order == k)[:, None], stacked[k][None], 0.0) for k in range(SOURCES))
    return picked[:, :2].astype(jnp.int32), picked[:, 2]


def body(mask_ids, trans_table, pupil, shifts, weights, dose, quencher):
    src = lax.axis_index(("zl", "c"))
    tile = lax.axis_index(("y", "zh", "x"))
    packed = columns_call(trans_table, mask_ids, jnp.asarray(forward_columns()))
    cols = lax.all_to_all(packed, ALL, 0, 0, tiled=True)

    all_shifts, all_weights = gather_sources(shifts, weights)
    flipped = jnp.transpose(pupil, (0, 2, 1))
    zero = jnp.zeros((), jnp.int32)
    windows = [
        lax.dynamic_slice(flipped, (zero, SHIFT - all_shifts[s, 1], SHIFT - all_shifts[s, 0]), (2, PASS, PASS))
        for s in range(SOURCES)
    ]
    window = jnp.concatenate(windows, axis=0)
    dose_ext = extend_dose(dose)
    row_table = lax.dynamic_index_in_dim(jnp.asarray(inverse_rows(32)), tile, 0, keepdims=False)
    col_table = lax.dynamic_index_in_dim(jnp.asarray(inverse_cols(4)), src, 0, keepdims=False)

    block = spectrum_call(jnp.asarray(forward_rows()), cols)
    own = lax.all_to_all(block, ("y", "x"), 0, 0, tiled=True)
    other = lax.ppermute(own, "c", [(0, 1), (1, 0)])
    core = lax.axis_index("c").reshape(1).astype(jnp.int32)
    return resist_call(core, all_weights, quencher, own, other, window, row_table, col_table, dose_ext)


def solution(mesh):
    parts = Mesh(mesh.devices.reshape(2, 2, 4, 2, 4), ALL)
    src, tile = ("zl", "c"), ("y", "zh", "x")
    inner = jax.shard_map(
        body,
        mesh=parts,
        in_specs=(
            P(ALL, None),
            P(),
            P(),
            P(src, None),
            P(src),
            P(None, tile, src),
            P(),
        ),
        out_specs=(P(None, tile, src), P(None, tile, src)),
        check_vma=False,
    )
    return inner
```

time: 556 us -> 127 us (0.23); the launches traced: 546 us -> 126 us
  waiting for transfers between devices: 291 us -> 6.58 us
  other arithmetic: 171 us -> 8.08 us
  Pallas kernels: 0 us -> 30.5 us
  matrix products: 26 us -> 0 us
  local copies, waits for them, and re-layouts: 22.9 us -> 42.8 us
  starting transfers between devices: 17.1 us -> 26.9 us
  between operations: 18.2 us -> 11.2 us
    all_gather x1 -> x0, waiting for transfers between devices: 210 us -> none  [body(): lax.all_gather(columns, ('src', 'tile'), axis=0, tiled=True)]
    dot_general x2 -> x0, other arithmetic: 65.2 us -> none  [the longest x1 32.7 us: row_terms(): jnp.dot(sine.astype(jnp.bfloat16), piece, preferred_element_type=jnp.floa...]
    ppermute x16 -> x8, waiting for transfers between devices: 53.2 us -> 1.36 us  [the longest x1 1.34 us: extend_dose(): above = lax.ppermute(wide[:, BRICK_ROWS - HALO:], tile, ring(tile, 1))]
    another operation x16 -> x0, other arithmetic: 44.6 us -> none
    convert_element_type x1 -> x2, other arithmetic: 36.7 us -> 0.67 us  [the longest x1 0.66 us: gather_sources(): mine = jnp.concatenate([shifts[0].astype(jnp.float32), weights])]
    pallas_call x0 -> x3, Pallas kernels: none -> 30.5 us  [the longest x1 22.3 us: resist_call(): pl.pallas_call(resist_kernel, out_shape=(out, out), in_specs=[smem, smem,...]
    reduce_scatter x1 -> x0, waiting for transfers between devices: 27.7 us -> none  [body(): lax.psum_scatter(partial_value, 'src', scatter_dimension=1, tiled=True)]
    dot_general x8 -> x0, matrix products: 26 us -> none  [the longest x1 8.45 us: row_terms(): jnp.dot(cosine.astype(jnp.bfloat16), piece, preferred_element_type=jnp.fl...]
  transfers between devices with their start and end apart: 18 -> 10, of which waited for: 17 -> 2; matrix products, arithmetic and copies ran while one was open for 20% -> 31% of each run, Pallas kernels for 0% -> 7%
where the time goes in v1:
time: 127 us; the launch traced here: 126 us
  local copies, waits for them, and re-layouts  42.8 us (34%)
  Pallas kernels  30.5 us (24%)
  starting transfers between devices  26.9 us (21%)
  between operations  11.2 us (9%)
  other arithmetic  8.08 us (6%)
  waiting for transfers between devices  6.58 us (5%)
    unnamed x16, local copies, waits for them, and re-layouts  22.4 us
    pallas_call x1, Pallas kernels, resist_call(): pl.pallas_call(resist_kernel, out_shape=(out, out), in_specs=[smem, smem,...  22.3 us
    all_to_all x1, starting transfers between devices, body(): cols = lax.all_to_all(packed, ALL, 0, 0, tiled=True)  10.1 us
    another operation x1, local copies, waits for them, and re-layouts  9.52 us
    concatenate x1, other arithmetic, body(): window = jnp.concatenate(windows, axis=0)  5.87 us
    ppermute x1, starting transfers between devices, extend_dose(): below = lax.ppermute(wide[:, :HALO], tile, ring(tile, -1))  5.67 us
    all_to_all x1, waiting for transfers between devices, body(): cols = lax.all_to_all(packed, ALL, 0, 0, tiled=True)  5.22 us
    squeeze x1, local copies, waits for them, and re-layouts, body(): lax.dynamic_index_in_dim(jnp.asarray(inverse_cols(4)), src, 0, keepdims=F...  4.88 us
  transfers between devices with their start and end apart: 10, of which 2 were waited for; matrix products, arithmetic and copies ran while one was open for 31% of the time, Pallas kernels for 7%

profile of v1, /device:TPU:1, one launch (start us, length us, event | category | flops | bytes accessed | tf_op | source)
XLA Modules:
  0.0 126.0 jit_solution(4792741085804945150)
XLA Ops:
  0.6 0.7 convert_bitcast_fusion
  1.9 0.1 pad_maximum_fusion.2
  2.0 1.4 %collective-permute-start = (f32[3]{0:T(128)S(1)}, f32[3]{0:T(128)S(1)}, u32[]{:S(2)}, u32[]{:S(2)}) collective-permute-start(f32[3]{0:T(128)S(1)} %pad_maximum_fusion.2), channel_id=1, source_target_pairs={{0,32},{32,0},{64,96},{96,64},{1,33},{33,1},{65,97},{97,65},{2,34}... | collective-permute-start | bytes 44 | tf_op jit(solution)/shard_map/ppermute | solution.py:352
  3.5 1.7 %collective-permute-start.1 = (f32[3]{0:T(128)S(1)}, f32[3]{0:T(128)S(1)}, u32[]{:S(2)}, u32[]{:S(2)}) collective-permute-start(f32[3]{0:T(128)S(1)} %pad_maximum_fusion.2), channel_id=1, source_target_pairs={{0,64},{32,96},{64,0},{96,32},{1,65},{33,97},{65,1},{97,33},{2,66}... | collective-permute-start | bytes 44 | tf_op jit(solution)/shard_map/ppermute | solution.py:352
  5.2 0.1 collective-permute-start.2
  5.2 1.1 fusion.5
  6.3 0.4 collective-permute-start.4
  6.7 1.4 %collective-permute-start.5 = (f32[2,128,4]{2,1,0:T(8,128)S(1)}, f32[2,128,4]{2,1,0:T(8,128)S(1)}, u32[]{:S(2)}, u32[]{:S(2)}) collective-permute-start(f32[2,128,4]{2,1,0:T(8,128)S(1)} %get-tuple-element.8), channel_id=1, source_target_pairs={{0,32},{32,64},{64,96},{96,0},{1,33},{33,65},{65,97},{97,1},{2,34}... | collective-permute-start | bytes 12296 | tf_op jit(solution)/shard_map/ppermute | solution.py:337
  8.2 0.0 copy-start.2
  8.2 3.4 %copy-done.2 = bf16[4096,1024]{1,0:T(8,128)(2,1)S(1)} copy-done((bf16[4096,1024]{1,0:T(8,128)(2,1)S(1)}, bf16[4096,1024]{1,0:T(8,128)(2,1)}, u32[]{:S(2)}) %copy-start.2) | copy-done | bytes 8388632
  11.5 1.0 copy-done.3
  12.6 0.7 copy-done.4
  13.3 3.6 %columns.1 = bf16[1024,128]{1,0:T(8,128)(2,1)} custom-call(f32[2,4]{1,0:T(2,128)S(1)} %copy-done.4, s32[32,4096]{1,0:T(8,128)S(1)} %copy-done.3, bf16[4096,1024]{1,0:T(8,128)(2,1)S(1)} %copy-done.2), custom_call_target="tpu_custom_call" | custom-call | tf_op jit(solution)/shard_map/columns/pallas_call | solution.py:148
  16.9 10.1 %all-to-all-start = ((bf16[128,8,128]{2,1,0:T(8,128)(2,1)}), bf16[128,8,128]{2,1,0:T(8,128)(2,1)S(1)}, u32[]{:S(2)}, u32[]{:S(2)}) async-start(bf16[128,8,128]{2,1,0:T(8,128)(2,1)} %bitcast.3), calls=%async_computation | async-start | bytes 524288 | tf_op jit(solution)/shard_map/all_to_all | solution.py:363
  27.0 1.1 dynamic-slice_bitcast_fusion.1.rows_ref
  28.1 4.9 %dynamic-slice_bitcast_fusion.cols_ref = bf16[9,1024,256]{2,1,0:T(8,128)(2,1)} fusion(bf16[4,9,1024,256]{3,2,1,0:T(8,128)(2,1)} %constant.84.clone, s32[]{:T(128)S(6)} %select_n.58), kind=kLoop, calls=%fused_computation.1 | loop fusion | bytes 9437188 | tf_op jit(solution)/shard_map/jit(dynamic_index_in_dim)/squeeze | solution.py:375
  33.0 5.2 %all-to-all-done = bf16[128,8,128]{2,1,0:T(8,128)(2,1)S(1)} async-done(((bf16[128,8,128]{2,1,0:T(8,128)(2,1)}), bf16[128,8,128]{2,1,0:T(8,128)(2,1)S(1)}, u32[]{:S(2)}, u32[]{:S(2)}) %all-to-all-start) | async-done | bytes 262176 | tf_op jit(solution)/shard_map/all_to_all | solution.py:363
  38.2 3.4 %copy-done.1 = bf16[4,1024,1024]{2,1,0:T(8,128)(2,1)S(1)} copy-done((bf16[4,1024,1024]{2,1,0:T(8,128)(2,1)S(1)}, bf16[4,1024,1024]{2,1,0:T(8,128)(2,1)}, u32[]{:S(2)}) %copy-start.1) | copy-done | bytes 8388632
  41.6 4.6 %spectrum.1 = f32[512,512]{1,0:T(8,128)} custom-call(bf16[4,1024,1024]{2,1,0:T(8,128)(2,1)S(1)} %copy-done.1, bf16[1024,128]{1,0:T(8,128)(2,1)S(1)} %bitcast.35), custom_call_target="tpu_custom_call" | custom-call | tf_op jit(solution)/shard_map/spectrum/pallas_call | solution.py:192
  46.2 3.7 %all-to-all-start.1 = ((f32[16,32,512]{2,1,0:T(8,128)}), f32[16,32,512]{2,1,0:T(8,128)S(1)}, u32[]{:S(2)}, u32[]{:S(2)}) async-start(f32[16,32,512]{2,1,0:T(8,128)} %bitcast.5), calls=%async_computation.1 | async-start | bytes 2097152 | tf_op jit(solution)/shard_map/all_to_all | solution.py:378
  49.9 0.0 collective-permute-done
  49.9 0.0 collective-permute-done.1
  49.9 0.0 collective-permute-done.2
  49.9 0.1 select_add_fusion
  50.0 0.7 fusion.6
  60.5 9.5 %constant_dynamic-slice_fusion.3 = (f32[2,512,512]{2,1,0:T(8,128)}, f32[2,512,512]{2,1,0:T(8,128)}, f32[2,512,512]{2,1,0:T(8,128)}, f32[2,512,512]{2,1,0:T(8,128)}) fusion(f32[2,640,640]{2,1,0:T(8,128)} %param.13, s32[]{:T(128)S(6)} %select_n.49, s32[]{:T(128)S(6)} %select_n.50, s32[]{:T(128)S(6)} %select_n.53, s32[]{:T(128)S(6)} %select_n.54, ...), kind=kLoop, calls=%fused_computation.8 | loop fusion | bytes 16777248 | tf_op jit(solution)/shard_map/dynamic-slice
  70.0 2.9 %copy.17 = f32[2,512,512]{1,2,0:T(8,128)} copy(f32[2,512,512]{2,1,0:T(8,128)} %get-tuple-element.2) | data formatting | bytes 4194304
  72.9 2.9 %copy.18 = f32[2,512,512]{1,2,0:T(8,128)} copy(f32[2,512,512]{2,1,0:T(8,128)} %get-tuple-element.4) | data formatting | bytes 4194304
  75.8 2.9 %copy.19 = f32[2,512,512]{1,2,0:T(8,128)} copy(f32[2,512,512]{2,1,0:T(8,128)} %get-tuple-element.3) | data formatting | bytes 4194304
  78.7 2.9 %copy.20 = f32[2,512,512]{1,2,0:T(8,128)} copy(f32[2,512,512]{2,1,0:T(8,128)} %get-tuple-element.5) | data formatting | bytes 4194304
  81.6 0.0 all-to-all-done.1
  81.6 0.8 collective-permute-start.3
  82.4 5.9 %pad_maximum_fusion.window_ref = f32[8,512,512]{2,1,0:T(8,128)} fusion(f32[2,512,512]{2,1,0:T(8,128)} %bitcast.39, f32[2,512,512]{2,1,0:T(8,128)} %bitcast.38, f32[2,512,512]{2,1,0:T(8,128)} %bitcast.37, f32[2,512,512]{2,1,0:T(8,128)} %bitcast.36), kind=kLoop, calls=%fused_computation | loop fusion | flops 6291456 | bytes 16777216 | tf_op jit(solution)/shard_map/concatenate | solution.py:372
  88.2 0.0 collective-permute-done.4
  88.2 0.0 collective-permute-done.5
  88.3 0.0 copy-start.5
  88.3 2.2 %concatenate.14 = f32[2,128,1152]{2,1,0:T(8,128)} concatenate(f32[2,128,1024]{2,1,0:T(8,128)} %param.16, f32[2,128,4]{2,1,0:T(8,128)S(1)} %collective-permute-done.4, f32[2,128,120]{2,1,0:T(8,128)S(1)} %broadcast_in_dim.69, f32[2,128,4]{2,1,0:T(8,128)S(1)} %collective-permute-done.5), dimensions={2} | concatenate | bytes 2359296 | tf_op jit(solution)/shard_map/concatenate | solution.py:340
  90.5 0.9 fusion.4
  91.4 1.6 %collective-permute-start.6 = (f32[2,4,1152]{2,1,0:T(4,128)S(1)}, f32[2,4,1152]{2,1,0:T(4,128)S(1)}, u32[]{:S(2)}, u32[]{:S(2)}) collective-permute-start(f32[2,4,1152]{2,1,0:T(4,128)S(1)} %get-tuple-element.6), channel_id=1, source_target_pairs={{0,1},{1,2},{2,3},{3,4},{4,5},{5,6},{6,7},{7,8},{8,9},{9,10},{10,1... | collective-permute-start | bytes 110600 | tf_op jit(solution)/shard_map/ppermute | solution.py:341
  93.0 5.7 %collective-permute-start.7 = (f32[2,4,1152]{2,1,0:T(4,128)S(1)}, f32[2,4,1152]{2,1,0:T(4,128)S(1)}, u32[]{:S(2)}, u32[]{:S(2)}) collective-permute-start(f32[2,4,1152]{2,1,0:T(4,128)S(1)} %get-tuple-element.7), channel_id=1, source_target_pairs={{0,31},{1,0},{2,1},{3,2},{4,3},{5,4},{6,5},{7,6},{8,7},{9,8},{10,9... | collective-permute-start | bytes 110600 | tf_op jit(solution)/shard_map/ppermute | solution.py:342
  98.7 1.3 %collective-permute-done.6 = f32[2,4,1152]{2,1,0:T(4,128)S(1)} collective-permute-done((f32[2,4,1152]{2,1,0:T(4,128)S(1)}, f32[2,4,1152]{2,1,0:T(4,128)S(1)}, u32[]{:S(2)}, u32[]{:S(2)}) %collective-permute-start.6) | collective-permute-done | bytes 36896 | tf_op jit(solution)/shard_map/ppermute | solution.py:341
  100.0 0.0 collective-permute-done.7
  100.0 1.4 %pad_maximum_fusion.1.dose_ref = f32[2,136,1152]{2,1,0:T(8,128)S(1)} fusion(f32[2,4,1152]{2,1,0:T(4,128)S(1)} %collective-permute-done.7, f32[2,128,1152]{2,1,0:T(8,128)} %concatenate.14, f32[2,4,1152]{2,1,0:T(4,128)S(1)} %collective-permute-done.6), kind=kLoop, calls=%fused_computation.2 | loop fusion | flops 626688 | bytes 2506752 | tf_op jit(solution)/shard_map/concatenate | solution.py:343
  101.4 0.0 collective-permute-done.3.other_ref
  101.4 0.0 copy-done.5
  101.4 0.0 copy-start
  101.4 2.3 %copy-done = bf16[9,1024,256]{2,1,0:T(8,128)(2,1)S(1)} copy-done((bf16[9,1024,256]{2,1,0:T(8,128)(2,1)S(1)}, bf16[9,1024,256]{2,1,0:T(8,128)(2,1)}, u32[]{:S(2)}) %copy-start) | copy-done | bytes 4718616
  103.7 22.3 %resist.1 = (f32[2,128,1024]{2,1,0:T(8,128)}, f32[2,128,1024]{2,1,0:T(8,128)}) custom-call(s32[1]{0:T(128)} %bitcast.core_ref, f32[4]{0:T(128)S(1)} %slice_bitcast_fusion.weights_ref, f32[2]{0:T(128)S(1)} %copy-done.5, f32[512,512]{1,0:T(8,128)S(1)} %bitcast.34, f32[512,512]{1,0:T(8,128)S(1)} %collective-permute-done.3.other_ref, ...), custom_call_target="tpu_custom_call" | custom-call | tf_op jit(solution)/shard_map/resist/pallas_call | solution.py:314
  (8 shorter events, 0.0 us)
Async XLA Ops:
  2.0 47.9 %collective-permute-start = (f32[3]{0:T(128)S(1)}, f32[3]{0:T(128)S(1)}, u32[]{:S(2)}, u32[]{:S(2)}) collective-permute-start(f32[3]{0:T(128)S(1)} %pad_maximum_fusion.2), channel_id=1, source_target_pairs={{0,32},{32,0},{64,96},{96,64},{1,33},{33,1},{65,97},{97,65},{2,34}... | collective-permute-start | bytes 44 | tf_op jit(solution)/shard_map/ppermute | solution.py:352
  3.5 46.5 %collective-permute-start.1 = (f32[3]{0:T(128)S(1)}, f32[3]{0:T(128)S(1)}, u32[]{:S(2)}, u32[]{:S(2)}) collective-permute-start(f32[3]{0:T(128)S(1)} %pad_maximum_fusion.2), channel_id=1, source_target_pairs={{0,64},{32,96},{64,0},{96,32},{1,65},{33,97},{65,1},{97,33},{2,66}... | collective-permute-start | bytes 44 | tf_op jit(solution)/shard_map/ppermute | solution.py:352
  5.2 44.7 %collective-permute-start.2 = (f32[3]{0:T(128)S(1)}, f32[3]{0:T(128)S(1)}, u32[]{:S(2)}, u32[]{:S(2)}) collective-permute-start(f32[3]{0:T(128)S(1)} %pad_maximum_fusion.2), channel_id=1, source_target_pairs={{0,96},{32,64},{64,32},{96,0},{1,97},{33,65},{65,33},{97,1},{2,98}... | collective-permute-start | bytes 44 | tf_op jit(solution)/shard_map/ppermute | solution.py:352
  6.3 81.9 %collective-permute-start.4 = (f32[2,128,4]{2,1,0:T(8,128)S(1)}, f32[2,128,4]{2,1,0:T(8,128)S(1)}, u32[]{:S(2)}, u32[]{:S(2)}) collective-permute-start(f32[2,128,4]{2,1,0:T(8,128)S(1)} %get-tuple-element.9), channel_id=1, source_target_pairs={{0,96},{32,0},{64,32},{96,64},{1,97},{33,1},{65,33},{97,65},{2,98}... | collective-permute-start | bytes 12296 | tf_op jit(solution)/shard_map/ppermute | solution.py:338
  6.7 81.5 %collective-permute-start.5 = (f32[2,128,4]{2,1,0:T(8,128)S(1)}, f32[2,128,4]{2,1,0:T(8,128)S(1)}, u32[]{:S(2)}, u32[]{:S(2)}) collective-permute-start(f32[2,128,4]{2,1,0:T(8,128)S(1)} %get-tuple-element.8), channel_id=1, source_target_pairs={{0,32},{32,64},{64,96},{96,0},{1,33},{33,65},{65,97},{97,1},{2,34}... | collective-permute-start | bytes 12296 | tf_op jit(solution)/shard_map/ppermute | solution.py:337
  8.2 3.4 %copy-start.2 = (bf16[4096,1024]{1,0:T(8,128)(2,1)S(1)}, bf16[4096,1024]{1,0:T(8,128)(2,1)}, u32[]{:S(2)}) copy-start(bf16[4096,1024]{1,0:T(8,128)(2,1)} %constant.82.clone.table_ref) | copy-start | bytes 25165828
  11.5 1.0 copy-start.3
  12.6 0.7 copy-start.4
  16.9 21.3 %all-to-all-start = ((bf16[128,8,128]{2,1,0:T(8,128)(2,1)}), bf16[128,8,128]{2,1,0:T(8,128)(2,1)S(1)}, u32[]{:S(2)}, u32[]{:S(2)}) async-start(bf16[128,8,128]{2,1,0:T(8,128)(2,1)} %bitcast.3), calls=%async_computation | async-start | bytes 524288 | tf_op jit(solution)/shard_map/all_to_all | solution.py:363
  38.2 3.4 %copy-start.1 = (bf16[4,1024,1024]{2,1,0:T(8,128)(2,1)S(1)}, bf16[4,1024,1024]{2,1,0:T(8,128)(2,1)}, u32[]{:S(2)}) copy-start(bf16[4,1024,1024]{2,1,0:T(8,128)(2,1)} %constant.85.clone.table_ref) | copy-start | bytes 25165828
  46.2 35.4 %all-to-all-start.1 = ((f32[16,32,512]{2,1,0:T(8,128)}), f32[16,32,512]{2,1,0:T(8,128)S(1)}, u32[]{:S(2)}, u32[]{:S(2)}) async-start(f32[16,32,512]{2,1,0:T(8,128)} %bitcast.5), calls=%async_computation.1 | async-start | bytes 2097152 | tf_op jit(solution)/shard_map/all_to_all | solution.py:378
  81.6 19.8 %collective-permute-start.3 = (f32[512,512]{1,0:T(8,128)S(1)}, f32[512,512]{1,0:T(8,128)S(1)}, u32[]{:S(2)}, u32[]{:S(2)}) collective-permute-start(f32[512,512]{1,0:T(8,128)S(1)} %bitcast.33), channel_id=1, source_target_pairs={{0,32},{32,0},{1,33},{33,1},{2,34},{34,2},{3,35},{35,3},{4,36},{36... | collective-permute-start | bytes 3145736 | tf_op jit(solution)/shard_map/ppermute | solution.py:379
  88.3 13.1 %copy-start.5 = (f32[2]{0:T(128)S(1)}, f32[2]{0:T(128)}, u32[]{:S(2)}) copy-start(f32[2]{0:T(128)} %quencher_ref.1) | copy-start | bytes 28
  91.4 8.6 %collective-permute-start.6 = (f32[2,4,1152]{2,1,0:T(4,128)S(1)}, f32[2,4,1152]{2,1,0:T(4,128)S(1)}, u32[]{:S(2)}, u32[]{:S(2)}) collective-permute-start(f32[2,4,1152]{2,1,0:T(4,128)S(1)} %get-tuple-element.6), channel_id=1, source_target_pairs={{0,1},{1,2},{2,3},{3,4},{4,5},{5,6},{6,7},{7,8},{8,9},{9,10},{10,1... | collective-permute-start | bytes 110600 | tf_op jit(solution)/shard_map/ppermute | solution.py:341
  93.0 7.0 %collective-permute-start.7 = (f32[2,4,1152]{2,1,0:T(4,128)S(1)}, f32[2,4,1152]{2,1,0:T(4,128)S(1)}, u32[]{:S(2)}, u32[]{:S(2)}) collective-permute-start(f32[2,4,1152]{2,1,0:T(4,128)S(1)} %get-tuple-element.7), channel_id=1, source_target_pairs={{0,31},{1,0},{2,1},{3,2},{4,3},{5,4},{6,5},{7,6},{8,7},{9,8},{10,9... | collective-permute-start | bytes 110600 | tf_op jit(solution)/shard_map/ppermute | solution.py:342
  101.4 2.3 %copy-start = (bf16[9,1024,256]{2,1,0:T(8,128)(2,1)S(1)}, bf16[9,1024,256]{2,1,0:T(8,128)(2,1)}, u32[]{:S(2)}) copy-start(bf16[9,1024,256]{2,1,0:T(8,128)(2,1)} %dynamic-slice_bitcast_fusion.cols_ref) | copy-start | bytes 14155780

commit v2 on v1

v2 whole, which is shorter than its diff:
```python
import math

import jax
import jax.numpy as jnp
import numpy as np
from jax import lax
from jax.experimental import pallas as pl
from jax.experimental.pallas import tpu as pltpu
from jax.sharding import Mesh, PartitionSpec as P

NPIX = 4096
PASS = 512
SHIFT = 64
LEVELS = 4
SOURCES = 4
BAKE = 4
Z = 2
PUPIL_TILES = (PASS + 2 * SHIFT) // 8
DIFF_ACID = 0.12
DIFF_QUENCH = 0.04
QUENCH_RATE = 0.6
CATALYSIS = 0.4

DEVICES = 128
ROWS = NPIX // DEVICES
OWNERS = 32
FREQS = PASS // OWNERS
WIDE = 2 * FREQS
HALO = 4
TALL = 144
BRICK_ROWS = 128
BRICK_COLS = 1024
EXT_ROWS = BRICK_ROWS + 2 * HALO
EXT_COLS = BRICK_COLS + 128
COL_TILES = EXT_COLS // 128
ALL = ("zl", "c", "y", "zh", "x")
MIB = 1024 * 1024
FILTER_UNROLL = 16
FIELD_UNROLL = 9
BAKE_UNROLL = 17


def cos_sin(first, second):
    theta = (np.mod(first[:, None] * second[None, :], NPIX)).astype(np.float32)
    theta = (theta * np.float32(2.0 * math.pi / NPIX)).astype(np.float64)
    return np.cos(theta).astype(np.float32), np.sin(theta).astype(np.float32)


def bf16(table):
    return table.astype(jnp.bfloat16)


FREQ = np.arange(PASS, dtype=np.int64) - PASS // 2
HALF = PASS // 2


def forward_columns():
    return bf16(np.concatenate(cos_sin(np.arange(NPIX), np.arange(HALF)), axis=1))


def forward_rows():
    order = np.arange(NPIX).reshape(DEVICES, 4, 8).transpose(1, 0, 2).reshape(NPIX)
    both = np.concatenate(cos_sin(np.arange(HALF), order), axis=0)
    return bf16(both.reshape(PASS, 4, NPIX // 4).transpose(1, 0, 2))


def edge_columns():
    cosine, sine = cos_sin(np.array([HALF]), np.arange(128))
    return np.asarray(bf16(np.concatenate([cosine, sine], axis=0))).astype(np.float32)


def edge_rows():
    rows = np.arange(4)[None, :] * 8 + np.arange(8)[:, None]
    cosine, sine = cos_sin(np.array([HALF]), rows.reshape(-1))
    both = np.stack([cosine.reshape(8, 4), sine.reshape(8, 4)])
    return np.asarray(bf16(np.repeat(both, WIDE, axis=2))).astype(np.float32)


def inverse_rows(tiles):
    blocks = []
    for tile in range(tiles):
        local = np.arange(TALL)
        local = np.where(local < BRICK_ROWS + HALO, local, local - EXT_ROWS)
        pixels = np.mod(tile * BRICK_ROWS + local, NPIX)
        cosine, sine = cos_sin(pixels, FREQ)
        upper = np.concatenate([cosine, -sine], axis=1)
        lower = np.concatenate([sine, cosine], axis=1)
        blocks.append(np.concatenate([upper, lower], axis=0))
    return bf16(np.stack(blocks))


def inverse_cols(sources):
    lanes = np.arange(EXT_COLS)
    local = np.where(lanes < BRICK_COLS + 64, lanes, lanes - EXT_COLS)
    blocks = []
    for source in range(sources):
        pixels = np.mod(source * BRICK_COLS + local, NPIX)
        cosine, sine = cos_sin(FREQ, pixels)
        real = np.concatenate([cosine, -sine], axis=0).reshape(2 * PASS, COL_TILES, 1, 128)
        imag = np.concatenate([sine, cosine], axis=0).reshape(2 * PASS, COL_TILES, 1, 128)
        both = np.concatenate([real, imag], axis=2).reshape(2 * PASS, COL_TILES, 256)
        blocks.append(both.transpose(1, 0, 2))
    return bf16(np.stack(blocks))


def lane_ids(shape):
    return lax.broadcasted_iota(jnp.int32, shape, len(shape) - 1)


def columns_kernel(trans_ref, ids_ref, table_ref, edge_ref, out_ref, acc_ref, sum_ref, perm_ref):
    step = pl.program_id(0)

    @pl.when(step == 0)
    def _():
        acc_ref[...] = jnp.zeros_like(acc_ref)
        sum_ref[...] = jnp.zeros_like(sum_ref)
        source = lax.broadcasted_iota(jnp.int32, (PASS, PASS), 0)
        lane = lax.broadcasted_iota(jnp.int32, (PASS, PASS), 1)
        plane, place = lane // FREQS % 2, lane // WIDE * FREQS + lane % FREQS
        perm_ref[0] = (source == plane * HALF + (HALF - place) % HALF).astype(jnp.float32).astype(jnp.bfloat16)
        perm_ref[1] = (source == plane * HALF + place).astype(jnp.float32).astype(jnp.bfloat16)

    ids = ids_ref[...]
    parts = []
    for plane in range(2):
        value = jnp.zeros(ids.shape, jnp.float32)
        for level in range(LEVELS):
            value = jnp.where(ids == level, trans_ref[plane, level], value)
        parts.append(value)
    trans = jnp.concatenate(parts, axis=0).astype(jnp.bfloat16)
    acc_ref[...] += jnp.dot(trans, table_ref[...], preferred_element_type=jnp.float32)
    exact = trans.astype(jnp.float32)
    total = sum_ref[...]
    for tile in range(ids.shape[1] // 128):
        total = total + exact[:, 128 * tile : 128 * tile + 128]
    sum_ref[...] = total

    @pl.when(step == pl.num_programs(0) - 1)
    def _():
        edge_cos = jnp.sum(sum_ref[...] * edge_ref[0:1, :], axis=1, keepdims=True)
        edge_sin = jnp.sum(sum_ref[...] * edge_ref[1:2, :], axis=1, keepdims=True)
        cos_real, cos_imag = acc_ref[:ROWS, :HALF], acc_ref[ROWS:, :HALF]
        sin_real, sin_imag = acc_ref[:ROWS, HALF:], acc_ref[ROWS:, HALF:]
        first = lane_ids((ROWS, HALF)) == 0
        low_real = jnp.where(first, edge_cos[:ROWS] - edge_sin[ROWS:], cos_real - sin_imag)
        low_imag = jnp.where(first, edge_cos[ROWS:] + edge_sin[:ROWS], cos_imag + sin_real)
        low = jnp.concatenate([low_real, low_imag], axis=1).astype(jnp.bfloat16)
        high = jnp.concatenate([cos_real + sin_imag, cos_imag - sin_real], axis=1).astype(jnp.bfloat16)
        sides = [
            jnp.dot(low, perm_ref[0], preferred_element_type=jnp.float32),
            jnp.dot(high, perm_ref[1], preferred_element_type=jnp.float32),
        ]
        group = lane_ids((8, 128)) // WIDE
        chunks = []
        for owner in range(OWNERS):
            major, minor = owner % 16 // 4, owner % 4
            chunk = jnp.zeros((8, 128), jnp.float32)
            for q in range(4):
                piece = sides[owner // 16][8 * q : 8 * q + 8, 128 * major : 128 * major + 128]
                turn = (q - minor) % 4 * WIDE
                piece = pltpu.roll(piece, turn, 1) if turn else piece
                chunk = jnp.where(group == q, piece, chunk)
            chunks.append(chunk)
        for pair in range(DEVICES // 2):
            both = []
            for dest in (2 * pair, 2 * pair + 1):
                core, y, x = dest // 32 % 2, dest // 8 % 4, dest % 4
                both.append(chunks[core * 16 + y * 4 + x])
            out_ref[16 * pair : 16 * pair + 16, :] = jnp.concatenate(both, axis=0).astype(jnp.bfloat16)


def columns_call(trans_table, mask_ids, table, edge):
    steps = 4
    depth = NPIX // steps
    return pl.pallas_call(
        columns_kernel,
        grid=(steps,),
        out_shape=jax.ShapeDtypeStruct((DEVICES * 8, 128), jnp.bfloat16),
        in_specs=[
            pl.BlockSpec(memory_space=pltpu.SMEM),
            pl.BlockSpec((ROWS, depth), lambda k: (0, k)),
            pl.BlockSpec((depth, PASS), lambda k: (k, 0)),
            pl.BlockSpec((2, 128), lambda k: (0, 0)),
        ],
        out_specs=pl.BlockSpec((DEVICES * 8, 128), lambda k: (0, 0)),
        scratch_shapes=[
            pltpu.VMEM((2 * ROWS, PASS), jnp.float32),
            pltpu.VMEM((2 * ROWS, 128), jnp.float32),
            pltpu.VMEM((2, PASS, PASS), jnp.bfloat16),
        ],
        compiler_params=pltpu.CompilerParams(vmem_limit_bytes=56 * MIB),
        name="columns",
    )(trans_table, mask_ids, table, edge)


def spectrum_kernel(table_ref, cols_ref, edge_ref, out_ref, acc_ref):
    step = pl.program_id(0)
    product = jnp.dot(table_ref[0], cols_ref[...], preferred_element_type=jnp.float32)
    group = lane_ids(product.shape) // WIDE

    @pl.when(step == 0)
    def _():
        acc_ref[...] = product

    @pl.when(step > 0)
    def _():
        acc_ref[...] = jnp.where(group == step, product, acc_ref[...])

    @pl.when(step == pl.num_programs(0) - 1)
    def _():
        columns = cols_ref[...].astype(jnp.float32)
        total = [columns[16 * k : 16 * k + 16] for k in range(DEVICES // 2)]
        while len(total) > 1:
            total = [a + b for a, b in zip(total[::2], total[1::2])]
        total = total[0][:8] + total[0][8:]
        edge_cos = jnp.sum(total * edge_ref[0], axis=0, keepdims=True)
        edge_sin = jnp.sum(total * edge_ref[1], axis=0, keepdims=True)

        def fold(value):
            value = value + pltpu.roll(value, 64, 1)
            return value + pltpu.roll(value, 32, 1)

        def turn(value):
            is_real = lane_ids(value.shape) % WIDE < FREQS
            return jnp.where(is_real, pltpu.roll(value, 128 - FREQS, 1), -pltpu.roll(value, FREQS, 1))

        edges = fold(jnp.concatenate([edge_cos, edge_sin, jnp.zeros((6, 128), jnp.float32)], axis=0))
        edge = edges[0:1] - turn(edges)[1:2]
        folded = fold(acc_ref[...])
        cosine, turned = folded[:HALF], turn(folded[HALF:])
        first = lax.broadcasted_iota(jnp.int32, cosine.shape, 0) == 0
        scale = 1.0 / (NPIX * NPIX)
        high = jnp.transpose((cosine + turned) * scale)[:WIDE]
        low = jnp.transpose(jnp.where(first, edge, cosine - turned) * scale)[:WIDE]
        source = lax.broadcasted_iota(jnp.int32, (HALF, HALF), 0)
        place = lax.broadcasted_iota(jnp.int32, (HALF, HALF), 1)
        perm = (source == (HALF - place) % HALF).astype(jnp.float32).astype(jnp.bfloat16)
        pieces = []
        rest = low
        for _ in range(3):
            piece = rest.astype(jnp.bfloat16)
            rest = rest - piece.astype(jnp.float32)
            pieces.append(jnp.dot(piece, perm, preferred_element_type=jnp.float32))
        block = jnp.concatenate([pieces[0] + pieces[1] + pieces[2], high], axis=1)
        for dest in range(16):
            out_ref[dest * WIDE : (dest + 1) * WIDE, :] = block


def spectrum_call(table, cols, edge):
    return pl.pallas_call(
        spectrum_kernel,
        grid=(4,),
        out_shape=jax.ShapeDtypeStruct((16 * WIDE, PASS), jnp.float32),
        in_specs=[
            pl.BlockSpec((1, PASS, NPIX // 4), lambda q: (q, 0, 0)),
            pl.BlockSpec((NPIX // 4, 128), lambda q: (0, 0)),
            pl.BlockSpec((2, 8, 128), lambda q: (0, 0, 0)),
        ],
        out_specs=pl.BlockSpec((16 * WIDE, PASS), lambda q: (0, 0)),
        scratch_shapes=[pltpu.VMEM((PASS, 128), jnp.float32)],
        compiler_params=pltpu.CompilerParams(vmem_limit_bytes=56 * MIB),
        name="spectrum",
    )(table, cols, edge)


def pack_kernel(shifts_ref, weights_ref, pupil_ref, dose_ref, turned_ref, last_ref, first_ref, note_ref):
    blocks = pupil_ref.shape[1] // 128
    for plane in range(2):
        for i in range(blocks):
            for j in range(blocks):
                piece = pupil_ref[plane, 128 * i : 128 * i + 128, 128 * j : 128 * j + 128]
                turned_ref[plane, 128 * j : 128 * j + 128, 128 * i : 128 * i + 128] = jnp.transpose(piece)

    def note(shape):
        lane = lane_ids(shape)
        shift_x, shift_y = shifts_ref[0, 0].astype(jnp.float32), shifts_ref[0, 1].astype(jnp.float32)
        return jnp.where(lane == 64, shift_x, jnp.where(lane == 65, shift_y, weights_ref[0]))

    lane = lane_ids((BRICK_ROWS, 128))
    middle = (lane >= 64) & (lane < 67)
    for z in range(Z):
        last_ref[z] = jnp.where(middle, note((BRICK_ROWS, 128)), dose_ref[z, :, BRICK_COLS - 128 :])
        first_ref[z] = jnp.where(middle, note((BRICK_ROWS, 128)), dose_ref[z, :, :128])
    note_ref[...] = note((8, 128))


def pack_call(shifts, weights, pupil, dose):
    vmem = pl.BlockSpec(memory_space=pltpu.VMEM)
    smem = pl.BlockSpec(memory_space=pltpu.SMEM)
    side = jax.ShapeDtypeStruct((Z, BRICK_ROWS, 128), jnp.float32)
    return pl.pallas_call(
        pack_kernel,
        out_shape=(
            jax.ShapeDtypeStruct(pupil.shape, jnp.float32),
            side,
            side,
            jax.ShapeDtypeStruct((8, 128), jnp.float32),
        ),
        in_specs=[smem, smem, vmem, vmem],
        out_specs=(vmem,) * 4,
        compiler_params=pltpu.CompilerParams(vmem_limit_bytes=12 * MIB),
        cost_estimate=pl.CostEstimate(flops=1_000_000, bytes_accessed=9_000_000, transcendentals=0),
        name="pack",
    )(shifts, weights, pupil, dose)


def edge_kernel(dose_ref, before_ref, after_ref, side_ref, last_ref, first_ref):
    lane = lane_ids((BRICK_ROWS, 128))
    for z in range(Z):
        side = jnp.where(lane < 64, after_ref[z], before_ref[z])
        side_ref[z] = side
        last_ref[z, :, :BRICK_COLS] = dose_ref[z, BRICK_ROWS - 8 :, :]
        last_ref[z, :, BRICK_COLS:] = side[BRICK_ROWS - 8 :]
        first_ref[z, :, :BRICK_COLS] = dose_ref[z, :8, :]
        first_ref[z, :, BRICK_COLS:] = side[:8]


def edge_call(dose, before, after):
    vmem = pl.BlockSpec(memory_space=pltpu.VMEM)
    row = jax.ShapeDtypeStruct((Z, 8, EXT_COLS), jnp.float32)
    return pl.pallas_call(
        edge_kernel,
        out_shape=(jax.ShapeDtypeStruct((Z, BRICK_ROWS, 128), jnp.float32), row, row),
        in_specs=[vmem] * 3,
        out_specs=(vmem,) * 3,
        compiler_params=pltpu.CompilerParams(vmem_limit_bytes=6 * MIB),
        cost_estimate=pl.CostEstimate(flops=1_000_000, bytes_accessed=2_000_000, transcendentals=0),
        name="edge",
    )(dose, before, after)


def window_kernel(shifts_ref, turned_ref, dose_hbm, out_ref, dose_ref, sem):
    copy = pltpu.make_async_copy(dose_hbm, dose_ref, sem)
    copy.start()
    lane = lane_ids((8, 128))
    row = lax.broadcasted_iota(jnp.int32, (8, 128), 0)
    zero = jnp.zeros((8, 128), jnp.float32)
    tiles, group, groups = PASS // 8, 13, 4
    edge = SHIFT * 2 // 8

    def source_step(s, carry):
        lift = SHIFT - shifts_ref[s, 1]
        shift = SHIFT - shifts_ref[s, 0]
        first, rest = lift // 8, lax.rem(lift, 8)
        rise = lax.rem(8 - rest, 8)
        turn = lax.rem(256 - shift, 128)
        keep_lane = lane < 128 - shift
        keep_row = row < 8 - rest
        begin = jnp.minimum(edge - first - jnp.where(rest > 0, 1, 0), tiles - group * groups)

        def clear(t, inner):
            for plane in range(2):
                for v in range(4):
                    out_ref[2 * s + plane, pl.ds(pl.multiple_of(t * 8, 8), 8), 128 * v : 128 * v + 128] = zero
            return inner

        lax.fori_loop(0, begin, clear, 0)
        lax.fori_loop(begin + group * groups, tiles, clear, 0)

        def block(t, inner):
            start = begin + t * group
            for plane in range(2):
                before = None
                for k in range(group + 1):
                    tile = jnp.minimum(start + k + first, PUPIL_TILES - 1)
                    base = pl.ds(pl.multiple_of(tile * 8, 8), 8)
                    turned = [zero] + [
                        pltpu.roll(turned_ref[plane, base, 128 * v : 128 * v + 128], turn, 1) for v in range(1, 5)
                    ]
                    cut = [jnp.where(keep_lane, turned[v], turned[v + 1]) for v in range(4)]
                    after = [pltpu.roll(c, rise, 0) for c in cut]
                    if before is not None:
                        place = pl.ds(pl.multiple_of((start + k - 1) * 8, 8), 8)
                        for v in range(4):
                            value = jnp.where(keep_row, before[v], after[v])
                            out_ref[2 * s + plane, place, 128 * v : 128 * v + 128] = value
                    before = after
            return inner

        lax.fori_loop(0, groups, block, 0)
        return carry

    lax.fori_loop(0, SOURCES, source_step, 0)
    copy.wait()


def window_call(shifts, pupil, dose):
    vmem = pl.BlockSpec(memory_space=pltpu.VMEM)
    anywhere = pl.BlockSpec(memory_space=pl.ANY)
    return pl.pallas_call(
        window_kernel,
        out_shape=(
            jax.ShapeDtypeStruct((2 * SOURCES, PASS, PASS), jnp.float32),
            jax.ShapeDtypeStruct(dose.shape, jnp.float32),
        ),
        in_specs=[pl.BlockSpec(memory_space=pltpu.SMEM), vmem, anywhere],
        out_specs=(vmem, anywhere),
        scratch_shapes=[pltpu.SemaphoreType.DMA],
        compiler_params=pltpu.CompilerParams(vmem_limit_bytes=20 * MIB),
        cost_estimate=pl.CostEstimate(flops=10_000_000, bytes_accessed=11_000_000, transcendentals=0),
        name="window",
    )(shifts, pupil, dose)


def resist_kernel(
    where_ref, weights_ref, quencher_ref, own_ref, other_ref, window_ref, rows_hbm, cols_hbm,
    dose_ref, side_ref, above_ref, below_ref, acid_ref, inhibitor_ref,
    rows_ref, cols_ref, filt_ref, field_ref, a_ref, b_ref, p_ref, q_ref, sum_ref, sems,
):
    core = where_ref[0]
    rows_copy = pltpu.make_async_copy(rows_hbm.at[where_ref[1]], rows_ref, sems.at[0])
    cols_copy = pltpu.make_async_copy(cols_hbm.at[where_ref[2]], cols_ref, sems.at[1])
    rows_copy.start()
    cols_copy.start()

    def filter_half(s, spec_ref, half, slot):
        def block(o, inner):
            base = pl.multiple_of(o * WIDE, WIDE)
            place = pl.multiple_of(o * FREQS, FREQS)
            row = pl.multiple_of(half * (PASS // 2) + o * FREQS, FREQS)
            real = spec_ref[pl.ds(base, FREQS), :]
            imag = spec_ref[pl.ds(base + FREQS, FREQS), :]
            w_real = window_ref[2 * s, pl.ds(row, FREQS), :]
            w_imag = window_ref[2 * s + 1, pl.ds(row, FREQS), :]
            filt_ref[slot, pl.ds(place, FREQS), :PASS] = (w_real * real - w_imag * imag).astype(jnp.bfloat16)
            filt_ref[slot, pl.ds(place, FREQS), PASS:] = (w_real * imag + w_imag * real).astype(jnp.bfloat16)
            return inner

        lax.fori_loop(0, 16, block, 0, unroll=FILTER_UNROLL)

    def rowfield_half(s, half, slot):
        rowfield = lax.dot_general(
            rows_ref[...], filt_ref[slot], (((1,), (1,)), ((), ())), preferred_element_type=jnp.float32
        ).astype(jnp.bfloat16)
        top = pl.multiple_of(s * TALL, 16)
        left = pl.multiple_of(half * (PASS // 2), PASS // 2)
        field_ref[pl.ds(top, TALL), pl.ds(left, PASS // 2)] = rowfield[:TALL]
        field_ref[pl.ds(top, TALL), pl.ds(PASS + left, PASS // 2)] = rowfield[TALL:]

    def source_step(s, carry):
        filter_half(s, own_ref, core, 0)
        rowfield_half(s, core, 0)
        filter_half(s, other_ref, 1 - core, 1)
        rowfield_half(s, 1 - core, 1)
        return carry

    rows_copy.wait()
    for s in range(SOURCES):
        source_step(s, 0)
    cols_copy.wait()

    row_of = lax.broadcasted_iota(jnp.int32, (8, 128), 0)

    def tile_step(b, carry):
        field = jnp.dot(field_ref[...], cols_ref[b], preferred_element_type=jnp.float32)
        intensity = jnp.zeros((EXT_ROWS, 128), jnp.float32)
        for s in range(SOURCES):
            part = field[s * TALL : s * TALL + EXT_ROWS]
            real, imag = part[:, :128], part[:, 128:]
            intensity = intensity + weights_ref[s] * (real * real + imag * imag)
        lanes = pl.ds(pl.multiple_of(b * 128, 128), 128)
        for z in range(Z):
            bottom = jnp.where(row_of < HALO, below_ref[z, :, lanes], above_ref[z, :, lanes])
            a_ref[z, BRICK_ROWS:, lanes] = 1.0 - jnp.exp(-bottom * intensity[BRICK_ROWS:])

        @pl.when(b < COL_TILES - 1)
        def _():
            for z in range(Z):
                a_ref[z, :BRICK_ROWS, lanes] = 1.0 - jnp.exp(-dose_ref[z, :, lanes] * intensity[:BRICK_ROWS])

        @pl.when(b == COL_TILES - 1)
        def _():
            for z in range(Z):
                a_ref[z, :BRICK_ROWS, lanes] = 1.0 - jnp.exp(-side_ref[z] * intensity[:BRICK_ROWS])

        return carry

    lax.fori_loop(0, COL_TILES, tile_step, 0, unroll=FIELD_UNROLL)

    tiles = EXT_ROWS // 8
    row_id = lax.broadcasted_iota(jnp.int32, (8, EXT_COLS), 0)
    quench = [quencher_ref[0], quencher_ref[1]]

    def neighbours(ref, z, t):
        here = ref[z, pl.ds(pl.multiple_of(t * 8, 8), 8), :]
        before = ref[z, pl.ds(pl.multiple_of(jnp.where(t == 0, tiles - 1, t - 1) * 8, 8), 8), :]
        after = ref[z, pl.ds(pl.multiple_of(jnp.where(t == tiles - 1, 0, t + 1) * 8, 8), 8), :]
        above = pltpu.roll(jnp.where(row_id == 7, before, here), 1, 0)
        below = pltpu.roll(jnp.where(row_id == 0, after, here), 7, 0)
        left = pltpu.roll(here, 1, 1)
        right = pltpu.roll(here, EXT_COLS - 1, 1)
        return here, (above + below) + (left + right)

    buffers = [(a_ref, b_ref), (b_ref, a_ref), (a_ref, b_ref), (b_ref, None)]
    quenches = [(None, p_ref), (p_ref, q_ref), (q_ref, p_ref), (p_ref, None)]
    for step in range(BAKE):
        old, new = buffers[step]
        q_old, q_new = quenches[step]

        def row_step(t, carry):
            rows = pl.ds(pl.multiple_of(t * 8, 8), 8)
            acid = [neighbours(old, z, t) for z in range(Z)]
            acid_z = acid[0][0] + acid[1][0]
            if q_old is None:
                quench_here = quench
                quench_sum = [4.0 * quench[z] for z in range(Z)]
            elif q_new is None:
                quench_here = [q_old[z, rows, :] for z in range(Z)]
            else:
                pairs = [neighbours(q_old, z, t) for z in range(Z)]
                quench_here = [pair[0] for pair in pairs]
                quench_sum = [pair[1] for pair in pairs]
            quench_z = quench_here[0] + quench_here[1]
            for z in range(Z):
                here, around = acid[z]
                reaction = QUENCH_RATE * here * quench_here[z]
                lap = (around + acid_z) - 6.0 * here
                fresh = here + DIFF_ACID * lap - reaction
                if new is not None:
                    new[z, rows, :] = fresh
                else:
                    acid_ref[z, rows, :] = fresh[:, :BRICK_COLS]
                if q_new is not None:
                    q_lap = (quench_sum[z] + quench_z) - 6.0 * quench_here[z]
                    q_new[z, rows, :] = quench_here[z] + DIFF_QUENCH * q_lap - reaction
                if step == 0:
                    sum_ref[z, rows, :] = here[:, :BRICK_COLS]
                elif new is not None:
                    sum_ref[z, rows, :] = sum_ref[z, rows, :] + here[:, :BRICK_COLS]
                else:
                    total = sum_ref[z, rows, :] + here[:, :BRICK_COLS]
                    inhibitor_ref[z, rows, :] = jnp.exp(-CATALYSIS * total)
            return carry

        lax.fori_loop(0, tiles if new is not None else BRICK_ROWS // 8, row_step, 0, unroll=BAKE_UNROLL)


def resist_call(where, weights, quencher, own, other, window, rows, cols, dose, side, above, below):
    smem = pl.BlockSpec(memory_space=pltpu.SMEM)
    vmem = pl.BlockSpec(memory_space=pltpu.VMEM)
    hbm = pl.BlockSpec(memory_space=pl.ANY)
    out = jax.ShapeDtypeStruct((Z, BRICK_ROWS, BRICK_COLS), jnp.float32)
    brick = pltpu.VMEM((Z, EXT_ROWS, EXT_COLS), jnp.float32)
    return pl.pallas_call(
        resist_kernel,
        out_shape=(out, out),
        in_specs=[smem] * 3 + [vmem] * 3 + [hbm] * 2 + [vmem] * 4,
        out_specs=(vmem, vmem),
        scratch_shapes=[
            pltpu.VMEM(rows.shape[1:], jnp.bfloat16),
            pltpu.VMEM(cols.shape[1:], jnp.bfloat16),
            pltpu.VMEM((2, PASS // 2, 2 * PASS), jnp.bfloat16),
            pltpu.VMEM((SOURCES * TALL, 2 * PASS), jnp.bfloat16),
            brick, brick, brick, brick,
            pltpu.VMEM((Z, EXT_ROWS, BRICK_COLS), jnp.float32),
            pltpu.SemaphoreType.DMA((2,)),
        ],
        compiler_params=pltpu.CompilerParams(vmem_limit_bytes=28 * MIB),
        name="resist",
    )(where, weights, quencher, own, other, window, rows, cols, dose, side, above, below)


def ring(axes, step):
    size = lax.axis_size(axes)
    return [(i, (i + step) % size) for i in range(size)]


def body(mask_ids, trans_table, pupil, shifts, weights, dose, quencher):
    src_axes, tile_axes = ("zl", "c"), ("y", "zh", "x")
    core, src, tile = lax.axis_index("c"), lax.axis_index(src_axes), lax.axis_index(tile_axes)
    packed = columns_call(trans_table, mask_ids, jnp.asarray(forward_columns()), jnp.asarray(edge_columns()))
    packed, shifts, weights, dose_late, pupil = lax.optimization_barrier((packed, shifts, weights, dose, pupil))
    cols = lax.all_to_all(packed, ALL, 0, 0, tiled=True)

    turned, last, first, note = pack_call(shifts, weights, pupil, dose_late)
    before = lax.ppermute(last, src_axes, ring(src_axes, 1))
    after = lax.ppermute(first, src_axes, ring(src_axes, -1))
    far = lax.ppermute(note, src_axes, ring(src_axes, 2))
    notes = [note[:1, 64:67], far[:1, 64:67], before[0, :1, 64:67], after[0, :1, 64:67]]
    sources = jnp.concatenate(notes, axis=0)
    all_shifts, all_weights = sources[:, :2].astype(jnp.int32), sources[:, 2]
    side, last, first = edge_call(dose_late, before, after)
    above = lax.ppermute(last, tile_axes, ring(tile_axes, 1))
    below = lax.ppermute(first, tile_axes, ring(tile_axes, -1))
    where = jnp.stack([core, tile, src]).astype(jnp.int32)

    block = spectrum_call(jnp.asarray(forward_rows()), cols, jnp.asarray(edge_rows()))
    own = lax.all_to_all(block, ("y", "x"), 0, 0, tiled=True)
    own, turned, all_shifts, all_weights, side, above, below, where = lax.optimization_barrier(
        (own, turned, all_shifts, all_weights, side, above, below, where)
    )
    other = lax.ppermute(own, "c", [(0, 1), (1, 0)])
    window, dose_near = window_call(all_shifts, turned, dose)
    return resist_call(
        where, all_weights, quencher, own, other, window,
        jnp.asarray(inverse_rows(32)), jnp.asarray(inverse_cols(4)), dose_near, side, above, below,
    )


def solution(mesh):
    parts = Mesh(mesh.devices.reshape(2, 2, 4, 2, 4), ALL)
    src, tile = ("zl", "c"), ("y", "zh", "x")
    inner = jax.shard_map(
        body,
        mesh=parts,
        in_specs=(
            P(ALL, None),
            P(),
            P(),
            P(src, None),
            P(src),
            P(None, tile, src),
            P(),
        ),
        out_specs=(P(None, tile, src), P(None, tile, src)),
        check_vma=False,
    )
    return inner
```

time: 127 us -> 80.2 us (0.63)
  local copies, waits for them, and re-layouts: 42.8 us -> 6.7 us
  between operations: 11.2 us -> 1.55 us
  waiting for transfers between devices: 6.58 us -> 14.6 us
  other arithmetic: 8.08 us -> 0.1 us
    unnamed x16 -> x14, local copies, waits for them, and re-layouts: 22.4 us -> 6.23 us
    ppermute x7 -> x5, waiting for transfers between devices: 1.35 us -> 12.4 us  [the longest x1 12.4 us: body(): above = lax.ppermute(last, tile_axes, ring(tile_axes, 1))]
    another operation x1 -> x0, local copies, waits for them, and re-layouts: 9.52 us -> none
    concatenate x3 -> x1, other arithmetic: 7.32 us -> 0.01 us  [body(): sources = jnp.concatenate(notes, axis=0)]
    squeeze x3 -> x2, local copies, waits for them, and re-layouts: 5.99 us -> 0.14 us  [the longest x1 0.07 us: body(): after[0, :1, 64:67]]
    pallas_call x1 -> x4, Pallas kernels: 22.3 us -> 18.8 us  [the longest x1 13.3 us: resist_call(): pl.pallas_call(resist_kernel, out_shape=(out, out), in_specs=[smem] * 3 +...]
    all_to_all x1, waiting for transfers between devices: 5.22 us -> 2.25 us  [body(): cols = lax.all_to_all(packed, ALL, 0, 0, tiled=True)]
    slice x3, local copies, waits for them, and re-layouts: 2.67 us -> 0.33 us  [the longest x1 0.18 us: body(): all_shifts, all_weights = (sources[:, :2].astype(jnp.int32), sources[:, 2])]
  transfers between devices with their start and end apart: 10 -> 8, of which waited for: 2 -> 2; matrix products, arithmetic and copies ran while one was open for 31% -> 1% of each run, Pallas kernels for 7% -> 14%
where the time goes in v2:
time: 80.2 us; the launch traced here: 79.8 us
  Pallas kernels  29.4 us (37%)
  starting transfers between devices  27.3 us (34%)
  waiting for transfers between devices  14.6 us (18%)
  local copies, waits for them, and re-layouts  6.7 us (8%)
  between operations  1.55 us (2%)
    pallas_call x1, Pallas kernels, resist_call(): pl.pallas_call(resist_kernel, out_shape=(out, out), in_specs=[smem] * 3 +...  13.3 us
    ppermute x1, waiting for transfers between devices, body(): above = lax.ppermute(last, tile_axes, ring(tile_axes, 1))  12.4 us
    all_to_all x1, starting transfers between devices, body(): cols = lax.all_to_all(packed, ALL, 0, 0, tiled=True)  11.5 us
    unnamed x14, local copies, waits for them, and re-layouts  6.23 us
    ppermute x1, starting transfers between devices, body(): below = lax.ppermute(first, tile_axes, ring(tile_axes, -1))  6.08 us
    pallas_call x1, Pallas kernels, spectrum_call(): pl.pallas_call(spectrum_kernel, grid=(4,), out_shape=jax.ShapeDtypeStruct...  5.53 us
    pallas_call x1, Pallas kernels, columns_call(): pl.pallas_call(columns_kernel, grid=(steps,), out_shape=jax.ShapeDtypeStr...  5.08 us
    all_to_all x1, starting transfers between devices, body(): own = lax.all_to_all(block, ('y', 'x'), 0, 0, tiled=True)  4.51 us
  transfers between devices with their start and end apart: 8, of which 2 were waited for; matrix products, arithmetic and copies ran while one was open for 1% of the time, Pallas kernels for 14%

profile of v2, /device:TPU:1, one launch (start us, length us, event | category | flops | bytes accessed | tf_op | source)
XLA Modules:
  0.0 79.8 jit_solution(17612635685672628544)
XLA Ops:
  0.6 0.0 copy-start.4
  0.6 0.0 copy-start
  0.7 5.1 %columns.1 = bf16[1024,128]{1,0:T(8,128)(2,1)} custom-call(f32[2,4]{1,0:T(2,128)} %trans_ref.1, s32[32,4096]{1,0:T(8,128)} %ids_ref.1, bf16[4096,512]{1,0:T(8,128)(2,1)} %constant.38.clone.table_ref, f32[2,128]{1,0:T(2,128)} %constant.39.clone.edge_ref), custom_call_target="tpu_custom_call" | custom-call | tf_op jit(solution)/shard_map/columns/pallas_call | solution.py:175
  5.7 11.5 %all-to-all-start = ((bf16[128,8,128]{2,1,0:T(8,128)(2,1)}), bf16[128,8,128]{2,1,0:T(8,128)(2,1)S(1)}, u32[]{:S(2)}, u32[]{:S(2)}) async-start(bf16[128,8,128]{2,1,0:T(8,128)(2,1)} %bitcast.14), calls=%async_computation | async-start | bytes 524288 | tf_op jit(solution)/shard_map/all_to_all | solution.py:573
  17.9 0.0 copy-done.4
  17.9 0.0 copy-done
  17.9 0.0 copy-start.1
  17.9 1.9 %copy-done.1 = f32[2,640,640]{2,1,0:T(8,128)S(1)} copy-done((f32[2,640,640]{2,1,0:T(8,128)S(1)}, f32[2,640,640]{2,1,0:T(8,128)}, u32[]{:S(2)}) %copy-start.1) | copy-done | bytes 3276824
  19.8 1.4 %pack.1 = (f32[2,640,640]{2,1,0:T(8,128)S(1)}, f32[2,128,128]{2,1,0:T(8,128)S(1)}, f32[2,128,128]{2,1,0:T(8,128)S(1)}, f32[8,128]{1,0:T(8,128)S(1)}) custom-call(s32[1,2]{1,0:T(1,128)S(1)} %copy-done.4, f32[1]{0:T(128)S(6)} %copy.15.weights_ref, f32[2,640,640]{2,1,0:T(8,128)S(1)} %copy-done.1, f32[2,128,1024]{2,1,0:T(8,128)S(1)} %copy-done), custom_call_target="tpu_custom_call" | custom-call | flops 1000000 | bytes 9000000 | tf_op jit(solution)/shard_map/pack/pallas_call | solution.py:291
  21.3 0.0 copy-start.2
  21.3 1.7 %copy-done.2 = f32[2,640,640]{2,1,0:T(8,128)} copy-done((f32[2,640,640]{2,1,0:T(8,128)}, f32[2,640,640]{2,1,0:T(8,128)S(1)}, u32[]{:S(2)}) %copy-start.2) | copy-done | bytes 3276824
  22.9 1.1 %collective-permute-start.2 = (f32[2,128,128]{2,1,0:T(8,128)S(1)}, f32[2,128,128]{2,1,0:T(8,128)S(1)}, u32[]{:S(2)}, u32[]{:S(2)}) collective-permute-start(f32[2,128,128]{2,1,0:T(8,128)S(1)} %get-tuple-element.32), channel_id=1, source_target_pairs={{0,96},{32,0},{64,32},{96,64},{1,97},{33,1},{65,33},{97,65},{2,98}... | collective-permute-start | bytes 393224 | tf_op jit(solution)/shard_map/ppermute | solution.py:577
  24.0 0.7 collective-permute-start.1
  24.7 1.5 %collective-permute-start = (f32[8,128]{1,0:T(8,128)S(1)}, f32[8,128]{1,0:T(8,128)S(1)}, u32[]{:S(2)}, u32[]{:S(2)}) collective-permute-start(f32[8,128]{1,0:T(8,128)S(1)} %get-tuple-element.30), channel_id=1, source_target_pairs={{0,64},{32,96},{64,0},{96,32},{1,65},{33,97},{65,1},{97,33},{2,66}... | collective-permute-start | bytes 12296 | tf_op jit(solution)/shard_map/ppermute | solution.py:578
  26.2 2.3 %all-to-all-done = bf16[128,8,128]{2,1,0:T(8,128)(2,1)S(1)} async-done(((bf16[128,8,128]{2,1,0:T(8,128)(2,1)}), bf16[128,8,128]{2,1,0:T(8,128)(2,1)S(1)}, u32[]{:S(2)}, u32[]{:S(2)}) %all-to-all-start) | async-done | bytes 262176 | tf_op jit(solution)/shard_map/all_to_all | solution.py:573
  28.5 0.0 copy-start.6
  28.5 0.7 copy-done.6
  29.2 5.5 %spectrum.1 = f32[512,512]{1,0:T(8,128)} custom-call(bf16[4,512,1024]{2,1,0:T(8,128)(2,1)} %constant.40.clone.table_ref, bf16[1024,128]{1,0:T(8,128)(2,1)} %bitcast.15, f32[2,8,128]{2,1,0:T(8,128)} %constant.41.clone.edge_ref), custom_call_target="tpu_custom_call" | custom-call | tf_op jit(solution)/shard_map/spectrum/pallas_call | solution.py:250
  34.7 0.0 copy-start.5
  34.7 4.5 %all-to-all-start.1 = ((f32[16,32,512]{2,1,0:T(8,128)}), f32[16,32,512]{2,1,0:T(8,128)S(1)}, u32[]{:S(2)}, u32[]{:S(2)}) async-start(f32[16,32,512]{2,1,0:T(8,128)} %bitcast.13), calls=%async_computation.1 | async-start | bytes 2097152 | tf_op jit(solution)/shard_map/all_to_all | solution.py:588
  39.2 0.1 pad_add_fusion.where_ref
  39.3 0.1 slice.18
  39.4 0.0 collective-permute-done
  39.4 0.1 slice.19
  39.4 0.0 collective-permute-done.2.after_ref
  39.4 0.0 collective-permute-done.1.before_ref
  39.5 1.4 %collective-permute-start.3 = (f32[2,8,1152]{2,1,0:T(8,128)S(1)}, f32[2,8,1152]{2,1,0:T(8,128)S(1)}, u32[]{:S(2)}, u32[]{:S(2)}) collective-permute-start(f32[2,8,1152]{2,1,0:T(8,128)S(1)} %get-tuple-element.34), channel_id=1, source_target_pairs={{0,1},{1,2},{2,3},{3,4},{4,5},{5,6},{6,7},{7,8},{8,9},{9,10},{10,1... | collective-permute-start | bytes 221192 | tf_op jit(solution)/shard_map/ppermute | solution.py:583
  40.9 6.1 %collective-permute-start.4 = (f32[2,8,1152]{2,1,0:T(8,128)S(1)}, f32[2,8,1152]{2,1,0:T(8,128)S(1)}, u32[]{:S(2)}, u32[]{:S(2)}) collective-permute-start(f32[2,8,1152]{2,1,0:T(8,128)S(1)} %get-tuple-element.35), channel_id=1, source_target_pairs={{0,31},{1,0},{2,1},{3,2},{4,3},{5,4},{6,5},{7,6},{8,7},{9,8},{10,9... | collective-permute-start | bytes 221192 | tf_op jit(solution)/shard_map/ppermute | solution.py:584
  47.0 0.1 slice_bitcast_fusion
  47.1 0.1 slice_bitcast_fusion.1
  47.2 0.2 slice_reduce_fusion.weights_ref
  47.3 12.4 %collective-permute-done.3.above_ref = f32[2,8,1152]{2,1,0:T(8,128)S(1)} collective-permute-done((f32[2,8,1152]{2,1,0:T(8,128)S(1)}, f32[2,8,1152]{2,1,0:T(8,128)S(1)}, u32[]{:S(2)}, u32[]{:S(2)}) %collective-permute-start.3) | collective-permute-done | bytes 73760 | tf_op jit(solution)/shard_map/ppermute | solution.py:583
  59.7 0.0 collective-permute-done.4.below_ref
  59.7 0.0 all-to-all-done.1
  59.7 0.5 collective-permute-start.5
  60.3 0.0 copy-start.3
  60.3 1.9 %copy-done.3 = f32[2,640,640]{2,1,0:T(8,128)S(1)} copy-done((f32[2,640,640]{2,1,0:T(8,128)S(1)}, f32[2,640,640]{2,1,0:T(8,128)}, u32[]{:S(2)}) %copy-start.3) | copy-done | bytes 3276824
  62.2 4.0 %window.1 = (f32[8,512,512]{2,1,0:T(8,128)S(1)}, f32[2,128,1024]{2,1,0:T(8,128)S(1)}) custom-call(s32[4,2]{1,0:T(4,128)S(1)} %slice_convert_fusion.shifts_ref, f32[2,640,640]{2,1,0:T(8,128)S(1)} %copy-done.3, f32[2,128,1024]{2,1,0:T(8,128)S(1)} %copy-done), custom_call_target="tpu_custom_call" | custom-call | flops 10000000 | bytes 11000000 | tf_op jit(solution)/shard_map/window/pallas_call | solution.py:390
  66.2 0.0 collective-permute-done.5.other_ref
  66.2 0.0 copy-done.5
  66.3 13.3 %resist.1 = (f32[2,128,1024]{2,1,0:T(8,128)}, f32[2,128,1024]{2,1,0:T(8,128)}) custom-call(s32[3]{0:T(128)S(1)} %pad_add_fusion.where_ref, f32[4]{0:T(128)S(1)} %slice_reduce_fusion.weights_ref, f32[2]{0:T(128)S(1)} %copy-done.5, f32[512,512]{1,0:T(8,128)S(1)} %bitcast.12, f32[512,512]{1,0:T(8,128)S(1)} %collective-permute-done.5.other_ref, ...), custom_call_target="tpu_custom_call" | custom-call | tf_op jit(solution)/shard_map/resist/pallas_call | solution.py:544
  (3 shorter events, 0.0 us)
Async XLA Ops:
  0.6 17.2 %copy-start.4 = (s32[1,2]{1,0:T(1,128)S(1)}, s32[1,2]{1,0:T(1,128)}, u32[]{:S(2)}) copy-start(s32[1,2]{1,0:T(1,128)} %shifts_ref) | copy-start | bytes 28
  0.6 17.2 %copy-start = (f32[2,128,1024]{2,1,0:T(8,128)S(1)}, f32[2,128,1024]{2,1,0:T(8,128)}, u32[]{:S(2)}) copy-start(f32[2,128,1024]{2,1,0:T(8,128)} %dose_hbm.1) | copy-start | bytes 3145732
  5.7 22.7 %all-to-all-start = ((bf16[128,8,128]{2,1,0:T(8,128)(2,1)}), bf16[128,8,128]{2,1,0:T(8,128)(2,1)S(1)}, u32[]{:S(2)}, u32[]{:S(2)}) async-start(bf16[128,8,128]{2,1,0:T(8,128)(2,1)} %bitcast.14), calls=%async_computation | async-start | bytes 524288 | tf_op jit(solution)/shard_map/all_to_all | solution.py:573
  17.9 1.9 %copy-start.1 = (f32[2,640,640]{2,1,0:T(8,128)S(1)}, f32[2,640,640]{2,1,0:T(8,128)}, u32[]{:S(2)}) copy-start(f32[2,640,640]{2,1,0:T(8,128)} %pupil_ref) | copy-start | bytes 9830404
  21.3 1.7 %copy-start.2 = (f32[2,640,640]{2,1,0:T(8,128)}, f32[2,640,640]{2,1,0:T(8,128)S(1)}, u32[]{:S(2)}) copy-start(f32[2,640,640]{2,1,0:T(8,128)S(1)} %get-tuple-element.40.turned_ref) | copy-start | bytes 9830404
  22.9 16.5 %collective-permute-start.2 = (f32[2,128,128]{2,1,0:T(8,128)S(1)}, f32[2,128,128]{2,1,0:T(8,128)S(1)}, u32[]{:S(2)}, u32[]{:S(2)}) collective-permute-start(f32[2,128,128]{2,1,0:T(8,128)S(1)} %get-tuple-element.32), channel_id=1, source_target_pairs={{0,96},{32,0},{64,32},{96,64},{1,97},{33,1},{65,33},{97,65},{2,98}... | collective-permute-start | bytes 393224 | tf_op jit(solution)/shard_map/ppermute | solution.py:577
  24.0 15.4 %collective-permute-start.1 = (f32[2,128,128]{2,1,0:T(8,128)S(1)}, f32[2,128,128]{2,1,0:T(8,128)S(1)}, u32[]{:S(2)}, u32[]{:S(2)}) collective-permute-start(f32[2,128,128]{2,1,0:T(8,128)S(1)} %get-tuple-element.31), channel_id=1, source_target_pairs={{0,32},{32,64},{64,96},{96,0},{1,33},{33,65},{65,97},{97,1},{2,34}... | collective-permute-start | bytes 393224 | tf_op jit(solution)/shard_map/ppermute | solution.py:576
  24.7 14.7 %collective-permute-start = (f32[8,128]{1,0:T(8,128)S(1)}, f32[8,128]{1,0:T(8,128)S(1)}, u32[]{:S(2)}, u32[]{:S(2)}) collective-permute-start(f32[8,128]{1,0:T(8,128)S(1)} %get-tuple-element.30), channel_id=1, source_target_pairs={{0,64},{32,96},{64,0},{96,32},{1,65},{33,97},{65,1},{97,33},{2,66}... | collective-permute-start | bytes 12296 | tf_op jit(solution)/shard_map/ppermute | solution.py:578
  28.5 0.7 copy-start.6
  34.7 31.5 %copy-start.5 = (f32[2]{0:T(128)S(1)}, f32[2]{0:T(128)}, u32[]{:S(2)}) copy-start(f32[2]{0:T(128)} %quencher_ref.1) | copy-start | bytes 28
  34.7 25.0 %all-to-all-start.1 = ((f32[16,32,512]{2,1,0:T(8,128)}), f32[16,32,512]{2,1,0:T(8,128)S(1)}, u32[]{:S(2)}, u32[]{:S(2)}) async-start(f32[16,32,512]{2,1,0:T(8,128)} %bitcast.13), calls=%async_computation.1 | async-start | bytes 2097152 | tf_op jit(solution)/shard_map/all_to_all | solution.py:588
  39.5 20.2 %collective-permute-start.3 = (f32[2,8,1152]{2,1,0:T(8,128)S(1)}, f32[2,8,1152]{2,1,0:T(8,128)S(1)}, u32[]{:S(2)}, u32[]{:S(2)}) collective-permute-start(f32[2,8,1152]{2,1,0:T(8,128)S(1)} %get-tuple-element.34), channel_id=1, source_target_pairs={{0,1},{1,2},{2,3},{3,4},{4,5},{5,6},{6,7},{7,8},{8,9},{9,10},{10,1... | collective-permute-start | bytes 221192 | tf_op jit(solution)/shard_map/ppermute | solution.py:583
  40.9 18.8 %collective-permute-start.4 = (f32[2,8,1152]{2,1,0:T(8,128)S(1)}, f32[2,8,1152]{2,1,0:T(8,128)S(1)}, u32[]{:S(2)}, u32[]{:S(2)}) collective-permute-start(f32[2,8,1152]{2,1,0:T(8,128)S(1)} %get-tuple-element.35), channel_id=1, source_target_pairs={{0,31},{1,0},{2,1},{3,2},{4,3},{5,4},{6,5},{7,6},{8,7},{9,8},{10,9... | collective-permute-start | bytes 221192 | tf_op jit(solution)/shard_map/ppermute | solution.py:584
  59.7 6.5 %collective-permute-start.5 = (f32[512,512]{1,0:T(8,128)S(1)}, f32[512,512]{1,0:T(8,128)S(1)}, u32[]{:S(2)}, u32[]{:S(2)}) collective-permute-start(f32[512,512]{1,0:T(8,128)S(1)} %bitcast.11), channel_id=1, source_target_pairs={{0,32},{32,0},{1,33},{33,1},{2,34},{34,2},{3,35},{35,3},{4,36},{36... | collective-permute-start | bytes 3145736 | tf_op jit(solution)/shard_map/ppermute | solution.py:592
  60.3 1.9 %copy-start.3 = (f32[2,640,640]{2,1,0:T(8,128)S(1)}, f32[2,640,640]{2,1,0:T(8,128)}, u32[]{:S(2)}) copy-start(f32[2,640,640]{2,1,0:T(8,128)} %copy-done.2) | copy-start | bytes 9830404

commit v3 on v2

--- a/solution.py
+++ b/solution.py
@@ -33,11 +33,9 @@
 EXT_ROWS = BRICK_ROWS + 2 * HALO
 EXT_COLS = BRICK_COLS + 128
 COL_TILES = EXT_COLS // 128
+EARLY = 2
 ALL = ("zl", "c", "y", "zh", "x")
 MIB = 1024 * 1024
-FILTER_UNROLL = 16
-FIELD_UNROLL = 9
-BAKE_UNROLL = 17
 
 
 def cos_sin(first, second):
@@ -258,7 +256,7 @@
         ],
         out_specs=pl.BlockSpec((16 * WIDE, PASS), lambda q: (0, 0)),
         scratch_shapes=[pltpu.VMEM((PASS, 128), jnp.float32)],
-        compiler_params=pltpu.CompilerParams(vmem_limit_bytes=56 * MIB),
+        compiler_params=pltpu.CompilerParams(vmem_limit_bytes=16 * MIB),
         name="spectrum",
     )(table, cols, edge)
 
@@ -329,9 +327,8 @@
     )(dose, before, after)
 
 
-def window_kernel(shifts_ref, turned_ref, dose_hbm, out_ref, dose_ref, sem):
-    copy = pltpu.make_async_copy(dose_hbm, dose_ref, sem)
-    copy.start()
+def window_kernel(shifts_ref, turned_ref, out_hbm, token_ref, out_ref, sems):
+    token_ref[...] = jnp.zeros_like(token_ref)
     lane = lane_ids((8, 128))
     row = lax.broadcasted_iota(jnp.int32, (8, 128), 0)
     zero = jnp.zeros((8, 128), jnp.float32)
@@ -378,127 +375,173 @@
             return inner
 
         lax.fori_loop(0, groups, block, 0)
+        leave(s).start()
         return carry
 
+    def leave(s):
+        planes = pl.ds(2 * s, 2)
+        return pltpu.make_async_copy(out_ref.at[planes], out_hbm.at[planes], sems.at[s])
+
     lax.fori_loop(0, SOURCES, source_step, 0)
-    copy.wait()
-
-
-def window_call(shifts, pupil, dose):
+    for s in range(SOURCES):
+        leave(s).wait()
+
+
+def window_call(shifts, pupil):
     vmem = pl.BlockSpec(memory_space=pltpu.VMEM)
-    anywhere = pl.BlockSpec(memory_space=pl.ANY)
+    planes = 2 * SOURCES
     return pl.pallas_call(
         window_kernel,
         out_shape=(
-            jax.ShapeDtypeStruct((2 * SOURCES, PASS, PASS), jnp.float32),
+            jax.ShapeDtypeStruct((3 * planes, PASS, PASS), jnp.float32),
+            jax.ShapeDtypeStruct((8, 128), jnp.float32),
+        ),
+        in_specs=[pl.BlockSpec(memory_space=pltpu.SMEM), vmem],
+        out_specs=(pl.BlockSpec(memory_space=pl.ANY), vmem),
+        scratch_shapes=[pltpu.VMEM((planes, PASS, PASS), jnp.float32), pltpu.SemaphoreType.DMA((SOURCES,))],
+        compiler_params=pltpu.CompilerParams(vmem_limit_bytes=44 * MIB),
+        cost_estimate=pl.CostEstimate(flops=10_000_000, bytes_accessed=11_000_000, transcendentals=0),
+        name="window",
+    )(shifts, pupil)
+
+
+def rowfield_half(s, spec_ref, window_ref, rows_ref, filt_ref):
+    slot = s % 2
+
+    def block(o, inner):
+        base = pl.multiple_of(o * WIDE, WIDE)
+        place = pl.ds(pl.multiple_of(o * FREQS, FREQS), FREQS)
+        real = spec_ref[pl.ds(base, FREQS), :]
+        imag = spec_ref[pl.ds(base + FREQS, FREQS), :]
+        w_real = window_ref[2 * s, place, :]
+        w_imag = window_ref[2 * s + 1, place, :]
+        filt_ref[slot, place, :PASS] = (w_real * real - w_imag * imag).astype(jnp.bfloat16)
+        filt_ref[slot, place, PASS:] = (w_real * imag + w_imag * real).astype(jnp.bfloat16)
+        return inner
+
+    lax.fori_loop(0, 16, block, 0, unroll=16)
+    return lax.dot_general(
+        rows_ref[...], filt_ref[slot], (((1,), (1,)), ((), ())), preferred_element_type=jnp.float32
+    ).astype(jnp.bfloat16)
+
+
+def own_kernel(
+    where_ref, token_ref, own_ref, window_hbm, rows_hbm, dose_hbm,
+    field_ref, rows_ref, other_ref, dose_ref, window_ref, filt_ref, sems,
+):
+    core = where_ref[0]
+    mine = pl.ds(pl.multiple_of(core * HALF, HALF), HALF)
+    theirs = pl.ds(pl.multiple_of((1 - core) * HALF, HALF), HALF)
+    rows_copy = pltpu.make_async_copy(rows_hbm.at[where_ref[1]], rows_ref, sems.at[0])
+    rows_copy.start()
+    copies = []
+    for s in range(SOURCES):
+        planes = pl.ds(2 * s, 2)
+        copies.append(pltpu.make_async_copy(window_hbm.at[planes, mine], window_ref.at[planes], sems.at[1 + s]))
+        copies[s].start()
+    later = [
+        pltpu.make_async_copy(dose_hbm, dose_ref, sems.at[1 + SOURCES]),
+        pltpu.make_async_copy(window_hbm.at[pl.ds(0, 2 * SOURCES), theirs], other_ref, sems.at[2 + SOURCES]),
+    ]
+    for copy in later:
+        copy.start()
+    rows_copy.wait()
+    for s in range(SOURCES):
+        if s % 2 == 0:
+            copies[s].wait()
+            copies[s + 1].wait()
+        rowfield = rowfield_half(s, own_ref, window_ref, rows_ref, filt_ref)
+        field_ref[s * TALL : (s + 1) * TALL, :HALF] = rowfield[:TALL]
+        field_ref[s * TALL : (s + 1) * TALL, HALF:] = rowfield[TALL:]
+    for copy in later:
+        copy.wait()
+
+
+def own_call(where, token, own, window, rows, dose):
+    smem = pl.BlockSpec(memory_space=pltpu.SMEM)
+    vmem = pl.BlockSpec(memory_space=pltpu.VMEM)
+    hbm = pl.BlockSpec(memory_space=pl.ANY)
+    half = (2 * SOURCES, HALF, PASS)
+    return pl.pallas_call(
+        own_kernel,
+        out_shape=(
+            jax.ShapeDtypeStruct((SOURCES * TALL, PASS), jnp.bfloat16),
+            jax.ShapeDtypeStruct(rows.shape[1:], jnp.bfloat16),
+            jax.ShapeDtypeStruct(half, jnp.float32),
             jax.ShapeDtypeStruct(dose.shape, jnp.float32),
         ),
-        in_specs=[pl.BlockSpec(memory_space=pltpu.SMEM), vmem, anywhere],
-        out_specs=(vmem, anywhere),
-        scratch_shapes=[pltpu.SemaphoreType.DMA],
-        compiler_params=pltpu.CompilerParams(vmem_limit_bytes=20 * MIB),
-        cost_estimate=pl.CostEstimate(flops=10_000_000, bytes_accessed=11_000_000, transcendentals=0),
-        name="window",
-    )(shifts, pupil, dose)
+        in_specs=[smem, hbm, vmem, hbm, hbm, hbm],
+        out_specs=(vmem,) * 4,
+        scratch_shapes=[
+            pltpu.VMEM(half, jnp.float32),
+            pltpu.VMEM((2, HALF, 2 * PASS), jnp.bfloat16),
+            pltpu.SemaphoreType.DMA((3 + SOURCES,)),
+        ],
+        compiler_params=pltpu.CompilerParams(vmem_limit_bytes=36 * MIB),
+        cost_estimate=pl.CostEstimate(flops=10_000_000, bytes_accessed=9_000_000, transcendentals=0),
+        name="own_half",
+    )(where, token, own, window, rows, dose)
 
 
 def resist_kernel(
-    where_ref, weights_ref, quencher_ref, own_ref, other_ref, window_ref, rows_hbm, cols_hbm,
-    dose_ref, side_ref, above_ref, below_ref, acid_ref, inhibitor_ref,
-    rows_ref, cols_ref, filt_ref, field_ref, a_ref, b_ref, p_ref, q_ref, sum_ref, sems,
+    where_ref, weights_ref, quencher_ref, half_ref, other_ref, window_ref, rows_ref, cols_hbm,
+    dose_ref, side_ref, above_ref, below_ref, acid_hbm, inhibitor_hbm,
+    cols_ref, filt_ref, field_ref, a_ref, b_ref, p_ref, q_ref, sum_ref, acid_ref, inhibitor_ref, sems, out_sems,
 ):
     core = where_ref[0]
-    rows_copy = pltpu.make_async_copy(rows_hbm.at[where_ref[1]], rows_ref, sems.at[0])
-    cols_copy = pltpu.make_async_copy(cols_hbm.at[where_ref[2]], cols_ref, sems.at[1])
-    rows_copy.start()
-    cols_copy.start()
-
-    def filter_half(s, spec_ref, half, slot):
-        def block(o, inner):
-            base = pl.multiple_of(o * WIDE, WIDE)
-            place = pl.multiple_of(o * FREQS, FREQS)
-            row = pl.multiple_of(half * (PASS // 2) + o * FREQS, FREQS)
-            real = spec_ref[pl.ds(base, FREQS), :]
-            imag = spec_ref[pl.ds(base + FREQS, FREQS), :]
-            w_real = window_ref[2 * s, pl.ds(row, FREQS), :]
-            w_imag = window_ref[2 * s + 1, pl.ds(row, FREQS), :]
-            filt_ref[slot, pl.ds(place, FREQS), :PASS] = (w_real * real - w_imag * imag).astype(jnp.bfloat16)
-            filt_ref[slot, pl.ds(place, FREQS), PASS:] = (w_real * imag + w_imag * real).astype(jnp.bfloat16)
-            return inner
-
-        lax.fori_loop(0, 16, block, 0, unroll=FILTER_UNROLL)
-
-    def rowfield_half(s, half, slot):
-        rowfield = lax.dot_general(
-            rows_ref[...], filt_ref[slot], (((1,), (1,)), ((), ())), preferred_element_type=jnp.float32
-        ).astype(jnp.bfloat16)
-        top = pl.multiple_of(s * TALL, 16)
-        left = pl.multiple_of(half * (PASS // 2), PASS // 2)
-        field_ref[pl.ds(top, TALL), pl.ds(left, PASS // 2)] = rowfield[:TALL]
-        field_ref[pl.ds(top, TALL), pl.ds(PASS + left, PASS // 2)] = rowfield[TALL:]
-
-    def source_step(s, carry):
-        filter_half(s, own_ref, core, 0)
-        rowfield_half(s, core, 0)
-        filter_half(s, other_ref, 1 - core, 1)
-        rowfield_half(s, 1 - core, 1)
-        return carry
-
-    rows_copy.wait()
+    cols_copies = []
+    for k, (begin, count) in enumerate(((0, EARLY), (EARLY, COL_TILES - EARLY))):
+        part = pl.ds(begin, count)
+        cols_copies.append(pltpu.make_async_copy(cols_hbm.at[where_ref[2], part], cols_ref.at[part], sems.at[k]))
+        cols_copies[k].start()
+    mine = pl.multiple_of(core * HALF, HALF)
+    theirs = pl.multiple_of((1 - core) * HALF, HALF)
+    field_ref[:, pl.ds(mine, HALF)] = half_ref[:, :HALF]
+    field_ref[:, pl.ds(PASS + mine, HALF)] = half_ref[:, HALF:]
     for s in range(SOURCES):
-        source_step(s, 0)
-    cols_copy.wait()
-
+        rowfield = rowfield_half(s, other_ref, window_ref, rows_ref, filt_ref)
+        field_ref[s * TALL : (s + 1) * TALL, pl.ds(theirs, HALF)] = rowfield[:TALL]
+        field_ref[s * TALL : (s + 1) * TALL, pl.ds(PASS + theirs, HALF)] = rowfield[TALL:]
+    cols_copies[0].wait()
     row_of = lax.broadcasted_iota(jnp.int32, (8, 128), 0)
 
-    def tile_step(b, carry):
+    for b in range(COL_TILES):
+        if b == EARLY:
+            cols_copies[1].wait()
         field = jnp.dot(field_ref[...], cols_ref[b], preferred_element_type=jnp.float32)
         intensity = jnp.zeros((EXT_ROWS, 128), jnp.float32)
         for s in range(SOURCES):
             part = field[s * TALL : s * TALL + EXT_ROWS]
             real, imag = part[:, :128], part[:, 128:]
             intensity = intensity + weights_ref[s] * (real * real + imag * imag)
-        lanes = pl.ds(pl.multiple_of(b * 128, 128), 128)
+        lanes = slice(b * 128, b * 128 + 128)
         for z in range(Z):
             bottom = jnp.where(row_of < HALO, below_ref[z, :, lanes], above_ref[z, :, lanes])
-            a_ref[z, BRICK_ROWS:, lanes] = 1.0 - jnp.exp(-bottom * intensity[BRICK_ROWS:])
-
-        @pl.when(b < COL_TILES - 1)
-        def _():
-            for z in range(Z):
-                a_ref[z, :BRICK_ROWS, lanes] = 1.0 - jnp.exp(-dose_ref[z, :, lanes] * intensity[:BRICK_ROWS])
-
-        @pl.when(b == COL_TILES - 1)
-        def _():
-            for z in range(Z):
-                a_ref[z, :BRICK_ROWS, lanes] = 1.0 - jnp.exp(-side_ref[z] * intensity[:BRICK_ROWS])
-
-        return carry
-
-    lax.fori_loop(0, COL_TILES, tile_step, 0, unroll=FIELD_UNROLL)
+            middle = dose_ref[z, :, lanes] if b < COL_TILES - 1 else side_ref[z]
+            a_ref[z, :BRICK_ROWS, lanes] = QUENCH_RATE - QUENCH_RATE * jnp.exp(-middle * intensity[:BRICK_ROWS])
+            a_ref[z, BRICK_ROWS:, lanes] = QUENCH_RATE - QUENCH_RATE * jnp.exp(-bottom * intensity[BRICK_ROWS:])
 
     tiles = EXT_ROWS // 8
     row_id = lax.broadcasted_iota(jnp.int32, (8, EXT_COLS), 0)
-    quench = [quencher_ref[0], quencher_ref[1]]
+    quench = [QUENCH_RATE * quencher_ref[0], QUENCH_RATE * quencher_ref[1]]
 
     def neighbours(ref, z, t):
-        here = ref[z, pl.ds(pl.multiple_of(t * 8, 8), 8), :]
-        before = ref[z, pl.ds(pl.multiple_of(jnp.where(t == 0, tiles - 1, t - 1) * 8, 8), 8), :]
-        after = ref[z, pl.ds(pl.multiple_of(jnp.where(t == tiles - 1, 0, t + 1) * 8, 8), 8), :]
-        above = pltpu.roll(jnp.where(row_id == 7, before, here), 1, 0)
-        below = pltpu.roll(jnp.where(row_id == 0, after, here), 7, 0)
+        here = ref[z, 8 * t : 8 * t + 8, :]
+        up, down = (t - 1) % tiles, (t + 1) % tiles
+        above = pltpu.roll(jnp.where(row_id == 7, ref[z, 8 * up : 8 * up + 8, :], here), 1, 0)
+        below = pltpu.roll(jnp.where(row_id == 0, ref[z, 8 * down : 8 * down + 8, :], here), 7, 0)
         left = pltpu.roll(here, 1, 1)
         right = pltpu.roll(here, EXT_COLS - 1, 1)
         return here, (above + below) + (left + right)
 
     buffers = [(a_ref, b_ref), (b_ref, a_ref), (a_ref, b_ref), (b_ref, None)]
     quenches = [(None, p_ref), (p_ref, q_ref), (q_ref, p_ref), (p_ref, None)]
+    copies = []
     for step in range(BAKE):
         old, new = buffers[step]
         q_old, q_new = quenches[step]
-
-        def row_step(t, carry):
-            rows = pl.ds(pl.multiple_of(t * 8, 8), 8)
+        for t in range(tiles if new is not None else BRICK_ROWS // 8):
+            rows = slice(8 * t, 8 * t + 8)
             acid = [neighbours(old, z, t) for z in range(Z)]
             acid_z = acid[0][0] + acid[1][0]
             if q_old is None:
@@ -513,51 +556,58 @@
             quench_z = quench_here[0] + quench_here[1]
             for z in range(Z):
                 here, around = acid[z]
-                reaction = QUENCH_RATE * here * quench_here[z]
-                lap = (around + acid_z) - 6.0 * here
-                fresh = here + DIFF_ACID * lap - reaction
+                reaction = here * quench_here[z]
+                fresh = ((1.0 - 6.0 * DIFF_ACID) * here + DIFF_ACID * (around + acid_z)) - reaction
                 if new is not None:
                     new[z, rows, :] = fresh
                 else:
-                    acid_ref[z, rows, :] = fresh[:, :BRICK_COLS]
+                    acid_ref[z, rows, :] = fresh[:, :BRICK_COLS] * (1.0 / QUENCH_RATE)
                 if q_new is not None:
-                    q_lap = (quench_sum[z] + quench_z) - 6.0 * quench_here[z]
-                    q_new[z, rows, :] = quench_here[z] + DIFF_QUENCH * q_lap - reaction
-                if step == 0:
-                    sum_ref[z, rows, :] = here[:, :BRICK_COLS]
-                elif new is not None:
-                    sum_ref[z, rows, :] = sum_ref[z, rows, :] + here[:, :BRICK_COLS]
-                else:
-                    total = sum_ref[z, rows, :] + here[:, :BRICK_COLS]
-                    inhibitor_ref[z, rows, :] = jnp.exp(-CATALYSIS * total)
-            return carry
-
-        lax.fori_loop(0, tiles if new is not None else BRICK_ROWS // 8, row_step, 0, unroll=BAKE_UNROLL)
-
-
-def resist_call(where, weights, quencher, own, other, window, rows, cols, dose, side, above, below):
+                    kept = (1.0 - 6.0 * DIFF_QUENCH) * quench_here[z]
+                    q_new[z, rows, :] = (kept + DIFF_QUENCH * (quench_sum[z] + quench_z)) - reaction
+                if t < BRICK_ROWS // 8:
+                    if step == 0:
+                        sum_ref[z, rows, :] = here[:, :BRICK_COLS]
+                    elif new is not None:
+                        sum_ref[z, rows, :] = sum_ref[z, rows, :] + here[:, :BRICK_COLS]
+                    else:
+                        total = sum_ref[z, rows, :] + here[:, :BRICK_COLS]
+                        inhibitor_ref[z, rows, :] = jnp.exp((-CATALYSIS / QUENCH_RATE) * total)
+            if new is None and t % 4 == 3:
+                ready = pl.ds(8 * (t - 3), 32)
+                for k, (near, far) in enumerate(((acid_ref, acid_hbm), (inhibitor_ref, inhibitor_hbm))):
+                    copy = pltpu.make_async_copy(near.at[:, ready], far.at[:, ready], out_sems.at[t // 4, k])
+                    copy.start()
+                    copies.append(copy)
+    for copy in copies:
+        copy.wait()
+
+
+def resist_call(where, weights, quencher, half, other, window, rows, cols, dose, side, above, below):
     smem = pl.BlockSpec(memory_space=pltpu.SMEM)
     vmem = pl.BlockSpec(memory_space=pltpu.VMEM)
     hbm = pl.BlockSpec(memory_space=pl.ANY)
-    out = jax.ShapeDtypeStruct((Z, BRICK_ROWS, BRICK_COLS), jnp.float32)
+    brick_shape = (Z, BRICK_ROWS, BRICK_COLS)
+    out = jax.ShapeDtypeStruct(brick_shape, jnp.float32)
     brick = pltpu.VMEM((Z, EXT_ROWS, EXT_COLS), jnp.float32)
+    near = pltpu.VMEM(brick_shape, jnp.float32)
     return pl.pallas_call(
         resist_kernel,
         out_shape=(out, out),
-        in_specs=[smem] * 3 + [vmem] * 3 + [hbm] * 2 + [vmem] * 4,
-        out_specs=(vmem, vmem),
+        in_specs=[smem] * 3 + [vmem] * 4 + [hbm] + [vmem] * 4,
+        out_specs=(hbm, hbm),
         scratch_shapes=[
-            pltpu.VMEM(rows.shape[1:], jnp.bfloat16),
             pltpu.VMEM(cols.shape[1:], jnp.bfloat16),
-            pltpu.VMEM((2, PASS // 2, 2 * PASS), jnp.bfloat16),
+            pltpu.VMEM((2, HALF, 2 * PASS), jnp.bfloat16),
             pltpu.VMEM((SOURCES * TALL, 2 * PASS), jnp.bfloat16),
             brick, brick, brick, brick,
-            pltpu.VMEM((Z, EXT_ROWS, BRICK_COLS), jnp.float32),
+            near, near, near,
             pltpu.SemaphoreType.DMA((2,)),
+            pltpu.SemaphoreType.DMA((4, 2)),
         ],
-        compiler_params=pltpu.CompilerParams(vmem_limit_bytes=28 * MIB),
+        compiler_params=pltpu.CompilerParams(vmem_limit_bytes=46 * MIB),
         name="resist",
-    )(where, weights, quencher, own, other, window, rows, cols, dose, side, above, below)
+    )(where, weights, quencher, half, other, window, rows, cols, dose, side, above, below)
 
 
 def ring(axes, step):
@@ -586,14 +636,15 @@
 
     block = spectrum_call(jnp.asarray(forward_rows()), cols, jnp.asarray(edge_rows()))
     own = lax.all_to_all(block, ("y", "x"), 0, 0, tiled=True)
-    own, turned, all_shifts, all_weights, side, above, below, where = lax.optimization_barrier(
-        (own, turned, all_shifts, all_weights, side, above, below, where)
+    window, token = window_call(all_shifts, turned)
+    own, token, all_weights, side, above, below, where = lax.optimization_barrier(
+        (own, token, all_weights, side, above, below, where)
     )
     other = lax.ppermute(own, "c", [(0, 1), (1, 0)])
-    window, dose_near = window_call(all_shifts, turned, dose)
+    half, row_table, window_other, dose_near = own_call(where, token, own, window, jnp.asarray(inverse_rows(32)), dose)
     return resist_call(
-        where, all_weights, quencher, own, other, window,
-        jnp.asarray(inverse_rows(32)), jnp.asarray(inverse_cols(4)), dose_near, side, above, below,
+        where, all_weights, quencher, half, other, window_other, row_table,
+        jnp.asarray(inverse_cols(4)), dose_near, side, above, below,
     )
 
 

time: 80.2 us -> 74.7 us (0.931)
  waiting for transfers between devices: 14.6 us -> 7.87 us
  local copies, waits for them, and re-layouts: 6.7 us -> 8.19 us
    ppermute x1, waiting for transfers between devices: 12.4 us -> 4.79 us  [body(): above = lax.ppermute(last, tile_axes, ring(tile_axes, 1))]
    pallas_call x1 -> x2, Pallas kernels: 4.04 us -> 9.62 us  [the longest x1 5.35 us: window_call(): pl.pallas_call(window_kernel, out_shape=(jax.ShapeDtypeStruct((3 * planes...]
    pallas_call x1, Pallas kernels: 13.3 us -> 10.5 us  [resist_call(): pl.pallas_call(resist_kernel, out_shape=(out, out), in_specs=[smem] * 3 +...]
    pallas_call x1, Pallas kernels: 5.53 us -> 3.42 us  [spectrum_call(): pl.pallas_call(spectrum_kernel, grid=(4,), out_shape=jax.ShapeDtypeStruct...]
    unnamed x14 -> x16, local copies, waits for them, and re-layouts: 6.23 us -> 7.72 us
    ppermute x1, starting transfers between devices: 1.07 us -> 0.01 us  [body(): after = lax.ppermute(first, src_axes, ring(src_axes, -1))]
    ppermute x1, starting transfers between devices: 0.69 us -> 1.75 us  [body(): before = lax.ppermute(last, src_axes, ring(src_axes, 1))]
    ppermute x1, starting transfers between devices: 0.55 us -> 1.61 us  [body(): other = lax.ppermute(own, 'c', [(0, 1), (1, 0)])]
  transfers between devices with their start and end apart: 8 -> 8, of which waited for: 2 -> 2; matrix products, arithmetic and copies ran while one was open for 1% -> 1% of each run, Pallas kernels for 14% -> 20%
where the time goes in v3:
time: 74.7 us; the launch traced here: 74.3 us
  Pallas kernels  30.1 us (40%)
  starting transfers between devices  26.5 us (35%)
  local copies, waits for them, and re-layouts  8.19 us (11%)
  waiting for transfers between devices  7.87 us (11%)
  between operations  1.58 us (2%)
    all_to_all x1, starting transfers between devices, body(): cols = lax.all_to_all(packed, ALL, 0, 0, tiled=True)  11.5 us
    pallas_call x1, Pallas kernels, resist_call(): pl.pallas_call(resist_kernel, out_shape=(out, out), in_specs=[smem] * 3 +...  10.5 us
    unnamed x16, local copies, waits for them, and re-layouts  7.72 us
    ppermute x1, starting transfers between devices, body(): below = lax.ppermute(first, tile_axes, ring(tile_axes, -1))  5.95 us
    pallas_call x1, Pallas kernels, window_call(): pl.pallas_call(window_kernel, out_shape=(jax.ShapeDtypeStruct((3 * planes...  5.35 us
    pallas_call x1, Pallas kernels, columns_call(): pl.pallas_call(columns_kernel, grid=(steps,), out_shape=jax.ShapeDtypeStr...  5.07 us
    ppermute x1, waiting for transfers between devices, body(): above = lax.ppermute(last, tile_axes, ring(tile_axes, 1))  4.79 us
    pallas_call x1, Pallas kernels, own_call(): pl.pallas_call(own_kernel, out_shape=(jax.ShapeDtypeStruct((SOURCES * TAL...  4.28 us
  transfers between devices with their start and end apart: 8, of which 2 were waited for; matrix products, arithmetic and copies ran while one was open for 1% of the time, Pallas kernels for 20%

profile of v3, /device:TPU:1, one launch (start us, length us, event | category | flops | bytes accessed | tf_op | source)
XLA Modules:
  0.0 74.3 jit_solution(15636179270602855253)
XLA Ops:
  0.6 0.0 copy-start.5
  0.6 0.0 copy-start
  0.7 0.0 copy-start.6
  0.7 5.1 %columns.1 = bf16[1024,128]{1,0:T(8,128)(2,1)} custom-call(f32[2,4]{1,0:T(2,128)} %trans_ref.1, s32[32,4096]{1,0:T(8,128)} %ids_ref.1, bf16[4096,512]{1,0:T(8,128)(2,1)} %constant.38.clone.table_ref, f32[2,128]{1,0:T(2,128)} %constant.39.clone.edge_ref), custom_call_target="tpu_custom_call" | custom-call | tf_op jit(solution)/shard_map/columns/pallas_call | solution.py:173
  5.7 11.5 %all-to-all-start = ((bf16[128,8,128]{2,1,0:T(8,128)(2,1)}), bf16[128,8,128]{2,1,0:T(8,128)(2,1)S(1)}, u32[]{:S(2)}, u32[]{:S(2)}) async-start(bf16[128,8,128]{2,1,0:T(8,128)(2,1)} %bitcast.14), calls=%async_computation | async-start | bytes 524288 | tf_op jit(solution)/shard_map/all_to_all | solution.py:623
  17.9 0.0 copy-done
  17.9 0.0 copy-done.6
  17.9 0.0 copy-start.2
  17.9 1.9 %copy-done.2 = f32[2,640,640]{2,1,0:T(8,128)S(1)} copy-done((f32[2,640,640]{2,1,0:T(8,128)S(1)}, f32[2,640,640]{2,1,0:T(8,128)}, u32[]{:S(2)}) %copy-start.2) | copy-done | bytes 3276824
  19.8 1.4 %pack.1 = (f32[2,640,640]{2,1,0:T(8,128)S(1)}, f32[2,128,128]{2,1,0:T(8,128)S(1)}, f32[2,128,128]{2,1,0:T(8,128)S(1)}, f32[8,128]{1,0:T(8,128)S(1)}) custom-call(s32[1,2]{1,0:T(1,128)S(1)} %copy-done.6, f32[1]{0:T(128)S(6)} %copy.15.weights_ref, f32[2,640,640]{2,1,0:T(8,128)S(1)} %copy-done.2, f32[2,128,1024]{2,1,0:T(8,128)S(1)} %copy-done), custom_call_target="tpu_custom_call" | custom-call | flops 1000000 | bytes 9000000 | tf_op jit(solution)/shard_map/pack/pallas_call | solution.py:289
  21.3 0.0 copy-start.3
  21.3 1.7 %copy-done.3 = f32[2,640,640]{2,1,0:T(8,128)} copy-done((f32[2,640,640]{2,1,0:T(8,128)}, f32[2,640,640]{2,1,0:T(8,128)S(1)}, u32[]{:S(2)}) %copy-start.3) | copy-done | bytes 3276824
  23.0 1.8 %collective-permute-start.1 = (f32[2,128,128]{2,1,0:T(8,128)S(1)}, f32[2,128,128]{2,1,0:T(8,128)S(1)}, u32[]{:S(2)}, u32[]{:S(2)}) collective-permute-start(f32[2,128,128]{2,1,0:T(8,128)S(1)} %get-tuple-element.33), channel_id=1, source_target_pairs={{0,32},{32,64},{64,96},{96,0},{1,33},{33,65},{65,97},{97,1},{2,34}... | collective-permute-start | bytes 393224 | tf_op jit(solution)/shard_map/ppermute | solution.py:626
  24.7 0.0 collective-permute-start.2
  24.7 0.7 collective-permute-start
  25.4 3.1 %all-to-all-done = bf16[128,8,128]{2,1,0:T(8,128)(2,1)S(1)} async-done(((bf16[128,8,128]{2,1,0:T(8,128)(2,1)}), bf16[128,8,128]{2,1,0:T(8,128)(2,1)S(1)}, u32[]{:S(2)}, u32[]{:S(2)}) %all-to-all-start) | async-done | bytes 262176 | tf_op jit(solution)/shard_map/all_to_all | solution.py:623
  28.5 0.0 copy-done.5
  28.5 0.0 copy-start.1
  28.5 2.2 %copy-done.1 = bf16[4,512,1024]{2,1,0:T(8,128)(2,1)S(1)} copy-done((bf16[4,512,1024]{2,1,0:T(8,128)(2,1)S(1)}, bf16[4,512,1024]{2,1,0:T(8,128)(2,1)}, u32[]{:S(2)}) %copy-start.1) | copy-done | bytes 4194328
  30.7 3.4 %spectrum.1 = f32[512,512]{1,0:T(8,128)} custom-call(bf16[4,512,1024]{2,1,0:T(8,128)(2,1)S(1)} %copy-done.1, bf16[1024,128]{1,0:T(8,128)(2,1)S(1)} %bitcast.13, f32[2,8,128]{2,1,0:T(8,128)S(1)} %copy-done.5), custom_call_target="tpu_custom_call" | custom-call | tf_op jit(solution)/shard_map/spectrum/pallas_call | solution.py:248
  34.1 3.7 %all-to-all-start.1 = ((f32[16,32,512]{2,1,0:T(8,128)}), f32[16,32,512]{2,1,0:T(8,128)S(1)}, u32[]{:S(2)}, u32[]{:S(2)}) async-start(f32[16,32,512]{2,1,0:T(8,128)} %bitcast.2), calls=%async_computation.1 | async-start | bytes 2097152 | tf_op jit(solution)/shard_map/all_to_all | solution.py:638
  37.8 0.1 pad_add_fusion.where_ref
  37.8 0.1 slice.18
  37.9 0.0 collective-permute-done
  37.9 0.1 slice.19
  38.0 0.0 collective-permute-done.1.before_ref
  38.0 0.0 collective-permute-done.2.after_ref
  38.0 1.3 %collective-permute-start.3 = (f32[2,8,1152]{2,1,0:T(8,128)S(1)}, f32[2,8,1152]{2,1,0:T(8,128)S(1)}, u32[]{:S(2)}, u32[]{:S(2)}) collective-permute-start(f32[2,8,1152]{2,1,0:T(8,128)S(1)} %get-tuple-element.38), channel_id=1, source_target_pairs={{0,1},{1,2},{2,3},{3,4},{4,5},{5,6},{6,7},{7,8},{8,9},{9,10},{10,1... | collective-permute-start | bytes 221192 | tf_op jit(solution)/shard_map/ppermute | solution.py:633
  39.3 5.9 %collective-permute-start.4 = (f32[2,8,1152]{2,1,0:T(8,128)S(1)}, f32[2,8,1152]{2,1,0:T(8,128)S(1)}, u32[]{:S(2)}, u32[]{:S(2)}) collective-permute-start(f32[2,8,1152]{2,1,0:T(8,128)S(1)} %get-tuple-element.39), channel_id=1, source_target_pairs={{0,31},{1,0},{2,1},{3,2},{4,3},{5,4},{6,5},{7,6},{8,7},{9,8},{10,9... | collective-permute-start | bytes 221192 | tf_op jit(solution)/shard_map/ppermute | solution.py:634
  45.3 0.1 slice_bitcast_fusion.1
  45.3 0.1 slice_bitcast_fusion
  45.4 0.0 copy-start.4
  45.5 1.9 %copy-done.4 = f32[2,640,640]{2,1,0:T(8,128)S(1)} copy-done((f32[2,640,640]{2,1,0:T(8,128)S(1)}, f32[2,640,640]{2,1,0:T(8,128)}, u32[]{:S(2)}) %copy-start.4) | copy-done | bytes 3276824
  47.4 5.3 %window.1 = (f32[24,512,512]{2,1,0:T(8,128)}, f32[8,128]{1,0:T(8,128)S(1)}) custom-call(s32[4,2]{1,0:T(4,128)S(1)} %slice_convert_fusion.shifts_ref, f32[2,640,640]{2,1,0:T(8,128)S(1)} %copy-done.4), custom_call_target="tpu_custom_call" | custom-call | flops 10000000 | bytes 11000000 | tf_op jit(solution)/shard_map/window/pallas_call | solution.py:393
  52.7 0.2 slice_reduce_fusion.weights_ref
  52.9 4.8 %collective-permute-done.3.above_ref = f32[2,8,1152]{2,1,0:T(8,128)S(1)} collective-permute-done((f32[2,8,1152]{2,1,0:T(8,128)S(1)}, f32[2,8,1152]{2,1,0:T(8,128)S(1)}, u32[]{:S(2)}, u32[]{:S(2)}) %collective-permute-start.3) | collective-permute-done | bytes 73760 | tf_op jit(solution)/shard_map/ppermute | solution.py:633
  57.7 0.0 collective-permute-done.4.below_ref
  57.7 0.0 all-to-all-done.1
  57.7 1.6 %collective-permute-start.5 = (f32[512,512]{1,0:T(8,128)S(1)}, f32[512,512]{1,0:T(8,128)S(1)}, u32[]{:S(2)}, u32[]{:S(2)}) collective-permute-start(f32[512,512]{1,0:T(8,128)S(1)} %bitcast.11), channel_id=1, source_target_pairs={{0,32},{32,0},{1,33},{33,1},{2,34},{34,2},{3,35},{35,3},{4,36},{36... | collective-permute-start | bytes 3145736 | tf_op jit(solution)/shard_map/ppermute | solution.py:643
  59.3 0.0 copy-start.7
  59.3 4.3 %own_half.1 = (bf16[576,512]{1,0:T(8,128)(2,1)S(1)}, bf16[288,1024]{1,0:T(8,128)(2,1)S(1)}, f32[8,256,512]{2,1,0:T(8,128)S(1)}, f32[2,128,1024]{2,1,0:T(8,128)S(1)}) custom-call(s32[3]{0:T(128)S(1)} %pad_add_fusion.where_ref, f32[8,128]{1,0:T(8,128)S(1)} %get-tuple-element.42.token_ref, f32[512,512]{1,0:T(8,128)S(1)} %bitcast.12, ...), custom_call_target="tpu_custom_call" | custom-call | flops 10000000 | bytes 9000000 | tf_op jit(solution)/shard_map/own_half/pallas_call | solution.py:465
  63.6 0.0 collective-permute-done.5.other_ref
  63.6 0.0 copy-done.7
  63.6 10.5 %resist.1 = (f32[2,128,1024]{2,1,0:T(8,128)}, f32[2,128,1024]{2,1,0:T(8,128)}) custom-call(s32[3]{0:T(128)S(1)} %pad_add_fusion.where_ref, f32[4]{0:T(128)S(1)} %slice_reduce_fusion.weights_ref, f32[2]{0:T(128)S(1)} %copy-done.7, bf16[576,512]{1,0:T(8,128)(2,1)S(1)} %get-tuple-element.45.half_ref, f32[512,512]{1,0:T(8,128)S(1)} %collective-permute-done.5.other_ref, ...), custom_call_target="tpu_custom_call" | custom-call | tf_op jit(solution)/shard_map/resist/pallas_call | solution.py:594
  (3 shorter events, 0.0 us)
Async XLA Ops:
  0.6 27.9 %copy-start.5 = (f32[2,8,128]{2,1,0:T(8,128)S(1)}, f32[2,8,128]{2,1,0:T(8,128)}, u32[]{:S(2)}) copy-start(f32[2,8,128]{2,1,0:T(8,128)} %constant.41.clone.edge_ref) | copy-start | bytes 24580
  0.6 17.2 %copy-start = (f32[2,128,1024]{2,1,0:T(8,128)S(1)}, f32[2,128,1024]{2,1,0:T(8,128)}, u32[]{:S(2)}) copy-start(f32[2,128,1024]{2,1,0:T(8,128)} %dose_hbm.1) | copy-start | bytes 3145732
  0.7 17.2 %copy-start.6 = (s32[1,2]{1,0:T(1,128)S(1)}, s32[1,2]{1,0:T(1,128)}, u32[]{:S(2)}) copy-start(s32[1,2]{1,0:T(1,128)} %shifts_ref) | copy-start | bytes 28
  5.7 22.7 %all-to-all-start = ((bf16[128,8,128]{2,1,0:T(8,128)(2,1)}), bf16[128,8,128]{2,1,0:T(8,128)(2,1)S(1)}, u32[]{:S(2)}, u32[]{:S(2)}) async-start(bf16[128,8,128]{2,1,0:T(8,128)(2,1)} %bitcast.14), calls=%async_computation | async-start | bytes 524288 | tf_op jit(solution)/shard_map/all_to_all | solution.py:623
  17.9 1.9 %copy-start.2 = (f32[2,640,640]{2,1,0:T(8,128)S(1)}, f32[2,640,640]{2,1,0:T(8,128)}, u32[]{:S(2)}) copy-start(f32[2,640,640]{2,1,0:T(8,128)} %pupil_ref) | copy-start | bytes 9830404
  21.3 1.7 %copy-start.3 = (f32[2,640,640]{2,1,0:T(8,128)}, f32[2,640,640]{2,1,0:T(8,128)S(1)}, u32[]{:S(2)}) copy-start(f32[2,640,640]{2,1,0:T(8,128)S(1)} %get-tuple-element.35.turned_ref) | copy-start | bytes 9830404
  23.0 15.0 %collective-permute-start.1 = (f32[2,128,128]{2,1,0:T(8,128)S(1)}, f32[2,128,128]{2,1,0:T(8,128)S(1)}, u32[]{:S(2)}, u32[]{:S(2)}) collective-permute-start(f32[2,128,128]{2,1,0:T(8,128)S(1)} %get-tuple-element.33), channel_id=1, source_target_pairs={{0,32},{32,64},{64,96},{96,0},{1,33},{33,65},{65,97},{97,1},{2,34}... | collective-permute-start | bytes 393224 | tf_op jit(solution)/shard_map/ppermute | solution.py:626
  24.7 13.3 %collective-permute-start.2 = (f32[2,128,128]{2,1,0:T(8,128)S(1)}, f32[2,128,128]{2,1,0:T(8,128)S(1)}, u32[]{:S(2)}, u32[]{:S(2)}) collective-permute-start(f32[2,128,128]{2,1,0:T(8,128)S(1)} %get-tuple-element.34), channel_id=1, source_target_pairs={{0,96},{32,0},{64,32},{96,64},{1,97},{33,1},{65,33},{97,65},{2,98}... | collective-permute-start | bytes 393224 | tf_op jit(solution)/shard_map/ppermute | solution.py:627
  24.7 13.2 %collective-permute-start = (f32[8,128]{1,0:T(8,128)S(1)}, f32[8,128]{1,0:T(8,128)S(1)}, u32[]{:S(2)}, u32[]{:S(2)}) collective-permute-start(f32[8,128]{1,0:T(8,128)S(1)} %get-tuple-element.32), channel_id=1, source_target_pairs={{0,64},{32,96},{64,0},{96,32},{1,65},{33,97},{65,1},{97,33},{2,66}... | collective-permute-start | bytes 12296 | tf_op jit(solution)/shard_map/ppermute | solution.py:628
  28.5 2.2 %copy-start.1 = (bf16[4,512,1024]{2,1,0:T(8,128)(2,1)S(1)}, bf16[4,512,1024]{2,1,0:T(8,128)(2,1)}, u32[]{:S(2)}) copy-start(bf16[4,512,1024]{2,1,0:T(8,128)(2,1)} %constant.40.clone.table_ref) | copy-start | bytes 12582916
  34.1 23.6 %all-to-all-start.1 = ((f32[16,32,512]{2,1,0:T(8,128)}), f32[16,32,512]{2,1,0:T(8,128)S(1)}, u32[]{:S(2)}, u32[]{:S(2)}) async-start(f32[16,32,512]{2,1,0:T(8,128)} %bitcast.2), calls=%async_computation.1 | async-start | bytes 2097152 | tf_op jit(solution)/shard_map/all_to_all | solution.py:638
  38.0 19.7 %collective-permute-start.3 = (f32[2,8,1152]{2,1,0:T(8,128)S(1)}, f32[2,8,1152]{2,1,0:T(8,128)S(1)}, u32[]{:S(2)}, u32[]{:S(2)}) collective-permute-start(f32[2,8,1152]{2,1,0:T(8,128)S(1)} %get-tuple-element.38), channel_id=1, source_target_pairs={{0,1},{1,2},{2,3},{3,4},{4,5},{5,6},{6,7},{7,8},{8,9},{9,10},{10,1... | collective-permute-start | bytes 221192 | tf_op jit(solution)/shard_map/ppermute | solution.py:633
  39.3 18.4 %collective-permute-start.4 = (f32[2,8,1152]{2,1,0:T(8,128)S(1)}, f32[2,8,1152]{2,1,0:T(8,128)S(1)}, u32[]{:S(2)}, u32[]{:S(2)}) collective-permute-start(f32[2,8,1152]{2,1,0:T(8,128)S(1)} %get-tuple-element.39), channel_id=1, source_target_pairs={{0,31},{1,0},{2,1},{3,2},{4,3},{5,4},{6,5},{7,6},{8,7},{9,8},{10,9... | collective-permute-start | bytes 221192 | tf_op jit(solution)/shard_map/ppermute | solution.py:634
  45.4 1.9 %copy-start.4 = (f32[2,640,640]{2,1,0:T(8,128)S(1)}, f32[2,640,640]{2,1,0:T(8,128)}, u32[]{:S(2)}) copy-start(f32[2,640,640]{2,1,0:T(8,128)} %copy-done.3) | copy-start | bytes 9830404
  57.7 5.9 %collective-permute-start.5 = (f32[512,512]{1,0:T(8,128)S(1)}, f32[512,512]{1,0:T(8,128)S(1)}, u32[]{:S(2)}, u32[]{:S(2)}) collective-permute-start(f32[512,512]{1,0:T(8,128)S(1)} %bitcast.11), channel_id=1, source_target_pairs={{0,32},{32,0},{1,33},{33,1},{2,34},{34,2},{3,35},{35,3},{4,36},{36... | collective-permute-start | bytes 3145736 | tf_op jit(solution)/shard_map/ppermute | solution.py:643
  59.3 4.3 %copy-start.7 = (f32[2]{0:T(128)S(1)}, f32[2]{0:T(128)}, u32[]{:S(2)}) copy-start(f32[2]{0:T(128)} %quencher_ref.1) | copy-start | bytes 28

commit v4 on v3

--- a/solution.py
+++ b/solution.py
@@ -36,6 +36,7 @@
 EARLY = 2
 ALL = ("zl", "c", "y", "zh", "x")
 MIB = 1024 * 1024
+PARTS = 4
 
 
 def cos_sin(first, second):
@@ -57,9 +58,9 @@
 
 
 def forward_rows():
-    order = np.arange(NPIX).reshape(DEVICES, 4, 8).transpose(1, 0, 2).reshape(NPIX)
+    order = np.arange(NPIX).reshape(2, 2, DEVICES // 4, 2, 16).transpose(1, 3, 0, 2, 4).reshape(NPIX)
     both = np.concatenate(cos_sin(np.arange(HALF), order), axis=0)
-    return bf16(both.reshape(PASS, 4, NPIX // 4).transpose(1, 0, 2))
+    return bf16(both.reshape(PASS, 2, 2, NPIX // 4).transpose(1, 2, 0, 3))
 
 
 def edge_columns():
@@ -68,10 +69,9 @@
 
 
 def edge_rows():
-    rows = np.arange(4)[None, :] * 8 + np.arange(8)[:, None]
-    cosine, sine = cos_sin(np.array([HALF]), rows.reshape(-1))
-    both = np.stack([cosine.reshape(8, 4), sine.reshape(8, 4)])
-    return np.asarray(bf16(np.repeat(both, WIDE, axis=2))).astype(np.float32)
+    cosine, sine = cos_sin(np.array([HALF]), np.arange(16))
+    both = np.repeat(np.stack([cosine.reshape(16, 1), sine.reshape(16, 1)]), 128, axis=2)
+    return np.asarray(bf16(both)).astype(np.float32)
 
 
 def inverse_rows(tiles):
@@ -105,160 +105,171 @@
     return lax.broadcasted_iota(jnp.int32, shape, len(shape) - 1)
 
 
-def columns_kernel(trans_ref, ids_ref, table_ref, edge_ref, out_ref, acc_ref, sum_ref, perm_ref):
-    step = pl.program_id(0)
-
-    @pl.when(step == 0)
-    def _():
-        acc_ref[...] = jnp.zeros_like(acc_ref)
-        sum_ref[...] = jnp.zeros_like(sum_ref)
-        source = lax.broadcasted_iota(jnp.int32, (PASS, PASS), 0)
-        lane = lax.broadcasted_iota(jnp.int32, (PASS, PASS), 1)
-        plane, place = lane // FREQS % 2, lane // WIDE * FREQS + lane % FREQS
-        perm_ref[0] = (source == plane * HALF + (HALF - place) % HALF).astype(jnp.float32).astype(jnp.bfloat16)
-        perm_ref[1] = (source == plane * HALF + place).astype(jnp.float32).astype(jnp.bfloat16)
-
-    ids = ids_ref[...]
-    parts = []
-    for plane in range(2):
-        value = jnp.zeros(ids.shape, jnp.float32)
-        for level in range(LEVELS):
-            value = jnp.where(ids == level, trans_ref[plane, level], value)
-        parts.append(value)
-    trans = jnp.concatenate(parts, axis=0).astype(jnp.bfloat16)
-    acc_ref[...] += jnp.dot(trans, table_ref[...], preferred_element_type=jnp.float32)
-    exact = trans.astype(jnp.float32)
-    total = sum_ref[...]
-    for tile in range(ids.shape[1] // 128):
-        total = total + exact[:, 128 * tile : 128 * tile + 128]
-    sum_ref[...] = total
-
-    @pl.when(step == pl.num_programs(0) - 1)
-    def _():
-        edge_cos = jnp.sum(sum_ref[...] * edge_ref[0:1, :], axis=1, keepdims=True)
-        edge_sin = jnp.sum(sum_ref[...] * edge_ref[1:2, :], axis=1, keepdims=True)
-        cos_real, cos_imag = acc_ref[:ROWS, :HALF], acc_ref[ROWS:, :HALF]
-        sin_real, sin_imag = acc_ref[:ROWS, HALF:], acc_ref[ROWS:, HALF:]
-        first = lane_ids((ROWS, HALF)) == 0
-        low_real = jnp.where(first, edge_cos[:ROWS] - edge_sin[ROWS:], cos_real - sin_imag)
-        low_imag = jnp.where(first, edge_cos[ROWS:] + edge_sin[:ROWS], cos_imag + sin_real)
-        low = jnp.concatenate([low_real, low_imag], axis=1).astype(jnp.bfloat16)
-        high = jnp.concatenate([cos_real + sin_imag, cos_imag - sin_real], axis=1).astype(jnp.bfloat16)
-        sides = [
-            jnp.dot(low, perm_ref[0], preferred_element_type=jnp.float32),
-            jnp.dot(high, perm_ref[1], preferred_element_type=jnp.float32),
-        ]
-        group = lane_ids((8, 128)) // WIDE
-        chunks = []
-        for owner in range(OWNERS):
-            major, minor = owner % 16 // 4, owner % 4
-            chunk = jnp.zeros((8, 128), jnp.float32)
-            for q in range(4):
-                piece = sides[owner // 16][8 * q : 8 * q + 8, 128 * major : 128 * major + 128]
-                turn = (q - minor) % 4 * WIDE
+def columns_kernel(trans_ref, ids_hbm, table_hbm, edge_ref, out_ref, ids_ref, table_ref, perm_ref, sems):
+    depth = NPIX // PARTS
+    copies = []
+    for k in range(PARTS):
+        part = pl.ds(k * depth, depth)
+        both = (
+            pltpu.make_async_copy(ids_hbm.at[:, part], ids_ref.at[:, part], sems.at[0, k]),
+            pltpu.make_async_copy(table_hbm.at[part], table_ref.at[part], sems.at[1, k]),
+        )
+        for copy in both:
+            copy.start()
+        copies.append(both)
+    source = lax.broadcasted_iota(jnp.int32, (PASS, PASS), 0)
+    lane = lax.broadcasted_iota(jnp.int32, (PASS, PASS), 1)
+    plane, place = lane // FREQS % 2, lane // WIDE * FREQS + lane % FREQS
+    perm_ref[0] = (source == plane * HALF + (HALF - place) % HALF).astype(jnp.float32).astype(jnp.bfloat16)
+    perm_ref[1] = (source == plane * HALF + place).astype(jnp.float32).astype(jnp.bfloat16)
+    acc = jnp.zeros((2 * ROWS, PASS), jnp.float32)
+    total = jnp.zeros((2 * ROWS, 128), jnp.float32)
+    for k in range(PARTS):
+        part = slice(k * depth, k * depth + depth)
+        copies[k][0].wait()
+        ids = ids_ref[:, part]
+        planes = []
+        for plane in range(2):
+            value = jnp.zeros(ids.shape, jnp.float32)
+            for level in range(LEVELS):
+                value = jnp.where(ids == level, trans_ref[plane, level], value)
+            planes.append(value)
+        trans = jnp.concatenate(planes, axis=0).astype(jnp.bfloat16)
+        exact = trans.astype(jnp.float32)
+        for tile in range(depth // 128):
+            total = total + exact[:, 128 * tile : 128 * tile + 128]
+        copies[k][1].wait()
+        acc = acc + jnp.dot(trans, table_ref[part, :], preferred_element_type=jnp.float32)
+    edge_cos = jnp.sum(total * edge_ref[0:1, :], axis=1, keepdims=True)
+    edge_sin = jnp.sum(total * edge_ref[1:2, :], axis=1, keepdims=True)
+    cos_real, cos_imag = acc[:ROWS, :HALF], acc[ROWS:, :HALF]
+    sin_real, sin_imag = acc[:ROWS, HALF:], acc[ROWS:, HALF:]
+    first = lane_ids((ROWS, HALF)) == 0
+    low_real = jnp.where(first, edge_cos[:ROWS] - edge_sin[ROWS:], cos_real - sin_imag)
+    low_imag = jnp.where(first, edge_cos[ROWS:] + edge_sin[:ROWS], cos_imag + sin_real)
+    low = jnp.concatenate([low_real, low_imag], axis=1).astype(jnp.bfloat16)
+    high = jnp.concatenate([cos_real + sin_imag, cos_imag - sin_real], axis=1).astype(jnp.bfloat16)
+    sides = [
+        jnp.dot(low, perm_ref[0], preferred_element_type=jnp.float32),
+        jnp.dot(high, perm_ref[1], preferred_element_type=jnp.float32),
+    ]
+    group = lane_ids((16, 128)) // WIDE
+    for y in range(4):
+        for x in range(4):
+            owner = y * 4 + x
+            chunk = jnp.zeros((16, 128), jnp.float32)
+            for g in range(4):
+                q, side = g // 2, g % 2
+                major = owner // 4 * 128
+                piece = sides[side][16 * q : 16 * q + 16, major : major + 128]
+                turn = (g - owner) % 4 * WIDE
                 piece = pltpu.roll(piece, turn, 1) if turn else piece
-                chunk = jnp.where(group == q, piece, chunk)
-            chunks.append(chunk)
-        for pair in range(DEVICES // 2):
-            both = []
-            for dest in (2 * pair, 2 * pair + 1):
-                core, y, x = dest // 32 % 2, dest // 8 % 4, dest % 4
-                both.append(chunks[core * 16 + y * 4 + x])
-            out_ref[16 * pair : 16 * pair + 16, :] = jnp.concatenate(both, axis=0).astype(jnp.bfloat16)
+                chunk = jnp.where(group == g, piece, chunk)
+            value = chunk.astype(jnp.bfloat16)
+            for plane_z in range(4):
+                dest = plane_z // 2 * 32 + y * 8 + plane_z % 2 * 4 + x
+                out_ref[16 * dest : 16 * dest + 16, :] = value
 
 
 def columns_call(trans_table, mask_ids, table, edge):
-    steps = 4
-    depth = NPIX // steps
+    vmem = pl.BlockSpec(memory_space=pltpu.VMEM)
+    hbm = pl.BlockSpec(memory_space=pl.ANY)
     return pl.pallas_call(
         columns_kernel,
-        grid=(steps,),
-        out_shape=jax.ShapeDtypeStruct((DEVICES * 8, 128), jnp.bfloat16),
-        in_specs=[
-            pl.BlockSpec(memory_space=pltpu.SMEM),
-            pl.BlockSpec((ROWS, depth), lambda k: (0, k)),
-            pl.BlockSpec((depth, PASS), lambda k: (k, 0)),
-            pl.BlockSpec((2, 128), lambda k: (0, 0)),
-        ],
-        out_specs=pl.BlockSpec((DEVICES * 8, 128), lambda k: (0, 0)),
+        out_shape=jax.ShapeDtypeStruct((DEVICES // 2 * 16, 128), jnp.bfloat16),
+        in_specs=[pl.BlockSpec(memory_space=pltpu.SMEM), hbm, hbm, vmem],
+        out_specs=vmem,
         scratch_shapes=[
-            pltpu.VMEM((2 * ROWS, PASS), jnp.float32),
-            pltpu.VMEM((2 * ROWS, 128), jnp.float32),
+            pltpu.VMEM((ROWS, NPIX), jnp.int32),
+            pltpu.VMEM((NPIX, PASS), jnp.bfloat16),
             pltpu.VMEM((2, PASS, PASS), jnp.bfloat16),
+            pltpu.SemaphoreType.DMA((2, PARTS)),
         ],
         compiler_params=pltpu.CompilerParams(vmem_limit_bytes=56 * MIB),
         name="columns",
     )(trans_table, mask_ids, table, edge)
 
 
-def spectrum_kernel(table_ref, cols_ref, edge_ref, out_ref, acc_ref):
-    step = pl.program_id(0)
-    product = jnp.dot(table_ref[0], cols_ref[...], preferred_element_type=jnp.float32)
-    group = lane_ids(product.shape) // WIDE
-
-    @pl.when(step == 0)
-    def _():
-        acc_ref[...] = product
-
-    @pl.when(step > 0)
-    def _():
-        acc_ref[...] = jnp.where(group == step, product, acc_ref[...])
-
-    @pl.when(step == pl.num_programs(0) - 1)
-    def _():
-        columns = cols_ref[...].astype(jnp.float32)
-        total = [columns[16 * k : 16 * k + 16] for k in range(DEVICES // 2)]
-        while len(total) > 1:
-            total = [a + b for a, b in zip(total[::2], total[1::2])]
-        total = total[0][:8] + total[0][8:]
-        edge_cos = jnp.sum(total * edge_ref[0], axis=0, keepdims=True)
-        edge_sin = jnp.sum(total * edge_ref[1], axis=0, keepdims=True)
-
-        def fold(value):
-            value = value + pltpu.roll(value, 64, 1)
-            return value + pltpu.roll(value, 32, 1)
-
-        def turn(value):
-            is_real = lane_ids(value.shape) % WIDE < FREQS
-            return jnp.where(is_real, pltpu.roll(value, 128 - FREQS, 1), -pltpu.roll(value, FREQS, 1))
-
-        edges = fold(jnp.concatenate([edge_cos, edge_sin, jnp.zeros((6, 128), jnp.float32)], axis=0))
-        edge = edges[0:1] - turn(edges)[1:2]
-        folded = fold(acc_ref[...])
-        cosine, turned = folded[:HALF], turn(folded[HALF:])
-        first = lax.broadcasted_iota(jnp.int32, cosine.shape, 0) == 0
-        scale = 1.0 / (NPIX * NPIX)
-        high = jnp.transpose((cosine + turned) * scale)[:WIDE]
-        low = jnp.transpose(jnp.where(first, edge, cosine - turned) * scale)[:WIDE]
-        source = lax.broadcasted_iota(jnp.int32, (HALF, HALF), 0)
-        place = lax.broadcasted_iota(jnp.int32, (HALF, HALF), 1)
-        perm = (source == (HALF - place) % HALF).astype(jnp.float32).astype(jnp.bfloat16)
-        pieces = []
-        rest = low
-        for _ in range(3):
-            piece = rest.astype(jnp.bfloat16)
-            rest = rest - piece.astype(jnp.float32)
-            pieces.append(jnp.dot(piece, perm, preferred_element_type=jnp.float32))
-        block = jnp.concatenate([pieces[0] + pieces[1] + pieces[2], high], axis=1)
-        for dest in range(16):
-            out_ref[dest * WIDE : (dest + 1) * WIDE, :] = block
-
-
-def spectrum_call(table, cols, edge):
+def spectrum_kernel(core_ref, table_hbm, cols_ref, edge_ref, keep_ref, send_ref, table_ref, block_ref, sems):
+    core = core_ref[0]
+    copies = []
+    for q in range(2):
+        copies.append(pltpu.make_async_copy(table_hbm.at[core, q], table_ref.at[q], sems.at[q]))
+        copies[q].start()
+    columns = cols_ref[...].astype(jnp.float32)
+    total = [columns[16 * k : 16 * k + 16] for k in range(DEVICES // 2)]
+    while len(total) > 1:
+        total = [a + b for a, b in zip(total[::2], total[1::2])]
+    edge_cos = jnp.sum(total[0] * edge_ref[0], axis=0, keepdims=True)
+    edge_sin = jnp.sum(total[0] * edge_ref[1], axis=0, keepdims=True)
+
+    def turn(value):
+        is_real = lane_ids(value.shape) % WIDE < FREQS
+        return jnp.where(is_real, pltpu.roll(value, 128 - FREQS, 1), -pltpu.roll(value, FREQS, 1))
+
+    edges = jnp.concatenate([edge_cos, edge_sin, jnp.zeros((6, 128), jnp.float32)], axis=0)
+    edges = edges + pltpu.roll(edges, 64, 1)
+    edge = edges[0:1] - turn(edges)[1:2]
+    source = lax.broadcasted_iota(jnp.int32, (HALF, HALF), 0)
+    place = lax.broadcasted_iota(jnp.int32, (HALF, HALF), 1)
+    perm = (source == (HALF - place) % HALF).astype(jnp.float32).astype(jnp.bfloat16)
+    products = []
+    for q in range(2):
+        copies[q].wait()
+        products.append(jnp.dot(table_ref[q], cols_ref[...], preferred_element_type=jnp.float32))
+    folded = jnp.where(lane_ids((PASS, 128)) < 64, products[0], products[1])
+    folded = folded + pltpu.roll(folded, 64, 1)
+    cosine, turned = folded[:HALF], turn(folded[HALF:])
+    first = lax.broadcasted_iota(jnp.int32, cosine.shape, 0) == 0
+    scale = 1.0 / (NPIX * NPIX)
+    high = jnp.transpose((cosine + turned) * scale)[: 2 * WIDE]
+    low = jnp.transpose(jnp.where(first, edge, cosine - turned) * scale)[: 2 * WIDE]
+    pieces = []
+    rest = low
+    for _ in range(3):
+        piece = rest.astype(jnp.bfloat16)
+        rest = rest - piece.astype(jnp.float32)
+        pieces.append(jnp.dot(piece, perm, preferred_element_type=jnp.float32))
+    block_ref[:, :HALF] = pieces[0] + pieces[1] + pieces[2]
+    block_ref[:, HALF:] = high
+    keep_ref[...] = block_ref[pl.ds(pl.multiple_of(core * WIDE, WIDE), WIDE), :]
+    send_ref[...] = block_ref[pl.ds(pl.multiple_of((1 - core) * WIDE, WIDE), WIDE), :]
+
+
+def spectrum_call(core, table, cols, edge):
+    vmem = pl.BlockSpec(memory_space=pltpu.VMEM)
+    part = jax.ShapeDtypeStruct((WIDE, PASS), jnp.float32)
     return pl.pallas_call(
         spectrum_kernel,
-        grid=(4,),
+        out_shape=(part, part),
+        in_specs=[pl.BlockSpec(memory_space=pltpu.SMEM), pl.BlockSpec(memory_space=pl.ANY), vmem, vmem],
+        out_specs=(vmem, vmem),
+        scratch_shapes=[
+            pltpu.VMEM(table.shape[1:], jnp.bfloat16),
+            pltpu.VMEM((2 * WIDE, PASS), jnp.float32),
+            pltpu.SemaphoreType.DMA((2,)),
+        ],
+        compiler_params=pltpu.CompilerParams(vmem_limit_bytes=50 * MIB),
+        name="spectrum",
+    )(core, table, cols, edge)
+
+
+def spread_kernel(keep_ref, come_ref, out_ref):
+    block = keep_ref[...] + come_ref[...]
+    for dest in range(16):
+        out_ref[dest * WIDE : (dest + 1) * WIDE, :] = block
+
+
+def spread_call(keep, come):
+    vmem = pl.BlockSpec(memory_space=pltpu.VMEM)
+    return pl.pallas_call(
+        spread_kernel,
         out_shape=jax.ShapeDtypeStruct((16 * WIDE, PASS), jnp.float32),
-        in_specs=[
-            pl.BlockSpec((1, PASS, NPIX // 4), lambda q: (q, 0, 0)),
-            pl.BlockSpec((NPIX // 4, 128), lambda q: (0, 0)),
-            pl.BlockSpec((2, 8, 128), lambda q: (0, 0, 0)),
-        ],
-        out_specs=pl.BlockSpec((16 * WIDE, PASS), lambda q: (0, 0)),
-        scratch_shapes=[pltpu.VMEM((PASS, 128), jnp.float32)],
-        compiler_params=pltpu.CompilerParams(vmem_limit_bytes=16 * MIB),
-        name="spectrum",
-    )(table, cols, edge)
+        in_specs=[vmem, vmem],
+        out_specs=vmem,
+        compiler_params=pltpu.CompilerParams(vmem_limit_bytes=6 * MIB),
+        name="spread",
+    )(keep, come)
 
 
 def pack_kernel(shifts_ref, weights_ref, pupil_ref, dose_ref, turned_ref, last_ref, first_ref, note_ref):
@@ -620,9 +631,10 @@
     core, src, tile = lax.axis_index("c"), lax.axis_index(src_axes), lax.axis_index(tile_axes)
     packed = columns_call(trans_table, mask_ids, jnp.asarray(forward_columns()), jnp.asarray(edge_columns()))
     packed, shifts, weights, dose_late, pupil = lax.optimization_barrier((packed, shifts, weights, dose, pupil))
-    cols = lax.all_to_all(packed, ALL, 0, 0, tiled=True)
+    cols = lax.all_to_all(packed, ("zl", "y", "zh", "x"), 0, 0, tiled=True)
 
     turned, last, first, note = pack_call(shifts, weights, pupil, dose_late)
+    cols, turned, last, first, note = lax.optimization_barrier((cols, turned, last, first, note))
     before = lax.ppermute(last, src_axes, ring(src_axes, 1))
     after = lax.ppermute(first, src_axes, ring(src_axes, -1))
     far = lax.ppermute(note, src_axes, ring(src_axes, 2))
@@ -634,13 +646,16 @@
     below = lax.ppermute(first, tile_axes, ring(tile_axes, -1))
     where = jnp.stack([core, tile, src]).astype(jnp.int32)
 
-    block = spectrum_call(jnp.asarray(forward_rows()), cols, jnp.asarray(edge_rows()))
+    swap = [(0, 1), (1, 0)]
+    core_ref = core.reshape(1).astype(jnp.int32)
+    keep, send = spectrum_call(core_ref, jnp.asarray(forward_rows()), cols, jnp.asarray(edge_rows()))
+    block = spread_call(keep, lax.ppermute(send, "c", swap))
     own = lax.all_to_all(block, ("y", "x"), 0, 0, tiled=True)
     window, token = window_call(all_shifts, turned)
     own, token, all_weights, side, above, below, where = lax.optimization_barrier(
         (own, token, all_weights, side, above, below, where)
     )
-    other = lax.ppermute(own, "c", [(0, 1), (1, 0)])
+    other = lax.ppermute(own, "c", swap)
     half, row_table, window_other, dose_near = own_call(where, token, own, window, jnp.asarray(inverse_rows(32)), dose)
     return resist_call(
         where, all_weights, quencher, half, other, window_other, row_table,

time: 74.7 us -> 73.6 us (0.985)
  local copies, waits for them, and re-layouts: 8.19 us -> 6 us
  starting transfers between devices: 26.5 us -> 28 us
  waiting for transfers between devices: 7.87 us -> 7.07 us
    unnamed x16 -> x14, local copies, waits for them, and re-layouts: 7.72 us -> 5.53 us
    ppermute x1 -> x2, starting transfers between devices: 1.61 us -> 3.69 us  [the longest x1 2.14 us: body(): block = spread_call(keep, lax.ppermute(send, 'c', swap))]
    ppermute x1, waiting for transfers between devices: 4.79 us -> 3.43 us  [body(): above = lax.ppermute(last, tile_axes, ring(tile_axes, 1))]
    ppermute x1, starting transfers between devices: 1.75 us -> 0.47 us  [body(): before = lax.ppermute(last, src_axes, ring(src_axes, 1))]
    pallas_call x2 -> x3, Pallas kernels: 8.49 us -> 8.81 us  [the longest x1 4.75 us: columns_call(): pl.pallas_call(columns_kernel, out_shape=jax.ShapeDtypeStruct((DEVICES //...]
  transfers between devices with their start and end apart: 8 -> 9, of which waited for: 2 -> 2; matrix products, arithmetic and copies ran while one was open for 1% -> 1% of each run, Pallas kernels for 20% -> 17%
where the time goes in v4:
time: 73.6 us; the launch traced here: 73.2 us
  Pallas kernels  30.4 us (41%)
  starting transfers between devices  28 us (38%)
  waiting for transfers between devices  7.07 us (10%)
  local copies, waits for them, and re-layouts  6 us (8%)
  between operations  1.6 us (2%)
    all_to_all x1, starting transfers between devices, body(): cols = lax.all_to_all(packed, ('zl', 'y', 'zh', 'x'), 0, 0, tiled=True)  12 us
    pallas_call x1, Pallas kernels, resist_call(): pl.pallas_call(resist_kernel, out_shape=(out, out), in_specs=[smem] * 3 +...  10.5 us
    ppermute x1, starting transfers between devices, body(): below = lax.ppermute(first, tile_axes, ring(tile_axes, -1))  5.95 us
    unnamed x14, local copies, waits for them, and re-layouts  5.53 us
    pallas_call x1, Pallas kernels, window_call(): pl.pallas_call(window_kernel, out_shape=(jax.ShapeDtypeStruct((3 * planes...  5.34 us
    pallas_call x1, Pallas kernels, columns_call(): pl.pallas_call(columns_kernel, out_shape=jax.ShapeDtypeStruct((DEVICES //...  4.75 us
    pallas_call x1, Pallas kernels, own_call(): pl.pallas_call(own_kernel, out_shape=(jax.ShapeDtypeStruct((SOURCES * TAL...  4.28 us
    all_to_all x1, starting transfers between devices, body(): own = lax.all_to_all(block, ('y', 'x'), 0, 0, tiled=True)  3.66 us
  transfers between devices with their start and end apart: 9, of which 2 were waited for; matrix products, arithmetic and copies ran while one was open for 1% of the time, Pallas kernels for 17%

profile of v4, /device:TPU:1, one launch (start us, length us, event | category | flops | bytes accessed | tf_op | source)
XLA Modules:
  0.0 73.2 jit_solution(14216161542100256094)
XLA Ops:
  0.6 0.0 copy-start.4
  0.6 0.0 copy-start
  0.7 0.0 copy-start.5
  0.7 4.8 %columns.1 = bf16[1024,128]{1,0:T(8,128)(2,1)} custom-call(f32[2,4]{1,0:T(2,128)} %trans_ref.1, s32[32,4096]{1,0:T(8,128)} %ids_hbm.1, bf16[4096,512]{1,0:T(8,128)(2,1)} %constant.38.clone.table_hbm, f32[2,128]{1,0:T(2,128)} %constant.39.clone.edge_ref), custom_call_target="tpu_custom_call" | custom-call | tf_op jit(solution)/shard_map/columns/pallas_call | solution.py:177
  5.4 12.0 %all-to-all-start = ((bf16[64,16,128]{2,1,0:T(8,128)(2,1)}), bf16[64,16,128]{2,1,0:T(8,128)(2,1)S(1)}, u32[]{:S(2)}, u32[]{:S(2)}) async-start(bf16[64,16,128]{2,1,0:T(8,128)(2,1)} %bitcast.14), calls=%async_computation | async-start | bytes 524288 | tf_op jit(solution)/shard_map/all_to_all | solution.py:634
  18.1 0.0 copy-done
  18.1 0.0 copy-done.5
  18.1 0.0 copy-start.1
  18.1 1.9 %copy-done.1 = f32[2,640,640]{2,1,0:T(8,128)S(1)} copy-done((f32[2,640,640]{2,1,0:T(8,128)S(1)}, f32[2,640,640]{2,1,0:T(8,128)}, u32[]{:S(2)}) %copy-start.1) | copy-done | bytes 3276824
  20.0 1.4 %pack.1 = (f32[2,640,640]{2,1,0:T(8,128)S(1)}, f32[2,128,128]{2,1,0:T(8,128)S(1)}, f32[2,128,128]{2,1,0:T(8,128)S(1)}, f32[8,128]{1,0:T(8,128)S(1)}) custom-call(s32[1,2]{1,0:T(1,128)S(1)} %copy-done.5, f32[1]{0:T(128)S(6)} %copy.15.weights_ref, f32[2,640,640]{2,1,0:T(8,128)S(1)} %copy-done.1, f32[2,128,1024]{2,1,0:T(8,128)S(1)} %copy-done), custom_call_target="tpu_custom_call" | custom-call | flops 1000000 | bytes 9000000 | tf_op jit(solution)/shard_map/pack/pallas_call | solution.py:300
  21.5 0.0 copy-start.2
  21.5 1.7 %copy-done.2 = f32[2,640,640]{2,1,0:T(8,128)} copy-done((f32[2,640,640]{2,1,0:T(8,128)}, f32[2,640,640]{2,1,0:T(8,128)S(1)}, u32[]{:S(2)}) %copy-start.2) | copy-done | bytes 3276824
  23.1 3.6 %all-to-all-done = bf16[64,16,128]{2,1,0:T(8,128)(2,1)S(1)} async-done(((bf16[64,16,128]{2,1,0:T(8,128)(2,1)}), bf16[64,16,128]{2,1,0:T(8,128)(2,1)S(1)}, u32[]{:S(2)}, u32[]{:S(2)}) %all-to-all-start) | async-done | bytes 262176 | tf_op jit(solution)/shard_map/all_to_all | solution.py:634
  26.8 0.0 copy-done.4
  26.8 3.0 %spectrum.1 = (f32[32,512]{1,0:T(8,128)S(1)}, f32[32,512]{1,0:T(8,128)S(1)}) custom-call(s32[1]{0:T(128)} %bitcast.core_ref, bf16[2,2,512,1024]{3,2,1,0:T(8,128)(2,1)} %constant.40.clone.table_hbm, bf16[1024,128]{1,0:T(8,128)(2,1)S(1)} %bitcast.13, f32[2,16,128]{2,1,0:T(8,128)S(1)} %copy-done.4), custom_call_target="tpu_custom_call" | custom-call | tf_op jit(solution)/shard_map/spectrum/pallas_call | solution.py:242
  29.7 2.1 %collective-permute-start = (f32[32,512]{1,0:T(8,128)S(1)}, f32[32,512]{1,0:T(8,128)S(1)}, u32[]{:S(2)}, u32[]{:S(2)}) collective-permute-start(f32[32,512]{1,0:T(8,128)S(1)} %get-tuple-element.45), channel_id=1, source_target_pairs={{0,32},{32,0},{1,33},{33,1},{2,34},{34,2},{3,35},{35,3},{4,36},{36... | collective-permute-start | bytes 196616 | tf_op jit(solution)/shard_map/ppermute | solution.py:652
  31.9 0.5 collective-permute-start.2
  32.4 0.0 collective-permute-start.3
  32.4 1.0 %collective-permute-start.1 = (f32[8,128]{1,0:T(8,128)S(1)}, f32[8,128]{1,0:T(8,128)S(1)}, u32[]{:S(2)}, u32[]{:S(2)}) collective-permute-start(f32[8,128]{1,0:T(8,128)S(1)} %get-tuple-element.46), channel_id=1, source_target_pairs={{0,64},{32,96},{64,0},{96,32},{1,65},{33,97},{65,1},{97,33},{2,66}... | collective-permute-start | bytes 12296 | tf_op jit(solution)/shard_map/ppermute | solution.py:640
  33.4 0.0 collective-permute-done.come_ref
  33.4 1.1 %spread.1 = f32[512,512]{1,0:T(8,128)} custom-call(f32[32,512]{1,0:T(8,128)S(1)} %get-tuple-element.44.keep_ref, f32[32,512]{1,0:T(8,128)S(1)} %collective-permute-done.come_ref), custom_call_target="tpu_custom_call" | custom-call | tf_op jit(solution)/shard_map/spread/pallas_call | solution.py:265
  34.4 3.7 %all-to-all-start.1 = ((f32[16,32,512]{2,1,0:T(8,128)}), f32[16,32,512]{2,1,0:T(8,128)S(1)}, u32[]{:S(2)}, u32[]{:S(2)}) async-start(f32[16,32,512]{2,1,0:T(8,128)} %bitcast.3), calls=%async_computation.1 | async-start | bytes 2097152 | tf_op jit(solution)/shard_map/all_to_all | solution.py:653
  38.1 0.1 pad_add_fusion.where_ref
  38.2 0.1 slice.18
  38.2 0.0 collective-permute-done.1
  38.3 0.1 slice.19
  38.3 0.0 collective-permute-done.2.before_ref
  38.3 0.0 collective-permute-done.3.after_ref
  38.4 1.3 %collective-permute-start.4 = (f32[2,8,1152]{2,1,0:T(8,128)S(1)}, f32[2,8,1152]{2,1,0:T(8,128)S(1)}, u32[]{:S(2)}, u32[]{:S(2)}) collective-permute-start(f32[2,8,1152]{2,1,0:T(8,128)S(1)} %get-tuple-element.52), channel_id=1, source_target_pairs={{0,1},{1,2},{2,3},{3,4},{4,5},{5,6},{6,7},{7,8},{8,9},{9,10},{10,1... | collective-permute-start | bytes 221192 | tf_op jit(solution)/shard_map/ppermute | solution.py:645
  39.7 5.9 %collective-permute-start.5 = (f32[2,8,1152]{2,1,0:T(8,128)S(1)}, f32[2,8,1152]{2,1,0:T(8,128)S(1)}, u32[]{:S(2)}, u32[]{:S(2)}) collective-permute-start(f32[2,8,1152]{2,1,0:T(8,128)S(1)} %get-tuple-element.53), channel_id=1, source_target_pairs={{0,31},{1,0},{2,1},{3,2},{4,3},{5,4},{6,5},{7,6},{8,7},{9,8},{10,9... | collective-permute-start | bytes 221192 | tf_op jit(solution)/shard_map/ppermute | solution.py:646
  45.6 0.1 slice_bitcast_fusion.1
  45.7 0.1 slice_bitcast_fusion
  45.8 0.0 copy-start.3
  45.8 1.9 %copy-done.3 = f32[2,640,640]{2,1,0:T(8,128)S(1)} copy-done((f32[2,640,640]{2,1,0:T(8,128)S(1)}, f32[2,640,640]{2,1,0:T(8,128)}, u32[]{:S(2)}) %copy-start.3) | copy-done | bytes 3276824
  47.7 5.3 %window.1 = (f32[24,512,512]{2,1,0:T(8,128)}, f32[8,128]{1,0:T(8,128)S(1)}) custom-call(s32[4,2]{1,0:T(4,128)S(1)} %slice_convert_fusion.shifts_ref, f32[2,640,640]{2,1,0:T(8,128)S(1)} %copy-done.3), custom_call_target="tpu_custom_call" | custom-call | flops 10000000 | bytes 11000000 | tf_op jit(solution)/shard_map/window/pallas_call | solution.py:404
  53.1 0.2 slice_reduce_fusion.weights_ref
  53.3 3.4 %collective-permute-done.4.above_ref = f32[2,8,1152]{2,1,0:T(8,128)S(1)} collective-permute-done((f32[2,8,1152]{2,1,0:T(8,128)S(1)}, f32[2,8,1152]{2,1,0:T(8,128)S(1)}, u32[]{:S(2)}, u32[]{:S(2)}) %collective-permute-start.4) | collective-permute-done | bytes 73760 | tf_op jit(solution)/shard_map/ppermute | solution.py:645
  56.7 0.0 collective-permute-done.5.below_ref
  56.7 0.0 all-to-all-done.1
  56.7 1.6 %collective-permute-start.6 = (f32[512,512]{1,0:T(8,128)S(1)}, f32[512,512]{1,0:T(8,128)S(1)}, u32[]{:S(2)}, u32[]{:S(2)}) collective-permute-start(f32[512,512]{1,0:T(8,128)S(1)} %bitcast.11), channel_id=1, source_target_pairs={{0,32},{32,0},{1,33},{33,1},{2,34},{34,2},{3,35},{35,3},{4,36},{36... | collective-permute-start | bytes 3145736 | tf_op jit(solution)/shard_map/ppermute | solution.py:658
  58.2 0.0 copy-start.6
  58.2 4.3 %own_half.1 = (bf16[576,512]{1,0:T(8,128)(2,1)S(1)}, bf16[288,1024]{1,0:T(8,128)(2,1)S(1)}, f32[8,256,512]{2,1,0:T(8,128)S(1)}, f32[2,128,1024]{2,1,0:T(8,128)S(1)}) custom-call(s32[3]{0:T(128)S(1)} %pad_add_fusion.where_ref, f32[8,128]{1,0:T(8,128)S(1)} %get-tuple-element.56.token_ref, f32[512,512]{1,0:T(8,128)S(1)} %bitcast.12, ...), custom_call_target="tpu_custom_call" | custom-call | flops 10000000 | bytes 9000000 | tf_op jit(solution)/shard_map/own_half/pallas_call | solution.py:476
  62.5 0.0 collective-permute-done.6.other_ref
  62.5 0.0 copy-done.6
  62.5 10.5 %resist.1 = (f32[2,128,1024]{2,1,0:T(8,128)}, f32[2,128,1024]{2,1,0:T(8,128)}) custom-call(s32[3]{0:T(128)S(1)} %pad_add_fusion.where_ref, f32[4]{0:T(128)S(1)} %slice_reduce_fusion.weights_ref, f32[2]{0:T(128)S(1)} %copy-done.6, bf16[576,512]{1,0:T(8,128)(2,1)S(1)} %get-tuple-element.59.half_ref, f32[512,512]{1,0:T(8,128)S(1)} %collective-permute-done.6.other_ref, ...), custom_call_target="tpu_custom_call" | custom-call | tf_op jit(solution)/shard_map/resist/pallas_call | solution.py:605
  (3 shorter events, 0.0 us)
Async XLA Ops:
  0.6 26.1 %copy-start.4 = (f32[2,16,128]{2,1,0:T(8,128)S(1)}, f32[2,16,128]{2,1,0:T(8,128)}, u32[]{:S(2)}) copy-start(f32[2,16,128]{2,1,0:T(8,128)} %constant.41.clone.edge_ref) | copy-start | bytes 49156
  0.6 17.4 %copy-start = (f32[2,128,1024]{2,1,0:T(8,128)S(1)}, f32[2,128,1024]{2,1,0:T(8,128)}, u32[]{:S(2)}) copy-start(f32[2,128,1024]{2,1,0:T(8,128)} %dose_hbm.1) | copy-start | bytes 3145732
  0.7 17.4 %copy-start.5 = (s32[1,2]{1,0:T(1,128)S(1)}, s32[1,2]{1,0:T(1,128)}, u32[]{:S(2)}) copy-start(s32[1,2]{1,0:T(1,128)} %shifts_ref) | copy-start | bytes 28
  5.4 21.3 %all-to-all-start = ((bf16[64,16,128]{2,1,0:T(8,128)(2,1)}), bf16[64,16,128]{2,1,0:T(8,128)(2,1)S(1)}, u32[]{:S(2)}, u32[]{:S(2)}) async-start(bf16[64,16,128]{2,1,0:T(8,128)(2,1)} %bitcast.14), calls=%async_computation | async-start | bytes 524288 | tf_op jit(solution)/shard_map/all_to_all | solution.py:634
  18.1 1.9 %copy-start.1 = (f32[2,640,640]{2,1,0:T(8,128)S(1)}, f32[2,640,640]{2,1,0:T(8,128)}, u32[]{:S(2)}) copy-start(f32[2,640,640]{2,1,0:T(8,128)} %pupil_ref) | copy-start | bytes 9830404
  21.5 1.7 %copy-start.2 = (f32[2,640,640]{2,1,0:T(8,128)}, f32[2,640,640]{2,1,0:T(8,128)S(1)}, u32[]{:S(2)}) copy-start(f32[2,640,640]{2,1,0:T(8,128)S(1)} %get-tuple-element.49.turned_ref) | copy-start | bytes 9830404
  29.7 3.6 %collective-permute-start = (f32[32,512]{1,0:T(8,128)S(1)}, f32[32,512]{1,0:T(8,128)S(1)}, u32[]{:S(2)}, u32[]{:S(2)}) collective-permute-start(f32[32,512]{1,0:T(8,128)S(1)} %get-tuple-element.45), channel_id=1, source_target_pairs={{0,32},{32,0},{1,33},{33,1},{2,34},{34,2},{3,35},{35,3},{4,36},{36... | collective-permute-start | bytes 196616 | tf_op jit(solution)/shard_map/ppermute | solution.py:652
  31.9 6.4 %collective-permute-start.2 = (f32[2,128,128]{2,1,0:T(8,128)S(1)}, f32[2,128,128]{2,1,0:T(8,128)S(1)}, u32[]{:S(2)}, u32[]{:S(2)}) collective-permute-start(f32[2,128,128]{2,1,0:T(8,128)S(1)} %get-tuple-element.47), channel_id=1, source_target_pairs={{0,32},{32,64},{64,96},{96,0},{1,33},{33,65},{65,97},{97,1},{2,34}... | collective-permute-start | bytes 393224 | tf_op jit(solution)/shard_map/ppermute | solution.py:638
  32.4 6.0 %collective-permute-start.3 = (f32[2,128,128]{2,1,0:T(8,128)S(1)}, f32[2,128,128]{2,1,0:T(8,128)S(1)}, u32[]{:S(2)}, u32[]{:S(2)}) collective-permute-start(f32[2,128,128]{2,1,0:T(8,128)S(1)} %get-tuple-element.48), channel_id=1, source_target_pairs={{0,96},{32,0},{64,32},{96,64},{1,97},{33,1},{65,33},{97,65},{2,98}... | collective-permute-start | bytes 393224 | tf_op jit(solution)/shard_map/ppermute | solution.py:639
  32.4 5.9 %collective-permute-start.1 = (f32[8,128]{1,0:T(8,128)S(1)}, f32[8,128]{1,0:T(8,128)S(1)}, u32[]{:S(2)}, u32[]{:S(2)}) collective-permute-start(f32[8,128]{1,0:T(8,128)S(1)} %get-tuple-element.46), channel_id=1, source_target_pairs={{0,64},{32,96},{64,0},{96,32},{1,65},{33,97},{65,1},{97,33},{2,66}... | collective-permute-start | bytes 12296 | tf_op jit(solution)/shard_map/ppermute | solution.py:640
  34.4 22.3 %all-to-all-start.1 = ((f32[16,32,512]{2,1,0:T(8,128)}), f32[16,32,512]{2,1,0:T(8,128)S(1)}, u32[]{:S(2)}, u32[]{:S(2)}) async-start(f32[16,32,512]{2,1,0:T(8,128)} %bitcast.3), calls=%async_computation.1 | async-start | bytes 2097152 | tf_op jit(solution)/shard_map/all_to_all | solution.py:653
  38.4 18.3 %collective-permute-start.4 = (f32[2,8,1152]{2,1,0:T(8,128)S(1)}, f32[2,8,1152]{2,1,0:T(8,128)S(1)}, u32[]{:S(2)}, u32[]{:S(2)}) collective-permute-start(f32[2,8,1152]{2,1,0:T(8,128)S(1)} %get-tuple-element.52), channel_id=1, source_target_pairs={{0,1},{1,2},{2,3},{3,4},{4,5},{5,6},{6,7},{7,8},{8,9},{9,10},{10,1... | collective-permute-start | bytes 221192 | tf_op jit(solution)/shard_map/ppermute | solution.py:645
  39.7 17.0 %collective-permute-start.5 = (f32[2,8,1152]{2,1,0:T(8,128)S(1)}, f32[2,8,1152]{2,1,0:T(8,128)S(1)}, u32[]{:S(2)}, u32[]{:S(2)}) collective-permute-start(f32[2,8,1152]{2,1,0:T(8,128)S(1)} %get-tuple-element.53), channel_id=1, source_target_pairs={{0,31},{1,0},{2,1},{3,2},{4,3},{5,4},{6,5},{7,6},{8,7},{9,8},{10,9... | collective-permute-start | bytes 221192 | tf_op jit(solution)/shard_map/ppermute | solution.py:646
  45.8 1.9 %copy-start.3 = (f32[2,640,640]{2,1,0:T(8,128)S(1)}, f32[2,640,640]{2,1,0:T(8,128)}, u32[]{:S(2)}) copy-start(f32[2,640,640]{2,1,0:T(8,128)} %copy-done.2) | copy-start | bytes 9830404
  56.7 5.8 %collective-permute-start.6 = (f32[512,512]{1,0:T(8,128)S(1)}, f32[512,512]{1,0:T(8,128)S(1)}, u32[]{:S(2)}, u32[]{:S(2)}) collective-permute-start(f32[512,512]{1,0:T(8,128)S(1)} %bitcast.11), channel_id=1, source_target_pairs={{0,32},{32,0},{1,33},{33,1},{2,34},{34,2},{3,35},{35,3},{4,36},{36... | collective-permute-start | bytes 3145736 | tf_op jit(solution)/shard_map/ppermute | solution.py:658
  58.2 4.3 %copy-start.6 = (f32[2]{0:T(128)S(1)}, f32[2]{0:T(128)}, u32[]{:S(2)}) copy-start(f32[2]{0:T(128)} %quencher_ref.1) | copy-start | bytes 28

commit v5 on v4

--- a/solution.py
+++ b/solution.py
@@ -36,7 +36,7 @@
 EARLY = 2
 ALL = ("zl", "c", "y", "zh", "x")
 MIB = 1024 * 1024
-PARTS = 4
+QUARTER = NPIX // 4
 
 
 def cos_sin(first, second):
@@ -46,7 +46,7 @@
 
 
 def bf16(table):
-    return table.astype(jnp.bfloat16)
+    return np.asarray(table).astype(jnp.bfloat16)
 
 
 FREQ = np.arange(PASS, dtype=np.int64) - PASS // 2
@@ -54,24 +54,25 @@
 
 
 def forward_columns():
-    return bf16(np.concatenate(cos_sin(np.arange(NPIX), np.arange(HALF)), axis=1))
+    return bf16(np.concatenate(cos_sin(np.arange(QUARTER), np.arange(HALF)), axis=1))
 
 
 def forward_rows():
-    order = np.arange(NPIX).reshape(2, 2, DEVICES // 4, 2, 16).transpose(1, 3, 0, 2, 4).reshape(NPIX)
+    order = np.arange(2 * QUARTER).reshape(2, DEVICES // 4, 2, 16).transpose(0, 2, 1, 3).reshape(2 * QUARTER)
     both = np.concatenate(cos_sin(np.arange(HALF), order), axis=0)
-    return bf16(both.reshape(PASS, 2, 2, NPIX // 4).transpose(1, 2, 0, 3))
-
-
-def edge_columns():
-    cosine, sine = cos_sin(np.array([HALF]), np.arange(128))
-    return np.asarray(bf16(np.concatenate([cosine, sine], axis=0))).astype(np.float32)
-
-
-def edge_rows():
-    cosine, sine = cos_sin(np.array([HALF]), np.arange(16))
-    both = np.repeat(np.stack([cosine.reshape(16, 1), sine.reshape(16, 1)]), 128, axis=2)
-    return np.asarray(bf16(both)).astype(np.float32)
+    table = both.reshape(PASS, 2, 2, QUARTER // 2).transpose(1, 2, 0, 3)
+    return bf16(np.pad(table, ((0, 0), (0, 14), (0, 0), (0, 0))))
+
+
+def edge_values(place):
+    tables = [bf16(part)[0] for part in cos_sin(np.array([HALF]), np.arange(16))]
+    results = []
+    for table in tables:
+        value = jnp.zeros(place.shape, jnp.float32)
+        for k in range(16):
+            value = jnp.where(place == k, float(table[k]), value)
+        results.append(value)
+    return results
 
 
 def inverse_rows(tiles):
@@ -105,29 +106,20 @@
     return lax.broadcasted_iota(jnp.int32, shape, len(shape) - 1)
 
 
-def columns_kernel(trans_ref, ids_hbm, table_hbm, edge_ref, out_ref, ids_ref, table_ref, perm_ref, sems):
-    depth = NPIX // PARTS
-    copies = []
-    for k in range(PARTS):
-        part = pl.ds(k * depth, depth)
-        both = (
-            pltpu.make_async_copy(ids_hbm.at[:, part], ids_ref.at[:, part], sems.at[0, k]),
-            pltpu.make_async_copy(table_hbm.at[part], table_ref.at[part], sems.at[1, k]),
-        )
-        for copy in both:
-            copy.start()
-        copies.append(both)
+def columns_kernel(trans_ref, ids_hbm, table_hbm, out_ref, ids_ref, table_ref, pixels_ref, perm_ref, sems):
+    ids_copy = pltpu.make_async_copy(ids_hbm, ids_ref, sems.at[0])
+    table_copy = pltpu.make_async_copy(table_hbm, table_ref, sems.at[1])
+    ids_copy.start()
+    table_copy.start()
     source = lax.broadcasted_iota(jnp.int32, (PASS, PASS), 0)
     lane = lax.broadcasted_iota(jnp.int32, (PASS, PASS), 1)
     plane, place = lane // FREQS % 2, lane // WIDE * FREQS + lane % FREQS
     perm_ref[0] = (source == plane * HALF + (HALF - place) % HALF).astype(jnp.float32).astype(jnp.bfloat16)
     perm_ref[1] = (source == plane * HALF + place).astype(jnp.float32).astype(jnp.bfloat16)
-    acc = jnp.zeros((2 * ROWS, PASS), jnp.float32)
+    ids_copy.wait()
     total = jnp.zeros((2 * ROWS, 128), jnp.float32)
-    for k in range(PARTS):
-        part = slice(k * depth, k * depth + depth)
-        copies[k][0].wait()
-        ids = ids_ref[:, part]
+    for m in range(4):
+        ids = ids_ref[:, m * QUARTER : (m + 1) * QUARTER]
         planes = []
         for plane in range(2):
             value = jnp.zeros(ids.shape, jnp.float32)
@@ -135,15 +127,30 @@
                 value = jnp.where(ids == level, trans_ref[plane, level], value)
             planes.append(value)
         trans = jnp.concatenate(planes, axis=0).astype(jnp.bfloat16)
+        pixels_ref[2 * ROWS * m : 2 * ROWS * (m + 1), :] = trans
         exact = trans.astype(jnp.float32)
-        for tile in range(depth // 128):
+        for tile in range(QUARTER // 128):
             total = total + exact[:, 128 * tile : 128 * tile + 128]
-        copies[k][1].wait()
-        acc = acc + jnp.dot(trans, table_ref[part, :], preferred_element_type=jnp.float32)
-    edge_cos = jnp.sum(total * edge_ref[0:1, :], axis=1, keepdims=True)
-    edge_sin = jnp.sum(total * edge_ref[1:2, :], axis=1, keepdims=True)
-    cos_real, cos_imag = acc[:ROWS, :HALF], acc[ROWS:, :HALF]
-    sin_real, sin_imag = acc[:ROWS, HALF:], acc[ROWS:, HALF:]
+    table_copy.wait()
+    product = jnp.dot(pixels_ref[...], table_ref[...], preferred_element_type=jnp.float32)
+    cosines = [product[2 * ROWS * m : 2 * ROWS * (m + 1), :HALF] for m in range(4)]
+    sines = [product[2 * ROWS * m : 2 * ROWS * (m + 1), HALF:] for m in range(4)]
+    turns = lane_ids((2 * ROWS, HALF)) % 4
+    zero = jnp.zeros((2 * ROWS, HALF), jnp.float32)
+
+    def quarter(value, first):
+        return jnp.where(turns == first, value, jnp.where(turns == first + 2, -value, zero))
+
+    odd = turns % 2 == 1
+    cosine = cosines[0] + jnp.where(odd, -cosines[2], cosines[2])
+    cosine = cosine + quarter(cosines[1] + cosines[3], 0) - quarter(sines[1] - sines[3], 1)
+    sine = sines[0] + jnp.where(odd, -sines[2], sines[2])
+    sine = sine + quarter(cosines[1] - cosines[3], 1) + quarter(sines[1] + sines[3], 0)
+    weight_cos, weight_sin = edge_values(lane_ids((1, 128)) % 16)
+    edge_cos = jnp.sum(total * weight_cos, axis=1, keepdims=True)
+    edge_sin = jnp.sum(total * weight_sin, axis=1, keepdims=True)
+    cos_real, cos_imag = cosine[:ROWS], cosine[ROWS:]
+    sin_real, sin_imag = sine[:ROWS], sine[ROWS:]
     first = lane_ids((ROWS, HALF)) == 0
     low_real = jnp.where(first, edge_cos[:ROWS] - edge_sin[ROWS:], cos_real - sin_imag)
     low_imag = jnp.where(first, edge_cos[ROWS:] + edge_sin[:ROWS], cos_imag + sin_real)
@@ -171,26 +178,27 @@
                 out_ref[16 * dest : 16 * dest + 16, :] = value
 
 
-def columns_call(trans_table, mask_ids, table, edge):
+def columns_call(trans_table, mask_ids, table):
     vmem = pl.BlockSpec(memory_space=pltpu.VMEM)
     hbm = pl.BlockSpec(memory_space=pl.ANY)
     return pl.pallas_call(
         columns_kernel,
         out_shape=jax.ShapeDtypeStruct((DEVICES // 2 * 16, 128), jnp.bfloat16),
-        in_specs=[pl.BlockSpec(memory_space=pltpu.SMEM), hbm, hbm, vmem],
+        in_specs=[pl.BlockSpec(memory_space=pltpu.SMEM), hbm, hbm],
         out_specs=vmem,
         scratch_shapes=[
             pltpu.VMEM((ROWS, NPIX), jnp.int32),
-            pltpu.VMEM((NPIX, PASS), jnp.bfloat16),
+            pltpu.VMEM((QUARTER, PASS), jnp.bfloat16),
+            pltpu.VMEM((8 * ROWS, QUARTER), jnp.bfloat16),
             pltpu.VMEM((2, PASS, PASS), jnp.bfloat16),
-            pltpu.SemaphoreType.DMA((2, PARTS)),
+            pltpu.SemaphoreType.DMA((2,)),
         ],
         compiler_params=pltpu.CompilerParams(vmem_limit_bytes=56 * MIB),
         name="columns",
-    )(trans_table, mask_ids, table, edge)
-
-
-def spectrum_kernel(core_ref, table_hbm, cols_ref, edge_ref, keep_ref, send_ref, table_ref, block_ref, sems):
+    )(trans_table, mask_ids, table)
+
+
+def spectrum_kernel(core_ref, table_hbm, cols_ref, keep_ref, send_ref, table_ref, block_ref, sems):
     core = core_ref[0]
     copies = []
     for q in range(2):
@@ -200,8 +208,9 @@
     total = [columns[16 * k : 16 * k + 16] for k in range(DEVICES // 2)]
     while len(total) > 1:
         total = [a + b for a, b in zip(total[::2], total[1::2])]
-    edge_cos = jnp.sum(total[0] * edge_ref[0], axis=0, keepdims=True)
-    edge_sin = jnp.sum(total[0] * edge_ref[1], axis=0, keepdims=True)
+    weight_cos, weight_sin = edge_values(lax.broadcasted_iota(jnp.int32, (16, 128), 0))
+    edge_cos = jnp.sum(total[0] * weight_cos, axis=0, keepdims=True)
+    edge_sin = jnp.sum(total[0] * weight_sin, axis=0, keepdims=True)
 
     def turn(value):
         is_real = lane_ids(value.shape) % WIDE < FREQS
@@ -213,10 +222,14 @@
     source = lax.broadcasted_iota(jnp.int32, (HALF, HALF), 0)
     place = lax.broadcasted_iota(jnp.int32, (HALF, HALF), 1)
     perm = (source == (HALF - place) % HALF).astype(jnp.float32).astype(jnp.bfloat16)
+    rows = DEVICES // 4 * 16
+    both = jnp.concatenate([cols_ref[:rows, :], cols_ref[rows:, :]], axis=1)
+    odd = lax.broadcasted_iota(jnp.int32, (PASS, 128), 0) % 2 == 1
     products = []
     for q in range(2):
         copies[q].wait()
-        products.append(jnp.dot(table_ref[q], cols_ref[...], preferred_element_type=jnp.float32))
+        product = jnp.dot(table_ref[q], both, preferred_element_type=jnp.float32)
+        products.append(product[:, :128] + jnp.where(odd, -product[:, 128:], product[:, 128:]))
     folded = jnp.where(lane_ids((PASS, 128)) < 64, products[0], products[1])
     folded = folded + pltpu.roll(folded, 64, 1)
     cosine, turned = folded[:HALF], turn(folded[HALF:])
@@ -236,22 +249,22 @@
     send_ref[...] = block_ref[pl.ds(pl.multiple_of((1 - core) * WIDE, WIDE), WIDE), :]
 
 
-def spectrum_call(core, table, cols, edge):
+def spectrum_call(core, table, cols):
     vmem = pl.BlockSpec(memory_space=pltpu.VMEM)
     part = jax.ShapeDtypeStruct((WIDE, PASS), jnp.float32)
     return pl.pallas_call(
         spectrum_kernel,
         out_shape=(part, part),
-        in_specs=[pl.BlockSpec(memory_space=pltpu.SMEM), pl.BlockSpec(memory_space=pl.ANY), vmem, vmem],
+        in_specs=[pl.BlockSpec(memory_space=pltpu.SMEM), pl.BlockSpec(memory_space=pl.ANY), vmem],
         out_specs=(vmem, vmem),
         scratch_shapes=[
-            pltpu.VMEM(table.shape[1:], jnp.bfloat16),
+            pltpu.VMEM((2,) + table.shape[2:], jnp.bfloat16),
             pltpu.VMEM((2 * WIDE, PASS), jnp.float32),
             pltpu.SemaphoreType.DMA((2,)),
         ],
         compiler_params=pltpu.CompilerParams(vmem_limit_bytes=50 * MIB),
         name="spectrum",
-    )(core, table, cols, edge)
+    )(core, table, cols)
 
 
 def spread_kernel(keep_ref, come_ref, out_ref):
@@ -272,14 +285,7 @@
     )(keep, come)
 
 
-def pack_kernel(shifts_ref, weights_ref, pupil_ref, dose_ref, turned_ref, last_ref, first_ref, note_ref):
-    blocks = pupil_ref.shape[1] // 128
-    for plane in range(2):
-        for i in range(blocks):
-            for j in range(blocks):
-                piece = pupil_ref[plane, 128 * i : 128 * i + 128, 128 * j : 128 * j + 128]
-                turned_ref[plane, 128 * j : 128 * j + 128, 128 * i : 128 * i + 128] = jnp.transpose(piece)
-
+def pack_kernel(shifts_ref, weights_ref, dose_ref, last_ref, first_ref, note_ref):
     def note(shape):
         lane = lane_ids(shape)
         shift_x, shift_y = shifts_ref[0, 0].astype(jnp.float32), shifts_ref[0, 1].astype(jnp.float32)
@@ -293,27 +299,23 @@
     note_ref[...] = note((8, 128))
 
 
-def pack_call(shifts, weights, pupil, dose):
+def pack_call(shifts, weights, dose):
     vmem = pl.BlockSpec(memory_space=pltpu.VMEM)
     smem = pl.BlockSpec(memory_space=pltpu.SMEM)
     side = jax.ShapeDtypeStruct((Z, BRICK_ROWS, 128), jnp.float32)
     return pl.pallas_call(
         pack_kernel,
-        out_shape=(
-            jax.ShapeDtypeStruct(pupil.shape, jnp.float32),
-            side,
-            side,
-            jax.ShapeDtypeStruct((8, 128), jnp.float32),
-        ),
-        in_specs=[smem, smem, vmem, vmem],
-        out_specs=(vmem,) * 4,
-        compiler_params=pltpu.CompilerParams(vmem_limit_bytes=12 * MIB),
+        out_shape=(side, side, jax.ShapeDtypeStruct((8, 128), jnp.float32)),
+        in_specs=[smem, smem, vmem],
+        out_specs=(vmem,) * 3,
+        compiler_params=pltpu.CompilerParams(vmem_limit_bytes=6 * MIB),
         cost_estimate=pl.CostEstimate(flops=1_000_000, bytes_accessed=9_000_000, transcendentals=0),
         name="pack",
-    )(shifts, weights, pupil, dose)
-
-
-def edge_kernel(dose_ref, before_ref, after_ref, side_ref, last_ref, first_ref):
+    )(shifts, weights, dose)
+
+
+def edge_kernel(dose_ref, before_ref, after_ref, side_ref, last_ref, first_ref, near_ref):
+    near_ref[...] = dose_ref[...]
     lane = lane_ids((BRICK_ROWS, 128))
     for z in range(Z):
         side = jnp.where(lane < 64, after_ref[z], before_ref[z])
@@ -329,16 +331,27 @@
     row = jax.ShapeDtypeStruct((Z, 8, EXT_COLS), jnp.float32)
     return pl.pallas_call(
         edge_kernel,
-        out_shape=(jax.ShapeDtypeStruct((Z, BRICK_ROWS, 128), jnp.float32), row, row),
+        out_shape=(
+            jax.ShapeDtypeStruct((Z, BRICK_ROWS, 128), jnp.float32),
+            row,
+            row,
+            jax.ShapeDtypeStruct(dose.shape, jnp.float32),
+        ),
         in_specs=[vmem] * 3,
-        out_specs=(vmem,) * 3,
+        out_specs=(vmem,) * 4,
         compiler_params=pltpu.CompilerParams(vmem_limit_bytes=6 * MIB),
         cost_estimate=pl.CostEstimate(flops=1_000_000, bytes_accessed=2_000_000, transcendentals=0),
         name="edge",
     )(dose, before, after)
 
 
-def window_kernel(shifts_ref, turned_ref, out_hbm, token_ref, out_ref, sems):
+def window_kernel(shifts_ref, pupil_ref, out_hbm, token_ref, out_ref, turned_ref, sems):
+    blocks = pupil_ref.shape[1] // 128
+    for plane in range(2):
+        for i in range(blocks):
+            for j in range(blocks):
+                piece = pupil_ref[plane, 128 * i : 128 * i + 128, 128 * j : 128 * j + 128]
+                turned_ref[plane, 128 * j : 128 * j + 128, 128 * i : 128 * i + 128] = jnp.transpose(piece)
     token_ref[...] = jnp.zeros_like(token_ref)
     lane = lane_ids((8, 128))
     row = lax.broadcasted_iota(jnp.int32, (8, 128), 0)
@@ -409,7 +422,11 @@
         ),
         in_specs=[pl.BlockSpec(memory_space=pltpu.SMEM), vmem],
         out_specs=(pl.BlockSpec(memory_space=pl.ANY), vmem),
-        scratch_shapes=[pltpu.VMEM((planes, PASS, PASS), jnp.float32), pltpu.SemaphoreType.DMA((SOURCES,))],
+        scratch_shapes=[
+            pltpu.VMEM((planes, PASS, PASS), jnp.float32),
+            pltpu.VMEM(pupil.shape, jnp.float32),
+            pltpu.SemaphoreType.DMA((SOURCES,)),
+        ],
         compiler_params=pltpu.CompilerParams(vmem_limit_bytes=44 * MIB),
         cost_estimate=pl.CostEstimate(flops=10_000_000, bytes_accessed=11_000_000, transcendentals=0),
         name="window",
@@ -437,8 +454,8 @@
 
 
 def own_kernel(
-    where_ref, token_ref, own_ref, window_hbm, rows_hbm, dose_hbm,
-    field_ref, rows_ref, other_ref, dose_ref, window_ref, filt_ref, sems,
+    where_ref, token_ref, own_ref, window_hbm, rows_hbm,
+    field_ref, rows_ref, other_ref, window_ref, filt_ref, sems,
 ):
     core = where_ref[0]
     mine = pl.ds(pl.multiple_of(core * HALF, HALF), HALF)
@@ -450,12 +467,8 @@
         planes = pl.ds(2 * s, 2)
         copies.append(pltpu.make_async_copy(window_hbm.at[planes, mine], window_ref.at[planes], sems.at[1 + s]))
         copies[s].start()
-    later = [
-        pltpu.make_async_copy(dose_hbm, dose_ref, sems.at[1 + SOURCES]),
-        pltpu.make_async_copy(window_hbm.at[pl.ds(0, 2 * SOURCES), theirs], other_ref, sems.at[2 + SOURCES]),
-    ]
-    for copy in later:
-        copy.start()
+    later = pltpu.make_async_copy(window_hbm.at[pl.ds(0, 2 * SOURCES), theirs], other_ref, sems.at[1 + SOURCES])
+    later.start()
     rows_copy.wait()
     for s in range(SOURCES):
         if s % 2 == 0:
@@ -464,11 +477,10 @@
         rowfield = rowfield_half(s, own_ref, window_ref, rows_ref, filt_ref)
         field_ref[s * TALL : (s + 1) * TALL, :HALF] = rowfield[:TALL]
         field_ref[s * TALL : (s + 1) * TALL, HALF:] = rowfield[TALL:]
-    for copy in later:
-        copy.wait()
-
-
-def own_call(where, token, own, window, rows, dose):
+    later.wait()
+
+
+def own_call(where, token, own, window, rows):
     smem = pl.BlockSpec(memory_space=pltpu.SMEM)
     vmem = pl.BlockSpec(memory_space=pltpu.VMEM)
     hbm = pl.BlockSpec(memory_space=pl.ANY)
@@ -479,19 +491,18 @@
             jax.ShapeDtypeStruct((SOURCES * TALL, PASS), jnp.bfloat16),
             jax.ShapeDtypeStruct(rows.shape[1:], jnp.bfloat16),
             jax.ShapeDtypeStruct(half, jnp.float32),
-            jax.ShapeDtypeStruct(dose.shape, jnp.float32),
         ),
-        in_specs=[smem, hbm, vmem, hbm, hbm, hbm],
-        out_specs=(vmem,) * 4,
+        in_specs=[smem, hbm, vmem, hbm, hbm],
+        out_specs=(vmem,) * 3,
         scratch_shapes=[
             pltpu.VMEM(half, jnp.float32),
             pltpu.VMEM((2, HALF, 2 * PASS), jnp.bfloat16),
-            pltpu.SemaphoreType.DMA((3 + SOURCES,)),
+            pltpu.SemaphoreType.DMA((2 + SOURCES,)),
         ],
         compiler_params=pltpu.CompilerParams(vmem_limit_bytes=36 * MIB),
         cost_estimate=pl.CostEstimate(flops=10_000_000, bytes_accessed=9_000_000, transcendentals=0),
         name="own_half",
-    )(where, token, own, window, rows, dose)
+    )(where, token, own, window, rows)
 
 
 def resist_kernel(
@@ -629,34 +640,34 @@
 def body(mask_ids, trans_table, pupil, shifts, weights, dose, quencher):
     src_axes, tile_axes = ("zl", "c"), ("y", "zh", "x")
     core, src, tile = lax.axis_index("c"), lax.axis_index(src_axes), lax.axis_index(tile_axes)
-    packed = columns_call(trans_table, mask_ids, jnp.asarray(forward_columns()), jnp.asarray(edge_columns()))
-    packed, shifts, weights, dose_late, pupil = lax.optimization_barrier((packed, shifts, weights, dose, pupil))
+    packed = columns_call(trans_table, mask_ids, jnp.asarray(forward_columns()))
+    packed, shifts, weights, dose_late = lax.optimization_barrier((packed, shifts, weights, dose))
     cols = lax.all_to_all(packed, ("zl", "y", "zh", "x"), 0, 0, tiled=True)
 
-    turned, last, first, note = pack_call(shifts, weights, pupil, dose_late)
-    cols, turned, last, first, note = lax.optimization_barrier((cols, turned, last, first, note))
+    last, first, note = pack_call(shifts, weights, dose_late)
+    cols, last, first, note = lax.optimization_barrier((cols, last, first, note))
     before = lax.ppermute(last, src_axes, ring(src_axes, 1))
     after = lax.ppermute(first, src_axes, ring(src_axes, -1))
     far = lax.ppermute(note, src_axes, ring(src_axes, 2))
     notes = [note[:1, 64:67], far[:1, 64:67], before[0, :1, 64:67], after[0, :1, 64:67]]
     sources = jnp.concatenate(notes, axis=0)
     all_shifts, all_weights = sources[:, :2].astype(jnp.int32), sources[:, 2]
-    side, last, first = edge_call(dose_late, before, after)
+    side, last, first, dose_near = edge_call(dose_late, before, after)
     above = lax.ppermute(last, tile_axes, ring(tile_axes, 1))
     below = lax.ppermute(first, tile_axes, ring(tile_axes, -1))
     where = jnp.stack([core, tile, src]).astype(jnp.int32)
 
     swap = [(0, 1), (1, 0)]
     core_ref = core.reshape(1).astype(jnp.int32)
-    keep, send = spectrum_call(core_ref, jnp.asarray(forward_rows()), cols, jnp.asarray(edge_rows()))
+    keep, send = spectrum_call(core_ref, jnp.asarray(forward_rows()), cols)
     block = spread_call(keep, lax.ppermute(send, "c", swap))
     own = lax.all_to_all(block, ("y", "x"), 0, 0, tiled=True)
-    window, token = window_call(all_shifts, turned)
+    window, token = window_call(all_shifts, pupil)
     own, token, all_weights, side, above, below, where = lax.optimization_barrier(
         (own, token, all_weights, side, above, below, where)
     )
     other = lax.ppermute(own, "c", swap)
-    half, row_table, window_other, dose_near = own_call(where, token, own, window, jnp.asarray(inverse_rows(32)), dose)
+    half, row_table, window_other = own_call(where, token, own, window, jnp.asarray(inverse_rows(32)))
     return resist_call(
         where, all_weights, quencher, half, other, window_other, row_table,
         jnp.asarray(inverse_cols(4)), dose_near, side, above, below,

time: 73.6 us -> 72 us (0.978)
  local copies, waits for them, and re-layouts: 6 us -> 4.28 us
  waiting for transfers between devices: 7.07 us -> 8.71 us
  Pallas kernels: 30.4 us -> 28.9 us
    all_to_all x1, waiting for transfers between devices: 3.62 us -> 6.25 us  [body(): cols = lax.all_to_all(packed, ('zl', 'y', 'zh', 'x'), 0, 0, tiled=True)]
    unnamed x14 -> x10, local copies, waits for them, and re-layouts: 5.53 us -> 3.81 us
    ppermute x1, waiting for transfers between devices: 3.43 us -> 2.45 us  [body(): above = lax.ppermute(last, tile_axes, ring(tile_axes, 1))]
    pallas_call x1, Pallas kernels: 5.34 us -> 6.26 us  [window_call(): pl.pallas_call(window_kernel, out_shape=(jax.ShapeDtypeStruct((3 * planes...]
    pallas_call x1, Pallas kernels: 1.44 us -> 0.56 us  [pack_call(): pl.pallas_call(pack_kernel, out_shape=(side, side, jax.ShapeDtypeStruct((...]
    pallas_call x1, Pallas kernels: 4.75 us -> 3.95 us  [columns_call(): pl.pallas_call(columns_kernel, out_shape=jax.ShapeDtypeStruct((DEVICES //...]
where the time goes in v5:
time: 72 us; the launch traced here: 71.6 us
  Pallas kernels  28.9 us (40%)
  starting transfers between devices  28 us (39%)
  waiting for transfers between devices  8.71 us (12%)
  local copies, waits for them, and re-layouts  4.28 us (6%)
  between operations  1.57 us (2%)
    all_to_all x1, starting transfers between devices, body(): cols = lax.all_to_all(packed, ('zl', 'y', 'zh', 'x'), 0, 0, tiled=True)  12 us
    pallas_call x1, Pallas kernels, resist_call(): pl.pallas_call(resist_kernel, out_shape=(out, out), in_specs=[smem] * 3 +...  10.5 us
    pallas_call x1, Pallas kernels, window_call(): pl.pallas_call(window_kernel, out_shape=(jax.ShapeDtypeStruct((3 * planes...  6.26 us
    all_to_all x1, waiting for transfers between devices, body(): cols = lax.all_to_all(packed, ('zl', 'y', 'zh', 'x'), 0, 0, tiled=True)  6.25 us
    ppermute x1, starting transfers between devices, body(): below = lax.ppermute(first, tile_axes, ring(tile_axes, -1))  5.95 us
    pallas_call x1, Pallas kernels, own_call(): pl.pallas_call(own_kernel, out_shape=(jax.ShapeDtypeStruct((SOURCES * TAL...  4.25 us
    pallas_call x1, Pallas kernels, columns_call(): pl.pallas_call(columns_kernel, out_shape=jax.ShapeDtypeStruct((DEVICES //...  3.95 us
    unnamed x10, local copies, waits for them, and re-layouts  3.81 us
  transfers between devices with their start and end apart: 9, of which 2 were waited for; matrix products, arithmetic and copies ran while one was open for 1% of the time, Pallas kernels for 17%

profile of v5, /device:TPU:1, one launch (start us, length us, event | category | flops | bytes accessed | tf_op | source)
XLA Modules:
  0.0 71.6 jit_solution(3446648733918909981)
XLA Ops:
  0.6 0.0 copy-start.1
  0.6 3.9 %columns.1 = bf16[1024,128]{1,0:T(8,128)(2,1)} custom-call(f32[2,4]{1,0:T(2,128)} %trans_ref.1, s32[32,4096]{1,0:T(8,128)} %ids_hbm.1, bf16[1024,512]{1,0:T(8,128)(2,1)} %constant.34.clone.table_hbm), custom_call_target="tpu_custom_call" | custom-call | tf_op jit(solution)/shard_map/columns/pallas_call | solution.py:184
  4.6 12.0 %all-to-all-start = ((bf16[64,16,128]{2,1,0:T(8,128)(2,1)}), bf16[64,16,128]{2,1,0:T(8,128)(2,1)S(1)}, u32[]{:S(2)}, u32[]{:S(2)}) async-start(bf16[64,16,128]{2,1,0:T(8,128)(2,1)} %bitcast.14), calls=%async_computation | async-start | bytes 524288 | tf_op jit(solution)/shard_map/all_to_all | solution.py:645
  17.2 0.0 copy-start
  17.2 1.2 %copy-done = f32[2,128,1024]{2,1,0:T(8,128)S(1)} copy-done((f32[2,128,1024]{2,1,0:T(8,128)S(1)}, f32[2,128,1024]{2,1,0:T(8,128)}, u32[]{:S(2)}) %copy-start) | copy-done | bytes 1048600
  18.5 0.0 copy-start.3
  18.5 0.7 copy-done.3
  19.1 0.6 pack.1
  19.7 6.2 %all-to-all-done = bf16[64,16,128]{2,1,0:T(8,128)(2,1)S(1)} async-done(((bf16[64,16,128]{2,1,0:T(8,128)(2,1)}), bf16[64,16,128]{2,1,0:T(8,128)(2,1)S(1)}, u32[]{:S(2)}, u32[]{:S(2)}) %all-to-all-start) | async-done | bytes 262176 | tf_op jit(solution)/shard_map/all_to_all | solution.py:645
  25.9 2.3 %spectrum.1 = (f32[32,512]{1,0:T(8,128)S(1)}, f32[32,512]{1,0:T(8,128)S(1)}) custom-call(s32[1]{0:T(128)} %bitcast.core_ref, bf16[2,16,512,512]{3,2,1,0:T(8,128)(2,1)} %constant.35.clone.table_hbm, bf16[1024,128]{1,0:T(8,128)(2,1)S(1)} %bitcast.13), custom_call_target="tpu_custom_call" | custom-call | tf_op jit(solution)/shard_map/spectrum/pallas_call | solution.py:255
  28.2 2.1 %collective-permute-start = (f32[32,512]{1,0:T(8,128)S(1)}, f32[32,512]{1,0:T(8,128)S(1)}, u32[]{:S(2)}, u32[]{:S(2)}) collective-permute-start(f32[32,512]{1,0:T(8,128)S(1)} %get-tuple-element.40), channel_id=1, source_target_pairs={{0,32},{32,0},{1,33},{33,1},{2,34},{34,2},{3,35},{35,3},{4,36},{36... | collective-permute-start | bytes 196616 | tf_op jit(solution)/shard_map/ppermute | solution.py:663
  30.3 0.5 collective-permute-start.2
  30.8 0.0 collective-permute-start.3
  30.9 1.0 %collective-permute-start.1 = (f32[8,128]{1,0:T(8,128)S(1)}, f32[8,128]{1,0:T(8,128)S(1)}, u32[]{:S(2)}, u32[]{:S(2)}) collective-permute-start(f32[8,128]{1,0:T(8,128)S(1)} %get-tuple-element.41), channel_id=1, source_target_pairs={{0,64},{32,96},{64,0},{96,32},{1,65},{33,97},{65,1},{97,33},{2,66}... | collective-permute-start | bytes 12296 | tf_op jit(solution)/shard_map/ppermute | solution.py:651
  31.8 0.0 collective-permute-done.come_ref
  31.8 1.1 %spread.1 = f32[512,512]{1,0:T(8,128)} custom-call(f32[32,512]{1,0:T(8,128)S(1)} %get-tuple-element.39.keep_ref, f32[32,512]{1,0:T(8,128)S(1)} %collective-permute-done.come_ref), custom_call_target="tpu_custom_call" | custom-call | tf_op jit(solution)/shard_map/spread/pallas_call | solution.py:278
  32.9 3.7 %all-to-all-start.1 = ((f32[16,32,512]{2,1,0:T(8,128)}), f32[16,32,512]{2,1,0:T(8,128)S(1)}, u32[]{:S(2)}, u32[]{:S(2)}) async-start(f32[16,32,512]{2,1,0:T(8,128)} %bitcast.3), calls=%async_computation.1 | async-start | bytes 2097152 | tf_op jit(solution)/shard_map/all_to_all | solution.py:664
  36.6 0.1 pad_add_fusion.where_ref
  36.6 0.1 slice.18
  36.7 0.0 collective-permute-done.1
  36.7 0.1 slice.19
  36.8 0.0 collective-permute-done.2.before_ref
  36.8 0.0 collective-permute-done.3.after_ref
  36.8 0.0 copy-done.1
  36.8 0.1 edge.1
  36.9 1.3 %collective-permute-start.4 = (f32[2,8,1152]{2,1,0:T(8,128)S(1)}, f32[2,8,1152]{2,1,0:T(8,128)S(1)}, u32[]{:S(2)}, u32[]{:S(2)}) collective-permute-start(f32[2,8,1152]{2,1,0:T(8,128)S(1)} %get-tuple-element.46), channel_id=1, source_target_pairs={{0,1},{1,2},{2,3},{3,4},{4,5},{5,6},{6,7},{7,8},{8,9},{9,10},{10,1... | collective-permute-start | bytes 221192 | tf_op jit(solution)/shard_map/ppermute | solution.py:656
  38.2 5.9 %collective-permute-start.5 = (f32[2,8,1152]{2,1,0:T(8,128)S(1)}, f32[2,8,1152]{2,1,0:T(8,128)S(1)}, u32[]{:S(2)}, u32[]{:S(2)}) collective-permute-start(f32[2,8,1152]{2,1,0:T(8,128)S(1)} %get-tuple-element.47), channel_id=1, source_target_pairs={{0,31},{1,0},{2,1},{3,2},{4,3},{5,4},{6,5},{7,6},{8,7},{9,8},{10,9... | collective-permute-start | bytes 221192 | tf_op jit(solution)/shard_map/ppermute | solution.py:657
  44.1 0.1 slice_bitcast_fusion.1
  44.2 0.1 slice_bitcast_fusion
  44.3 0.0 copy-start.2
  44.3 1.9 %copy-done.2 = f32[2,640,640]{2,1,0:T(8,128)S(1)} copy-done((f32[2,640,640]{2,1,0:T(8,128)S(1)}, f32[2,640,640]{2,1,0:T(8,128)}, u32[]{:S(2)}) %copy-start.2) | copy-done | bytes 3276824
  46.2 6.3 %window.1 = (f32[24,512,512]{2,1,0:T(8,128)}, f32[8,128]{1,0:T(8,128)S(1)}) custom-call(s32[4,2]{1,0:T(4,128)S(1)} %slice_convert_fusion.shifts_ref, f32[2,640,640]{2,1,0:T(8,128)S(1)} %copy-done.2), custom_call_target="tpu_custom_call" | custom-call | flops 10000000 | bytes 11000000 | tf_op jit(solution)/shard_map/window/pallas_call | solution.py:417
  52.5 0.2 slice_reduce_fusion.weights_ref
  52.7 2.4 %collective-permute-done.4.above_ref = f32[2,8,1152]{2,1,0:T(8,128)S(1)} collective-permute-done((f32[2,8,1152]{2,1,0:T(8,128)S(1)}, f32[2,8,1152]{2,1,0:T(8,128)S(1)}, u32[]{:S(2)}, u32[]{:S(2)}) %collective-permute-start.4) | collective-permute-done | bytes 73760 | tf_op jit(solution)/shard_map/ppermute | solution.py:656
  55.1 0.0 collective-permute-done.5.below_ref
  55.1 0.0 all-to-all-done.1
  55.1 1.5 %collective-permute-start.6 = (f32[512,512]{1,0:T(8,128)S(1)}, f32[512,512]{1,0:T(8,128)S(1)}, u32[]{:S(2)}, u32[]{:S(2)}) collective-permute-start(f32[512,512]{1,0:T(8,128)S(1)} %bitcast.11), channel_id=1, source_target_pairs={{0,32},{32,0},{1,33},{33,1},{2,34},{34,2},{3,35},{35,3},{4,36},{36... | collective-permute-start | bytes 3145736 | tf_op jit(solution)/shard_map/ppermute | solution.py:669
  56.7 0.0 copy-start.4
  56.7 4.3 %own_half.1 = (bf16[576,512]{1,0:T(8,128)(2,1)S(1)}, bf16[288,1024]{1,0:T(8,128)(2,1)S(1)}, f32[8,256,512]{2,1,0:T(8,128)S(1)}) custom-call(s32[3]{0:T(128)S(1)} %pad_add_fusion.where_ref, f32[8,128]{1,0:T(8,128)S(1)} %get-tuple-element.50.token_ref, f32[512,512]{1,0:T(8,128)S(1)} %bitcast.12, f32[24,512,512]{2,1,0:T(8,128)} %get-tuple-element.52.window_hbm, ...), custom_call_target="tpu_custom_call" | custom-call | flops 10000000 | bytes 9000000 | tf_op jit(solution)/shard_map/own_half/pallas_call | solution.py:488
  60.9 0.0 collective-permute-done.6.other_ref
  61.0 0.0 copy-done.4
  61.0 10.5 %resist.1 = (f32[2,128,1024]{2,1,0:T(8,128)}, f32[2,128,1024]{2,1,0:T(8,128)}) custom-call(s32[3]{0:T(128)S(1)} %pad_add_fusion.where_ref, f32[4]{0:T(128)S(1)} %slice_reduce_fusion.weights_ref, f32[2]{0:T(128)S(1)} %copy-done.4, bf16[576,512]{1,0:T(8,128)(2,1)S(1)} %get-tuple-element.53.half_ref, f32[512,512]{1,0:T(8,128)S(1)} %collective-permute-done.6.other_ref, ...), custom_call_target="tpu_custom_call" | custom-call | tf_op jit(solution)/shard_map/resist/pallas_call | solution.py:616
  (2 shorter events, 0.0 us)
Async XLA Ops:
  0.6 36.2 %copy-start.1 = (f32[2,128,1024]{2,1,0:T(8,128)S(1)}, f32[2,128,1024]{2,1,0:T(8,128)}, u32[]{:S(2)}) copy-start(f32[2,128,1024]{2,1,0:T(8,128)} %dose_ref.1) | copy-start | bytes 3145732
  4.6 21.3 %all-to-all-start = ((bf16[64,16,128]{2,1,0:T(8,128)(2,1)}), bf16[64,16,128]{2,1,0:T(8,128)(2,1)S(1)}, u32[]{:S(2)}, u32[]{:S(2)}) async-start(bf16[64,16,128]{2,1,0:T(8,128)(2,1)} %bitcast.14), calls=%async_computation | async-start | bytes 524288 | tf_op jit(solution)/shard_map/all_to_all | solution.py:645
  17.2 1.2 %copy-start = (f32[2,128,1024]{2,1,0:T(8,128)S(1)}, f32[2,128,1024]{2,1,0:T(8,128)}, u32[]{:S(2)}) copy-start(f32[2,128,1024]{2,1,0:T(8,128)} %dose_ref.1) | copy-start | bytes 3145732
  18.5 0.7 copy-start.3
  28.2 3.6 %collective-permute-start = (f32[32,512]{1,0:T(8,128)S(1)}, f32[32,512]{1,0:T(8,128)S(1)}, u32[]{:S(2)}, u32[]{:S(2)}) collective-permute-start(f32[32,512]{1,0:T(8,128)S(1)} %get-tuple-element.40), channel_id=1, source_target_pairs={{0,32},{32,0},{1,33},{33,1},{2,34},{34,2},{3,35},{35,3},{4,36},{36... | collective-permute-start | bytes 196616 | tf_op jit(solution)/shard_map/ppermute | solution.py:663
  30.3 6.4 %collective-permute-start.2 = (f32[2,128,128]{2,1,0:T(8,128)S(1)}, f32[2,128,128]{2,1,0:T(8,128)S(1)}, u32[]{:S(2)}, u32[]{:S(2)}) collective-permute-start(f32[2,128,128]{2,1,0:T(8,128)S(1)} %get-tuple-element.42), channel_id=1, source_target_pairs={{0,32},{32,64},{64,96},{96,0},{1,33},{33,65},{65,97},{97,1},{2,34}... | collective-permute-start | bytes 393224 | tf_op jit(solution)/shard_map/ppermute | solution.py:649
  30.8 6.0 %collective-permute-start.3 = (f32[2,128,128]{2,1,0:T(8,128)S(1)}, f32[2,128,128]{2,1,0:T(8,128)S(1)}, u32[]{:S(2)}, u32[]{:S(2)}) collective-permute-start(f32[2,128,128]{2,1,0:T(8,128)S(1)} %get-tuple-element.43), channel_id=1, source_target_pairs={{0,96},{32,0},{64,32},{96,64},{1,97},{33,1},{65,33},{97,65},{2,98}... | collective-permute-start | bytes 393224 | tf_op jit(solution)/shard_map/ppermute | solution.py:650
  30.9 5.9 %collective-permute-start.1 = (f32[8,128]{1,0:T(8,128)S(1)}, f32[8,128]{1,0:T(8,128)S(1)}, u32[]{:S(2)}, u32[]{:S(2)}) collective-permute-start(f32[8,128]{1,0:T(8,128)S(1)} %get-tuple-element.41), channel_id=1, source_target_pairs={{0,64},{32,96},{64,0},{96,32},{1,65},{33,97},{65,1},{97,33},{2,66}... | collective-permute-start | bytes 12296 | tf_op jit(solution)/shard_map/ppermute | solution.py:651
  32.9 22.3 %all-to-all-start.1 = ((f32[16,32,512]{2,1,0:T(8,128)}), f32[16,32,512]{2,1,0:T(8,128)S(1)}, u32[]{:S(2)}, u32[]{:S(2)}) async-start(f32[16,32,512]{2,1,0:T(8,128)} %bitcast.3), calls=%async_computation.1 | async-start | bytes 2097152 | tf_op jit(solution)/shard_map/all_to_all | solution.py:664
  36.9 18.3 %collective-permute-start.4 = (f32[2,8,1152]{2,1,0:T(8,128)S(1)}, f32[2,8,1152]{2,1,0:T(8,128)S(1)}, u32[]{:S(2)}, u32[]{:S(2)}) collective-permute-start(f32[2,8,1152]{2,1,0:T(8,128)S(1)} %get-tuple-element.46), channel_id=1, source_target_pairs={{0,1},{1,2},{2,3},{3,4},{4,5},{5,6},{6,7},{7,8},{8,9},{9,10},{10,1... | collective-permute-start | bytes 221192 | tf_op jit(solution)/shard_map/ppermute | solution.py:656
  38.2 16.9 %collective-permute-start.5 = (f32[2,8,1152]{2,1,0:T(8,128)S(1)}, f32[2,8,1152]{2,1,0:T(8,128)S(1)}, u32[]{:S(2)}, u32[]{:S(2)}) collective-permute-start(f32[2,8,1152]{2,1,0:T(8,128)S(1)} %get-tuple-element.47), channel_id=1, source_target_pairs={{0,31},{1,0},{2,1},{3,2},{4,3},{5,4},{6,5},{7,6},{8,7},{9,8},{10,9... | collective-permute-start | bytes 221192 | tf_op jit(solution)/shard_map/ppermute | solution.py:657
  44.3 1.9 %copy-start.2 = (f32[2,640,640]{2,1,0:T(8,128)S(1)}, f32[2,640,640]{2,1,0:T(8,128)}, u32[]{:S(2)}) copy-start(f32[2,640,640]{2,1,0:T(8,128)} %pupil_ref.1) | copy-start | bytes 9830404
  55.1 5.8 %collective-permute-start.6 = (f32[512,512]{1,0:T(8,128)S(1)}, f32[512,512]{1,0:T(8,128)S(1)}, u32[]{:S(2)}, u32[]{:S(2)}) collective-permute-start(f32[512,512]{1,0:T(8,128)S(1)} %bitcast.11), channel_id=1, source_target_pairs={{0,32},{32,0},{1,33},{33,1},{2,34},{34,2},{3,35},{35,3},{4,36},{36... | collective-permute-start | bytes 3145736 | tf_op jit(solution)/shard_map/ppermute | solution.py:669
  56.7 4.3 %copy-start.4 = (f32[2]{0:T(128)S(1)}, f32[2]{0:T(128)}, u32[]{:S(2)}) copy-start(f32[2]{0:T(128)} %quencher_ref.1) | copy-start | bytes 28

commit v6 on v5

--- a/solution.py
+++ b/solution.py
@@ -95,9 +95,8 @@
     for source in range(sources):
         pixels = np.mod(source * BRICK_COLS + local, NPIX)
         cosine, sine = cos_sin(FREQ, pixels)
-        real = np.concatenate([cosine, -sine], axis=0).reshape(2 * PASS, COL_TILES, 1, 128)
-        imag = np.concatenate([sine, cosine], axis=0).reshape(2 * PASS, COL_TILES, 1, 128)
-        both = np.concatenate([real, imag], axis=2).reshape(2 * PASS, COL_TILES, 256)
+        planes = [table.reshape(PASS, COL_TILES, 1, 128) for table in (cosine, sine)]
+        both = np.concatenate(planes, axis=2).reshape(PASS, COL_TILES, 256)
         blocks.append(both.transpose(1, 0, 2))
     return bf16(np.stack(blocks))
 
@@ -530,11 +529,13 @@
     for b in range(COL_TILES):
         if b == EARLY:
             cols_copies[1].wait()
-        field = jnp.dot(field_ref[...], cols_ref[b], preferred_element_type=jnp.float32)
+        upper = jnp.dot(field_ref[:, :PASS], cols_ref[b], preferred_element_type=jnp.float32)
+        lower = jnp.dot(field_ref[:, PASS:], cols_ref[b], preferred_element_type=jnp.float32)
         intensity = jnp.zeros((EXT_ROWS, 128), jnp.float32)
         for s in range(SOURCES):
-            part = field[s * TALL : s * TALL + EXT_ROWS]
-            real, imag = part[:, :128], part[:, 128:]
+            rows = slice(s * TALL, s * TALL + EXT_ROWS)
+            real = upper[rows, :128] - lower[rows, 128:]
+            imag = upper[rows, 128:] + lower[rows, :128]
             intensity = intensity + weights_ref[s] * (real * real + imag * imag)
         lanes = slice(b * 128, b * 128 + 128)
         for z in range(Z):

time: 72 us -> 71.4 us (level)
  no operation moved by 1% of the time
where the time goes in v6:
time: 71.4 us; the launch traced here: 71 us
  Pallas kernels  28.3 us (40%)
  starting transfers between devices  28 us (39%)
  waiting for transfers between devices  8.71 us (12%)
  local copies, waits for them, and re-layouts  4.28 us (6%)
  between operations  1.57 us (2%)
    all_to_all x1, starting transfers between devices, body(): cols = lax.all_to_all(packed, ('zl', 'y', 'zh', 'x'), 0, 0, tiled=True)  12 us
    pallas_call x1, Pallas kernels, resist_call(): pl.pallas_call(resist_kernel, out_shape=(out, out), in_specs=[smem] * 3 +...  9.85 us
    pallas_call x1, Pallas kernels, window_call(): pl.pallas_call(window_kernel, out_shape=(jax.ShapeDtypeStruct((3 * planes...  6.25 us
    all_to_all x1, waiting for transfers between devices, body(): cols = lax.all_to_all(packed, ('zl', 'y', 'zh', 'x'), 0, 0, tiled=True)  6.25 us
    ppermute x1, starting transfers between devices, body(): below = lax.ppermute(first, tile_axes, ring(tile_axes, -1))  5.95 us
    pallas_call x1, Pallas kernels, own_call(): pl.pallas_call(own_kernel, out_shape=(jax.ShapeDtypeStruct((SOURCES * TAL...  4.25 us
    pallas_call x1, Pallas kernels, columns_call(): pl.pallas_call(columns_kernel, out_shape=jax.ShapeDtypeStruct((DEVICES //...  3.95 us
    unnamed x10, local copies, waits for them, and re-layouts  3.81 us
  transfers between devices with their start and end apart: 9, of which 2 were waited for; matrix products, arithmetic and copies ran while one was open for 1% of the time, Pallas kernels for 17%

profile of v6, /device:TPU:1, one launch (start us, length us, event | category | flops | bytes accessed | tf_op | source)
XLA Modules:
  0.0 71.0 jit_solution(3681293158190609787)
XLA Ops:
  0.6 0.0 copy-start.1
  0.6 3.9 %columns.1 = bf16[1024,128]{1,0:T(8,128)(2,1)} custom-call(f32[2,4]{1,0:T(2,128)} %trans_ref.1, s32[32,4096]{1,0:T(8,128)} %ids_hbm.1, bf16[1024,512]{1,0:T(8,128)(2,1)} %constant.34.clone.table_hbm), custom_call_target="tpu_custom_call" | custom-call | tf_op jit(solution)/shard_map/columns/pallas_call | solution.py:183
  4.6 12.0 %all-to-all-start = ((bf16[64,16,128]{2,1,0:T(8,128)(2,1)}), bf16[64,16,128]{2,1,0:T(8,128)(2,1)S(1)}, u32[]{:S(2)}, u32[]{:S(2)}) async-start(bf16[64,16,128]{2,1,0:T(8,128)(2,1)} %bitcast.14), calls=%async_computation | async-start | bytes 524288 | tf_op jit(solution)/shard_map/all_to_all | solution.py:646
  17.2 0.0 copy-start
  17.2 1.2 %copy-done = f32[2,128,1024]{2,1,0:T(8,128)S(1)} copy-done((f32[2,128,1024]{2,1,0:T(8,128)S(1)}, f32[2,128,1024]{2,1,0:T(8,128)}, u32[]{:S(2)}) %copy-start) | copy-done | bytes 1048600
  18.5 0.0 copy-start.3
  18.5 0.7 copy-done.3
  19.1 0.6 pack.1
  19.7 6.2 %all-to-all-done = bf16[64,16,128]{2,1,0:T(8,128)(2,1)S(1)} async-done(((bf16[64,16,128]{2,1,0:T(8,128)(2,1)}), bf16[64,16,128]{2,1,0:T(8,128)(2,1)S(1)}, u32[]{:S(2)}, u32[]{:S(2)}) %all-to-all-start) | async-done | bytes 262176 | tf_op jit(solution)/shard_map/all_to_all | solution.py:646
  25.9 2.3 %spectrum.1 = (f32[32,512]{1,0:T(8,128)S(1)}, f32[32,512]{1,0:T(8,128)S(1)}) custom-call(s32[1]{0:T(128)} %bitcast.core_ref, bf16[2,16,512,512]{3,2,1,0:T(8,128)(2,1)} %constant.35.clone.table_hbm, bf16[1024,128]{1,0:T(8,128)(2,1)S(1)} %bitcast.13), custom_call_target="tpu_custom_call" | custom-call | tf_op jit(solution)/shard_map/spectrum/pallas_call | solution.py:254
  28.2 2.1 %collective-permute-start = (f32[32,512]{1,0:T(8,128)S(1)}, f32[32,512]{1,0:T(8,128)S(1)}, u32[]{:S(2)}, u32[]{:S(2)}) collective-permute-start(f32[32,512]{1,0:T(8,128)S(1)} %get-tuple-element.40), channel_id=1, source_target_pairs={{0,32},{32,0},{1,33},{33,1},{2,34},{34,2},{3,35},{35,3},{4,36},{36... | collective-permute-start | bytes 196616 | tf_op jit(solution)/shard_map/ppermute | solution.py:664
  30.3 0.5 collective-permute-start.2
  30.8 0.0 collective-permute-start.3
  30.9 1.0 %collective-permute-start.1 = (f32[8,128]{1,0:T(8,128)S(1)}, f32[8,128]{1,0:T(8,128)S(1)}, u32[]{:S(2)}, u32[]{:S(2)}) collective-permute-start(f32[8,128]{1,0:T(8,128)S(1)} %get-tuple-element.41), channel_id=1, source_target_pairs={{0,64},{32,96},{64,0},{96,32},{1,65},{33,97},{65,1},{97,33},{2,66}... | collective-permute-start | bytes 12296 | tf_op jit(solution)/shard_map/ppermute | solution.py:652
  31.8 0.0 collective-permute-done.come_ref
  31.8 1.1 %spread.1 = f32[512,512]{1,0:T(8,128)} custom-call(f32[32,512]{1,0:T(8,128)S(1)} %get-tuple-element.39.keep_ref, f32[32,512]{1,0:T(8,128)S(1)} %collective-permute-done.come_ref), custom_call_target="tpu_custom_call" | custom-call | tf_op jit(solution)/shard_map/spread/pallas_call | solution.py:277
  32.9 3.7 %all-to-all-start.1 = ((f32[16,32,512]{2,1,0:T(8,128)}), f32[16,32,512]{2,1,0:T(8,128)S(1)}, u32[]{:S(2)}, u32[]{:S(2)}) async-start(f32[16,32,512]{2,1,0:T(8,128)} %bitcast.3), calls=%async_computation.1 | async-start | bytes 2097152 | tf_op jit(solution)/shard_map/all_to_all | solution.py:665
  36.6 0.1 pad_add_fusion.where_ref
  36.6 0.1 slice.18
  36.7 0.0 collective-permute-done.1
  36.7 0.1 slice.19
  36.8 0.0 collective-permute-done.2.before_ref
  36.8 0.0 collective-permute-done.3.after_ref
  36.8 0.0 copy-done.1
  36.8 0.1 edge.1
  36.9 1.3 %collective-permute-start.4 = (f32[2,8,1152]{2,1,0:T(8,128)S(1)}, f32[2,8,1152]{2,1,0:T(8,128)S(1)}, u32[]{:S(2)}, u32[]{:S(2)}) collective-permute-start(f32[2,8,1152]{2,1,0:T(8,128)S(1)} %get-tuple-element.46), channel_id=1, source_target_pairs={{0,1},{1,2},{2,3},{3,4},{4,5},{5,6},{6,7},{7,8},{8,9},{9,10},{10,1... | collective-permute-start | bytes 221192 | tf_op jit(solution)/shard_map/ppermute | solution.py:657
  38.2 5.9 %collective-permute-start.5 = (f32[2,8,1152]{2,1,0:T(8,128)S(1)}, f32[2,8,1152]{2,1,0:T(8,128)S(1)}, u32[]{:S(2)}, u32[]{:S(2)}) collective-permute-start(f32[2,8,1152]{2,1,0:T(8,128)S(1)} %get-tuple-element.47), channel_id=1, source_target_pairs={{0,31},{1,0},{2,1},{3,2},{4,3},{5,4},{6,5},{7,6},{8,7},{9,8},{10,9... | collective-permute-start | bytes 221192 | tf_op jit(solution)/shard_map/ppermute | solution.py:658
  44.1 0.1 slice_bitcast_fusion.1
  44.2 0.1 slice_bitcast_fusion
  44.3 0.0 copy-start.2
  44.3 1.9 %copy-done.2 = f32[2,640,640]{2,1,0:T(8,128)S(1)} copy-done((f32[2,640,640]{2,1,0:T(8,128)S(1)}, f32[2,640,640]{2,1,0:T(8,128)}, u32[]{:S(2)}) %copy-start.2) | copy-done | bytes 3276824
  46.2 6.3 %window.1 = (f32[24,512,512]{2,1,0:T(8,128)}, f32[8,128]{1,0:T(8,128)S(1)}) custom-call(s32[4,2]{1,0:T(4,128)S(1)} %slice_convert_fusion.shifts_ref, f32[2,640,640]{2,1,0:T(8,128)S(1)} %copy-done.2), custom_call_target="tpu_custom_call" | custom-call | flops 10000000 | bytes 11000000 | tf_op jit(solution)/shard_map/window/pallas_call | solution.py:416
  52.5 0.2 slice_reduce_fusion.weights_ref
  52.7 2.4 %collective-permute-done.4.above_ref = f32[2,8,1152]{2,1,0:T(8,128)S(1)} collective-permute-done((f32[2,8,1152]{2,1,0:T(8,128)S(1)}, f32[2,8,1152]{2,1,0:T(8,128)S(1)}, u32[]{:S(2)}, u32[]{:S(2)}) %collective-permute-start.4) | collective-permute-done | bytes 73760 | tf_op jit(solution)/shard_map/ppermute | solution.py:657
  55.1 0.0 collective-permute-done.5.below_ref
  55.1 0.0 all-to-all-done.1
  55.1 1.5 %collective-permute-start.6 = (f32[512,512]{1,0:T(8,128)S(1)}, f32[512,512]{1,0:T(8,128)S(1)}, u32[]{:S(2)}, u32[]{:S(2)}) collective-permute-start(f32[512,512]{1,0:T(8,128)S(1)} %bitcast.11), channel_id=1, source_target_pairs={{0,32},{32,0},{1,33},{33,1},{2,34},{34,2},{3,35},{35,3},{4,36},{36... | collective-permute-start | bytes 3145736 | tf_op jit(solution)/shard_map/ppermute | solution.py:670
  56.7 0.0 copy-start.4
  56.7 4.3 %own_half.1 = (bf16[576,512]{1,0:T(8,128)(2,1)S(1)}, bf16[288,1024]{1,0:T(8,128)(2,1)S(1)}, f32[8,256,512]{2,1,0:T(8,128)S(1)}) custom-call(s32[3]{0:T(128)S(1)} %pad_add_fusion.where_ref, f32[8,128]{1,0:T(8,128)S(1)} %get-tuple-element.50.token_ref, f32[512,512]{1,0:T(8,128)S(1)} %bitcast.12, f32[24,512,512]{2,1,0:T(8,128)} %get-tuple-element.52.window_hbm, ...), custom_call_target="tpu_custom_call" | custom-call | flops 10000000 | bytes 9000000 | tf_op jit(solution)/shard_map/own_half/pallas_call | solution.py:487
  60.9 0.0 collective-permute-done.6.other_ref
  61.0 0.0 copy-done.4
  61.0 9.9 %resist.1 = (f32[2,128,1024]{2,1,0:T(8,128)}, f32[2,128,1024]{2,1,0:T(8,128)}) custom-call(s32[3]{0:T(128)S(1)} %pad_add_fusion.where_ref, f32[4]{0:T(128)S(1)} %slice_reduce_fusion.weights_ref, f32[2]{0:T(128)S(1)} %copy-done.4, bf16[576,512]{1,0:T(8,128)(2,1)S(1)} %get-tuple-element.53.half_ref, f32[512,512]{1,0:T(8,128)S(1)} %collective-permute-done.6.other_ref, ...), custom_call_target="tpu_custom_call" | custom-call | tf_op jit(solution)/shard_map/resist/pallas_call | solution.py:617
  (2 shorter events, 0.0 us)
Async XLA Ops:
  0.6 36.2 %copy-start.1 = (f32[2,128,1024]{2,1,0:T(8,128)S(1)}, f32[2,128,1024]{2,1,0:T(8,128)}, u32[]{:S(2)}) copy-start(f32[2,128,1024]{2,1,0:T(8,128)} %dose_ref.1) | copy-start | bytes 3145732
  4.6 21.3 %all-to-all-start = ((bf16[64,16,128]{2,1,0:T(8,128)(2,1)}), bf16[64,16,128]{2,1,0:T(8,128)(2,1)S(1)}, u32[]{:S(2)}, u32[]{:S(2)}) async-start(bf16[64,16,128]{2,1,0:T(8,128)(2,1)} %bitcast.14), calls=%async_computation | async-start | bytes 524288 | tf_op jit(solution)/shard_map/all_to_all | solution.py:646
  17.2 1.2 %copy-start = (f32[2,128,1024]{2,1,0:T(8,128)S(1)}, f32[2,128,1024]{2,1,0:T(8,128)}, u32[]{:S(2)}) copy-start(f32[2,128,1024]{2,1,0:T(8,128)} %dose_ref.1) | copy-start | bytes 3145732
  18.5 0.7 copy-start.3
  28.2 3.6 %collective-permute-start = (f32[32,512]{1,0:T(8,128)S(1)}, f32[32,512]{1,0:T(8,128)S(1)}, u32[]{:S(2)}, u32[]{:S(2)}) collective-permute-start(f32[32,512]{1,0:T(8,128)S(1)} %get-tuple-element.40), channel_id=1, source_target_pairs={{0,32},{32,0},{1,33},{33,1},{2,34},{34,2},{3,35},{35,3},{4,36},{36... | collective-permute-start | bytes 196616 | tf_op jit(solution)/shard_map/ppermute | solution.py:664
  30.3 6.4 %collective-permute-start.2 = (f32[2,128,128]{2,1,0:T(8,128)S(1)}, f32[2,128,128]{2,1,0:T(8,128)S(1)}, u32[]{:S(2)}, u32[]{:S(2)}) collective-permute-start(f32[2,128,128]{2,1,0:T(8,128)S(1)} %get-tuple-element.42), channel_id=1, source_target_pairs={{0,32},{32,64},{64,96},{96,0},{1,33},{33,65},{65,97},{97,1},{2,34}... | collective-permute-start | bytes 393224 | tf_op jit(solution)/shard_map/ppermute | solution.py:650
  30.8 6.0 %collective-permute-start.3 = (f32[2,128,128]{2,1,0:T(8,128)S(1)}, f32[2,128,128]{2,1,0:T(8,128)S(1)}, u32[]{:S(2)}, u32[]{:S(2)}) collective-permute-start(f32[2,128,128]{2,1,0:T(8,128)S(1)} %get-tuple-element.43), channel_id=1, source_target_pairs={{0,96},{32,0},{64,32},{96,64},{1,97},{33,1},{65,33},{97,65},{2,98}... | collective-permute-start | bytes 393224 | tf_op jit(solution)/shard_map/ppermute | solution.py:651
  30.9 5.9 %collective-permute-start.1 = (f32[8,128]{1,0:T(8,128)S(1)}, f32[8,128]{1,0:T(8,128)S(1)}, u32[]{:S(2)}, u32[]{:S(2)}) collective-permute-start(f32[8,128]{1,0:T(8,128)S(1)} %get-tuple-element.41), channel_id=1, source_target_pairs={{0,64},{32,96},{64,0},{96,32},{1,65},{33,97},{65,1},{97,33},{2,66}... | collective-permute-start | bytes 12296 | tf_op jit(solution)/shard_map/ppermute | solution.py:652
  32.9 22.3 %all-to-all-start.1 = ((f32[16,32,512]{2,1,0:T(8,128)}), f32[16,32,512]{2,1,0:T(8,128)S(1)}, u32[]{:S(2)}, u32[]{:S(2)}) async-start(f32[16,32,512]{2,1,0:T(8,128)} %bitcast.3), calls=%async_computation.1 | async-start | bytes 2097152 | tf_op jit(solution)/shard_map/all_to_all | solution.py:665
  36.9 18.3 %collective-permute-start.4 = (f32[2,8,1152]{2,1,0:T(8,128)S(1)}, f32[2,8,1152]{2,1,0:T(8,128)S(1)}, u32[]{:S(2)}, u32[]{:S(2)}) collective-permute-start(f32[2,8,1152]{2,1,0:T(8,128)S(1)} %get-tuple-element.46), channel_id=1, source_target_pairs={{0,1},{1,2},{2,3},{3,4},{4,5},{5,6},{6,7},{7,8},{8,9},{9,10},{10,1... | collective-permute-start | bytes 221192 | tf_op jit(solution)/shard_map/ppermute | solution.py:657
  38.2 16.9 %collective-permute-start.5 = (f32[2,8,1152]{2,1,0:T(8,128)S(1)}, f32[2,8,1152]{2,1,0:T(8,128)S(1)}, u32[]{:S(2)}, u32[]{:S(2)}) collective-permute-start(f32[2,8,1152]{2,1,0:T(8,128)S(1)} %get-tuple-element.47), channel_id=1, source_target_pairs={{0,31},{1,0},{2,1},{3,2},{4,3},{5,4},{6,5},{7,6},{8,7},{9,8},{10,9... | collective-permute-start | bytes 221192 | tf_op jit(solution)/shard_map/ppermute | solution.py:658
  44.3 1.9 %copy-start.2 = (f32[2,640,640]{2,1,0:T(8,128)S(1)}, f32[2,640,640]{2,1,0:T(8,128)}, u32[]{:S(2)}) copy-start(f32[2,640,640]{2,1,0:T(8,128)} %pupil_ref.1) | copy-start | bytes 9830404
  55.1 5.8 %collective-permute-start.6 = (f32[512,512]{1,0:T(8,128)S(1)}, f32[512,512]{1,0:T(8,128)S(1)}, u32[]{:S(2)}, u32[]{:S(2)}) collective-permute-start(f32[512,512]{1,0:T(8,128)S(1)} %bitcast.11), channel_id=1, source_target_pairs={{0,32},{32,0},{1,33},{33,1},{2,34},{34,2},{3,35},{35,3},{4,36},{36... | collective-permute-start | bytes 3145736 | tf_op jit(solution)/shard_map/ppermute | solution.py:670
  56.7 4.3 %copy-start.4 = (f32[2]{0:T(128)S(1)}, f32[2]{0:T(128)}, u32[]{:S(2)}) copy-start(f32[2]{0:T(128)} %quencher_ref.1) | copy-start | bytes 28
